TPU v7x, 32 devices: a whole 2x2x4 slice. The times are simulated.
32 devices in a mesh: gx: 4 (over y, x), gy: 8 (over z, core).
Axes of the slice: x: 2, y: 2, z: 4, core: 2. Of those that a mesh axis runs over, the one named last changes fastest.
Arguments:
- hidden_in: bfloat16 [4096, 2048], P('gy', 'gx'), may hold values from -6 to 6
- expert_routes: int32 [4096, 6], P('gy'), may hold values from 0 to 63, all different within a row; in each aligned block of 512 rows (0 to 511, 512 to 1023, ...) at most 64 rows name the same one
- piece_starts: int32 [4, 2], P('gx'), may hold values from 0 to 768, as said below
- query_weight: bfloat16 [2048, 3072], P('gx', 'gy'), may hold values from -0.125 to 0.125
- latent_weight: bfloat16 [2048, 576], P('gx', 'gy'), may hold values from -0.125 to 0.125
- latent_gain: bfloat16 [512], replicated, may hold values from 0.5 to 1.5
- expand_weight: bfloat16 [512, 4096], P(None, 'gy'), may hold values from -0.25 to 0.25
- output_weight: bfloat16 [2048, 2048], P('gy', 'gx'), may hold values from -2 to 2
- attention_gain: bfloat16 [2048], P('gx'), may hold values from 0.5 to 1.5
- ffn_gain: bfloat16 [2048], P('gx'), may hold values from 0.5 to 1.5
- router_weight: bfloat16 [2048, 64], P('gx'), may hold values from -0.0625 to 0.0625
- gate_weight: bfloat16 [64, 2048, 1408], P('gy', 'gx'), may hold values from -0.125 to 0.125
- up_weight: bfloat16 [64, 2048, 1408], P('gy', 'gx'), may hold values from -0.125 to 0.125
- down_weight: bfloat16 [64, 1408, 2048], P('gy', None, 'gx'), may hold values from -2.5 to 2.5
- shared_gate: bfloat16 [2048, 2816], P('gx', 'gy'), may hold values from -0.125 to 0.125
- shared_up: bfloat16 [2048, 2816], P('gx', 'gy'), may hold values from -0.125 to 0.125
- shared_down: bfloat16 [2816, 2048], P('gy', 'gx'), may hold values from -0.21875 to 0.21875
- grad_out: bfloat16 [4096, 2048], P('gy', 'gx'), may hold values from -6 to 6
Outputs:
- mixed: bfloat16 [4096, 2048], P('gy', 'gx')
- grad_hidden: float32 [4096, 2048], P('gy', 'gx')
- grad_query: float32 [2048, 3072], P('gx', 'gy')
- grad_latent: float32 [2048, 576], P('gx', 'gy')
- grad_latent_gain: float32 [512], replicated
- grad_expand: float32 [512, 4096], P(None, 'gy')
- grad_output: float32 [2048, 2048], P('gy', 'gx')
- grad_attention_gain: float32 [2048], P('gx')
- grad_ffn_gain: float32 [2048], P('gx')
- grad_router: float32 [2048, 64], P('gx')
- grad_gate: float32 [64, 2048, 1408], P('gy', 'gx')
- grad_up: float32 [64, 2048, 1408], P('gy', 'gx')
- grad_down: float32 [64, 1408, 2048], P('gy', None, 'gx')
- grad_shared_gate: float32 [2048, 2816], P('gx', 'gy')
- grad_shared_up: float32 [2048, 2816], P('gx', 'gy')
- grad_shared_down: float32 [2816, 2048], P('gy', 'gx')
Inputs may be any that keep to these rules, and one draw needn't show every extreme that they name: `expert_routes`: each row names 6 different experts. In each aligned block of 512 rows no expert is named by more than 64 rows, a bound that some block reaches. `piece_starts`: two pieces of 256 tokens per sequence: the first starts in the first half of the sequence and the second in the second half, so they never intersect and stay inside the sequence.
All inputs are finite; a program needn't handle non-finite values.
Results may differ from a plain program's by a relative error of at most 0.035.
Values may be sent and summed in bfloat16 or wider, within the bound.
A program may use at most 576 MiB of HBM per device.

v0:
```python
import math

import jax
import jax.numpy as jnp
from jax import lax
from jax.sharding import PartitionSpec as P

D = 2048
DN = 128
DR = 64
DV = 128
L = 512
EXPERTS = 64
FF = 1408
TOPK = 6
SEQ_LEN = 1024
PIECE = 256


EPS = 1e-06


def for_sending(shard):

    def short(part):
        return part.astype(jnp.bfloat16) if part.dtype == jnp.float32 else part

    return jax.tree.map(short, shard)


def feature_total(value):
    return lax.psum(value, "gx")


def head_total(value):
    return jax.tree.map(lambda part: part.astype(jnp.float32), lax.psum(for_sending(value), "gy"))


def spread_rows(value):
    return lax.all_gather(value, "gy", axis=0, tiled=True)


def collect_rows(value):
    return lax.all_gather(value, "gx", axis=0, tiled=True)


def inner_total(function, rows):
    return lax.psum_scatter(
        function(jnp.int32(0), lax.axis_size("gx") * rows), "gx", scatter_dimension=0, tiled=True
    )


def outer_total(function, rows):
    return lax.psum_scatter(
        function(jnp.int32(0), lax.axis_size("gy") * rows).astype(jnp.bfloat16),
        "gy",
        scatter_dimension=0,
        tiled=True,
    ).astype(jnp.float32)


def expert_total(function, rows):
    return lax.psum_scatter(
        function(jnp.int32(0), lax.axis_size("gx") * rows).astype(jnp.bfloat16),
        "gx",
        scatter_dimension=0,
        tiled=True,
    ).astype(jnp.float32)


def expert_rows(value, function):
    return function(lax.all_gather(value, "gx", axis=0, tiled=True), jnp.int32(0))


def expert_swap(value):
    return lax.all_to_all(value, "gy", split_axis=0, concat_axis=0, tiled=True)


def keep_piece(piece, start):
    return piece


def silu(value):
    return value * jax.nn.sigmoid(value)


def silu_grad(value):
    sigma = jax.nn.sigmoid(value)
    return sigma * (1.0 + value * (1.0 - sigma))


def rotate(value, cosine, sine):
    half = value.shape[-1] // 2
    first = value[..., :half]
    second = value[..., half:]
    return jnp.concatenate(
        [first * cosine - second * sine, second * cosine + first * sine], axis=-1
    )


def rope_tables(length):
    half = DR // 2
    position = jnp.arange(length).astype(jnp.float32)
    inverse = jnp.exp(-math.log(10000.0) * jnp.arange(half).astype(jnp.float32) / half)
    angle = position[:, None] * inverse[None, :]
    return (jnp.cos(angle), jnp.sin(angle))


def piece_ids(starts, length):
    position = jnp.arange(length, dtype=jnp.int32)
    ids = jnp.zeros(starts.shape[:-1] + (length,), jnp.int32)
    for number in range(starts.shape[-1]):
        begin = starts[..., number : number + 1]
        inside = (position >= begin) & (position < begin + PIECE)
        ids = ids + jnp.where(inside, number + 1, 0)
    return ids


def allowed_keys(query_pos, key_pos, query_ids, key_ids):
    causal = key_pos[None, :] <= query_pos[:, None]
    same = (query_ids[:, None] == key_ids[None, :]) & (query_ids[:, None] > 0)
    return causal | same


def block_mask(offset, block, ids):
    length = ids.shape[0]
    query_pos = offset + jnp.arange(block, dtype=jnp.int32)
    key_pos = jnp.arange(length, dtype=jnp.int32)
    query_ids = lax.dynamic_slice_in_dim(ids, offset, block, 0)
    return allowed_keys(query_pos, key_pos, query_ids, ids)


def block_scores(query_block, keys, mask):
    scale = (DN + DR) ** (-0.5)
    scores = (
        jnp.einsum("qhc,khc->hqk", query_block, keys, preferred_element_type=jnp.float32) * scale
    )
    return jnp.where(mask[None], scores, -1e30)


def block_inputs(query_seq, key_seq, value_seq, ids, item, blocks, block):
    sequence = item // blocks
    offset = item % blocks * block
    query_here = lax.dynamic_index_in_dim(query_seq, sequence, 0, keepdims=False)
    query_block = lax.dynamic_slice_in_dim(query_here, offset, block, 0)
    keys = lax.dynamic_index_in_dim(key_seq, sequence, 0, keepdims=False)
    values = lax.dynamic_index_in_dim(value_seq, sequence, 0, keepdims=False)
    ids_here = lax.dynamic_index_in_dim(ids, sequence, 0, keepdims=False)
    return (sequence, offset, query_block, keys, values, block_mask(offset, block, ids_here))


def attention_forward(query_seq, key_seq, value_seq, ids, block):
    blocks = key_seq.shape[1] // block
    count = key_seq.shape[0] * blocks

    def one_block(item):
        sequence, offset, query_block, keys, values, mask = block_inputs(
            query_seq, key_seq, value_seq, ids, item, blocks, block
        )
        scores = block_scores(query_block, keys, mask)
        peak = jnp.max(scores, axis=2, keepdims=True)
        expo = jnp.exp(scores - peak)
        total = jnp.sum(expo, axis=2, keepdims=True)
        weights = (expo / total).astype(jnp.bfloat16)
        out = jnp.einsum(
            "hqk,khc->qhc", weights, values, preferred_element_type=jnp.float32
        ).astype(jnp.bfloat16)
        return (out, (peak + jnp.log(total))[:, :, 0])

    return lax.map(one_block, jnp.arange(count, dtype=jnp.int32))


def attention_backward(query_seq, key_seq, value_seq, ids, log_totals, grad_seq, block):
    seqs, length, heads = (key_seq.shape[0], key_seq.shape[1], key_seq.shape[2])
    blocks = length // block
    scale = (DN + DR) ** (-0.5)

    def one_block(item):
        sequence, offset, query_block, keys, values, mask = block_inputs(
            query_seq, key_seq, value_seq, ids, item, blocks, block
        )
        grad_here = lax.dynamic_index_in_dim(grad_seq, sequence, 0, keepdims=False)
        grad_block = lax.dynamic_slice_in_dim(grad_here, offset, block, 0)
        scores = block_scores(query_block, keys, mask)
        totals = lax.dynamic_index_in_dim(log_totals, item, 0, keepdims=False)
        weights = jnp.exp(scores - totals[:, :, None])
        grad_weights = jnp.einsum(
            "qhc,khc->hqk", grad_block, values, preferred_element_type=jnp.float32
        )
        centre = jnp.sum(weights * grad_weights, axis=2, keepdims=True)
        grad_scores = (weights * (grad_weights - centre)).astype(jnp.bfloat16)
        grad_query = (
            jnp.einsum("hqk,khc->qhc", grad_scores, keys, preferred_element_type=jnp.float32)
            * scale
        )
        grad_keys = (
            jnp.einsum("hqk,qhc->khc", grad_scores, query_block, preferred_element_type=jnp.float32)
            * scale
        )
        grad_values = jnp.einsum(
            "hqk,qhc->khc",
            weights.astype(jnp.bfloat16),
            grad_block,
            preferred_element_type=jnp.float32,
        )
        return (grad_query, grad_keys, grad_values)

    grad_query, grad_keys, grad_values = lax.map(
        one_block, jnp.arange(seqs * blocks, dtype=jnp.int32)
    )
    grad_query = grad_query.reshape(seqs * length, heads, grad_query.shape[-1])
    grad_keys = jnp.sum(
        grad_keys.reshape(seqs, blocks, length, heads, grad_keys.shape[-1]), axis=1
    ).reshape(seqs * length, heads, grad_keys.shape[-1])
    grad_values = jnp.sum(
        grad_values.reshape(seqs, blocks, length, heads, grad_values.shape[-1]), axis=1
    ).reshape(seqs * length, heads, grad_values.shape[-1])
    return (grad_query, grad_keys, grad_values)


def row_product(source, weight, transposed):

    def compute(start, count):
        if transposed:
            return lax.dot_general(
                source, weight, (((1,), (1,)), ((), ())), preferred_element_type=jnp.float32
            )
        return jnp.dot(source, weight, preferred_element_type=jnp.float32)

    return compute


def norm_forward(value, gain):
    total = feature_total(jnp.sum(value * value, axis=1))
    scale = lax.rsqrt(total / D + EPS)
    return (scale, (value * scale[:, None] * gain).astype(jnp.bfloat16))


def norm_backward(value, scale, gain, grad_norm, row_total, width):
    return (
        scale[:, None] * gain * grad_norm - value * (scale**3 / width)[:, None] * row_total[:, None]
    )


def per_device(
    hidden_in,
    expert_routes,
    piece_starts,
    query_weight,
    latent_weight,
    latent_gain,
    expand_weight,
    output_weight,
    attention_gain,
    ffn_gain,
    router_weight,
    gate_weight,
    up_weight,
    down_weight,
    shared_gate,
    shared_up,
    shared_down,
    grad_out,
):
    row_parts = lax.axis_size("gx")
    column_parts = lax.axis_size("gy")
    local_rows = hidden_in.shape[0]
    local_width = hidden_in.shape[1]
    all_tokens = local_rows * column_parts
    band_rows = all_tokens // row_parts
    head_width = query_weight.shape[1]
    heads_here = head_width // (DN + DR)
    latent_width = latent_weight.shape[1]
    experts_here = gate_weight.shape[0]
    shared_width = shared_gate.shape[1]
    pair_count = local_rows * TOPK
    capacity = 8 * ((local_rows * TOPK * 5 + 32 * EXPERTS - 1) // (32 * EXPERTS))
    slots_all = capacity * column_parts
    slots_here = slots_all // row_parts
    seqs_here = band_rows // SEQ_LEN
    block = min(512, SEQ_LEN)
    hidden = hidden_in.astype(jnp.float32)
    scale_one, norm_one = norm_forward(hidden, attention_gain)
    gathered_one = spread_rows(norm_one)
    in_weight = jnp.concatenate([query_weight, latent_weight], axis=1)
    projected = inner_total(row_product(gathered_one, in_weight, False), band_rows)
    query = projected[:, :head_width].reshape(band_rows, heads_here, DN + DR)
    latent_part = projected[:, head_width:].astype(jnp.bfloat16)
    latent_all = lax.all_gather(latent_part, "gy", axis=1, tiled=True).astype(jnp.float32)
    compressed = latent_all[:, :L]
    rope_key = latent_all[:, L:]
    latent_scale = lax.rsqrt(jnp.mean(compressed * compressed, axis=1) + EPS)
    latent_norm = (compressed * latent_scale[:, None] * latent_gain).astype(jnp.bfloat16)
    expanded = jnp.dot(latent_norm, expand_weight, preferred_element_type=jnp.float32).reshape(
        band_rows, heads_here, DN + DV
    )
    cosine, sine = rope_tables(SEQ_LEN)
    cosine = jnp.tile(cosine, (seqs_here, 1))
    sine = jnp.tile(sine, (seqs_here, 1))
    query_full = jnp.concatenate(
        [query[..., :DN], rotate(query[..., DN:], cosine[:, None], sine[:, None])], axis=-1
    ).astype(jnp.bfloat16)
    key_rope = rotate(rope_key, cosine, sine)
    key_full = jnp.concatenate(
        [expanded[..., :DN], jnp.broadcast_to(key_rope[:, None, :], (band_rows, heads_here, DR))],
        axis=-1,
    ).astype(jnp.bfloat16)
    value_full = expanded[..., DN:].astype(jnp.bfloat16)
    ids = piece_ids(piece_starts, SEQ_LEN)
    query_seq = query_full.reshape(seqs_here, SEQ_LEN, heads_here, DN + DR)
    key_seq = key_full.reshape(seqs_here, SEQ_LEN, heads_here, DN + DR)
    value_seq = value_full.reshape(seqs_here, SEQ_LEN, heads_here, DV)
    attended, log_totals = attention_forward(query_seq, key_seq, value_seq, ids, block)
    attended = attended.reshape(band_rows, heads_here * DV)
    attended_all = collect_rows(attended)
    attention_part = outer_total(row_product(attended_all, output_weight, False), local_rows)
    after_attention = hidden + attention_part
    scale_two, norm_two = norm_forward(after_attention, ffn_gain)
    logits = feature_total(jnp.dot(norm_two, router_weight, preferred_element_type=jnp.float32))
    probs = jax.nn.softmax(logits, axis=-1)
    chosen = (
        expert_routes[:, :, None] == jnp.arange(EXPERTS, dtype=jnp.int32)[None, None, :]
    ).astype(jnp.float32)
    gates = jnp.sum(chosen * probs[:, None, :], axis=2)
    flat = expert_routes.reshape(-1)
    hits = (flat[:, None] == jnp.arange(EXPERTS, dtype=jnp.int32)[None, :]).astype(jnp.int32)
    slot = jnp.sum((jnp.cumsum(hits, axis=0) - hits) * hits, axis=1)
    position = (flat // experts_here * capacity + slot) * experts_here + flat % experts_here
    owner = (
        jnp.full((slots_all * experts_here,), pair_count, jnp.int32)
        .at[position]
        .set(jnp.arange(pair_count, dtype=jnp.int32))
    )
    padded_two = jnp.concatenate([norm_two, jnp.zeros((1, local_width), jnp.bfloat16)], axis=0)
    outgoing = padded_two[owner // TOPK].reshape(column_parts, capacity, experts_here, local_width)
    dispatched = expert_swap(outgoing).reshape(slots_all, experts_here, local_width)
    joined_weight = jnp.concatenate([gate_weight, up_weight], axis=2)

    def gate_up_terms(start, count):
        return jnp.einsum(
            "sed,edf->sef", dispatched, joined_weight, preferred_element_type=jnp.float32
        )

    gate_up = expert_total(gate_up_terms, slots_here)
    gate_pre = gate_up[..., :FF]
    up_pre = gate_up[..., FF:]
    gate_act = silu(gate_pre)
    expert_hidden = (gate_act * up_pre).astype(jnp.bfloat16)

    def expand_down(piece, start):
        return jnp.einsum(
            "sef,efd->sed", piece, down_weight, preferred_element_type=jnp.float32
        ).astype(jnp.bfloat16)

    expert_out = expert_rows(expert_hidden, expand_down)
    returned = expert_swap(
        expert_out.reshape(column_parts, capacity, experts_here, local_width)
    ).reshape(slots_all * experts_here, local_width)
    picked = returned[position].reshape(local_rows, TOPK, local_width).astype(jnp.float32)
    routed = jnp.sum(gates[:, :, None] * picked, axis=1)
    gathered_two = spread_rows(norm_two)
    shared_weight = jnp.concatenate([shared_gate, shared_up], axis=1)
    shared_pre = inner_total(row_product(gathered_two, shared_weight, False), band_rows)
    shared_gate_pre = shared_pre[:, :shared_width]
    shared_up_pre = shared_pre[:, shared_width:]
    shared_hidden = (silu(shared_gate_pre) * shared_up_pre).astype(jnp.bfloat16)
    shared_all = collect_rows(shared_hidden)
    shared_part = outer_total(row_product(shared_all, shared_down, False), local_rows)
    mixed = (after_attention + routed + shared_part).astype(jnp.bfloat16)
    grad_top = grad_out.astype(jnp.float32)
    weighted = (gates[:, :, None] * grad_top[:, None, :]).reshape(pair_count, local_width)
    weighted = jnp.concatenate([weighted, jnp.zeros((1, local_width), jnp.float32)], axis=0)
    grad_outgoing = (
        weighted[owner]
        .astype(jnp.bfloat16)
        .reshape(column_parts, capacity, experts_here, local_width)
    )
    grad_rows = expert_swap(grad_outgoing).reshape(slots_all, experts_here, local_width)

    def down_back(start, count):
        return jnp.einsum(
            "sed,efd->sef", grad_rows, down_weight, preferred_element_type=jnp.float32
        )

    grad_expert_hidden = expert_total(down_back, slots_here)
    hidden_gathered = expert_rows(expert_hidden, keep_piece)
    grad_down = jnp.einsum(
        "sef,sed->efd", hidden_gathered, grad_rows, preferred_element_type=jnp.float32
    )
    grad_gate_up = jnp.concatenate(
        [grad_expert_hidden * up_pre * silu_grad(gate_pre), grad_expert_hidden * gate_act], axis=-1
    ).astype(jnp.bfloat16)
    all_grad = expert_rows(grad_gate_up, keep_piece)
    grad_joined = jnp.einsum(
        "sed,sef->edf", dispatched, all_grad, preferred_element_type=jnp.float32
    )
    grad_dispatched = jnp.einsum(
        "sef,edf->sed", all_grad, joined_weight, preferred_element_type=jnp.float32
    ).astype(jnp.bfloat16)
    grad_gate = grad_joined[..., :FF]
    grad_up = grad_joined[..., FF:]
    back_rows = expert_swap(
        grad_dispatched.reshape(column_parts, capacity, experts_here, local_width)
    ).reshape(slots_all * experts_here, local_width)
    grad_norm_routed = jnp.sum(
        back_rows[position].reshape(local_rows, TOPK, local_width).astype(jnp.float32), axis=1
    )
    grad_top_all = spread_rows(grad_out)
    grad_shared_down = jnp.einsum(
        "tc,td->cd", shared_all, grad_top_all, preferred_element_type=jnp.float32
    )
    grad_shared_hidden = inner_total(row_product(grad_top_all, shared_down, True), band_rows)
    grad_shared_pre = jnp.concatenate(
        [
            grad_shared_hidden * shared_up_pre * silu_grad(shared_gate_pre),
            grad_shared_hidden * silu(shared_gate_pre),
        ],
        axis=1,
    ).astype(jnp.bfloat16)
    grad_shared_all = collect_rows(grad_shared_pre)
    grad_shared_weight = jnp.einsum(
        "td,tc->dc", gathered_two, grad_shared_all, preferred_element_type=jnp.float32
    )
    grad_shared_gate = grad_shared_weight[:, :shared_width]
    grad_shared_up = grad_shared_weight[:, shared_width:]
    grad_norm_shared = outer_total(row_product(grad_shared_all, shared_weight, True), local_rows)
    grad_gates_part = jnp.sum(grad_top[:, None, :] * picked, axis=2)
    other = grad_norm_routed + grad_norm_shared
    scaled = after_attention * ffn_gain
    grad_gates = feature_total(grad_gates_part)
    grad_probs = jnp.sum(chosen * grad_gates[:, :, None], axis=1)
    grad_logits = (
        probs * (grad_probs - jnp.sum(probs * grad_probs, axis=1, keepdims=True))
    ).astype(jnp.bfloat16)
    grad_norm_two = other + lax.dot_general(
        grad_logits, router_weight, (((1,), (1,)), ((), ())), preferred_element_type=jnp.float32
    )
    row_two = feature_total(jnp.sum(scaled * grad_norm_two, axis=1))
    grad_after = grad_top + norm_backward(
        after_attention, scale_two, ffn_gain, grad_norm_two, row_two, D
    )
    grad_ffn_part = jnp.sum(grad_norm_two * after_attention * scale_two[:, None], axis=0)
    grad_router_part = jnp.einsum(
        "td,te->de", norm_two, grad_logits, preferred_element_type=jnp.float32
    )
    grad_after_all = spread_rows(grad_after.astype(jnp.bfloat16))
    grad_output = jnp.einsum(
        "tc,td->cd", attended_all, grad_after_all, preferred_element_type=jnp.float32
    )
    grad_attended = inner_total(row_product(grad_after_all, output_weight, True), band_rows).astype(
        jnp.bfloat16
    )
    grad_query_full, grad_key_full, grad_value_full = attention_backward(
        query_seq,
        key_seq,
        value_seq,
        ids,
        log_totals,
        grad_attended.reshape(seqs_here, SEQ_LEN, heads_here, DV),
        block,
    )
    grad_query_pre = (
        jnp.concatenate(
            [
                grad_query_full[..., :DN],
                rotate(grad_query_full[..., DN:], cosine[:, None], -sine[:, None]),
            ],
            axis=-1,
        )
        .reshape(band_rows, head_width)
        .astype(jnp.bfloat16)
    )
    grad_rope_part = jnp.sum(
        rotate(grad_key_full[..., DN:], cosine[:, None], -sine[:, None]), axis=1
    )
    grad_expanded = (
        jnp.concatenate([grad_key_full[..., :DN], grad_value_full], axis=-1)
        .reshape(band_rows, heads_here * (DN + DV))
        .astype(jnp.bfloat16)
    )
    grad_expand_part = jnp.einsum(
        "tl,tc->lc", latent_norm, grad_expanded, preferred_element_type=jnp.float32
    )
    grad_latent_part = lax.dot_general(
        grad_expanded, expand_weight, (((1,), (1,)), ((), ())), preferred_element_type=jnp.float32
    )
    grad_latent_norm, grad_rope_key = head_total((grad_latent_part, grad_rope_part))
    latent_row = jnp.sum(compressed * latent_gain * grad_latent_norm, axis=1)
    grad_compressed = norm_backward(
        compressed, latent_scale, latent_gain, grad_latent_norm, latent_row, L
    )
    grad_gain_part = jnp.sum(grad_latent_norm * compressed * latent_scale[:, None], axis=0)
    grad_expand, grad_latent_gain = feature_total((grad_expand_part, grad_gain_part))
    grad_latent_all = jnp.concatenate([grad_compressed, grad_rope_key], axis=1)
    grad_latent_own = lax.dynamic_slice_in_dim(
        grad_latent_all, lax.axis_index("gy") * latent_width, latent_width, 1
    ).astype(jnp.bfloat16)
    grad_projected = jnp.concatenate([grad_query_pre, grad_latent_own], axis=1)
    grad_projected_all = collect_rows(grad_projected)
    grad_in_weight = jnp.einsum(
        "td,tc->dc", gathered_one, grad_projected_all, preferred_element_type=jnp.float32
    )
    grad_query = grad_in_weight[:, :head_width]
    grad_latent = grad_in_weight[:, head_width:]
    grad_norm_one = outer_total(row_product(grad_projected_all, in_weight, True), local_rows)
    row_one = feature_total(jnp.sum(hidden * attention_gain * grad_norm_one, axis=1))
    grad_hidden = grad_after + norm_backward(
        hidden, scale_one, attention_gain, grad_norm_one, row_one, D
    )
    grad_attention_part = jnp.sum(grad_norm_one * hidden * scale_one[:, None], axis=0)
    grad_attention_gain, grad_ffn_gain, grad_router = head_total(
        (grad_attention_part, grad_ffn_part, grad_router_part)
    )
    return (
        mixed,
        grad_hidden,
        grad_query,
        grad_latent,
        grad_latent_gain,
        grad_expand,
        grad_output,
        grad_attention_gain,
        grad_ffn_gain,
        grad_router,
        grad_gate,
        grad_up,
        grad_down,
        grad_shared_gate,
        grad_shared_up,
        grad_shared_down,
    )


def solution(mesh):
    return jax.shard_map(
        per_device,
        mesh=mesh,
        in_specs=(
            P("gy", "gx"),
            P("gy", None),
            P("gx", None),
            P("gx", "gy"),
            P("gx", "gy"),
            P(),
            P(None, "gy"),
            P("gy", "gx"),
            P("gx"),
            P("gx"),
            P("gx", None),
            P("gy", "gx", None),
            P("gy", "gx", None),
            P("gy", None, "gx"),
            P("gx", "gy"),
            P("gx", "gy"),
            P("gy", "gx"),
            P("gy", "gx"),
        ),
        out_specs=(
            P("gy", "gx"),
            P("gy", "gx"),
            P("gx", "gy"),
            P("gx", "gy"),
            P(),
            P(None, "gy"),
            P("gy", "gx"),
            P("gx"),
            P("gx"),
            P("gx", None),
            P("gy", "gx", None),
            P("gy", "gx", None),
            P("gy", None, "gx"),
            P("gx", "gy"),
            P("gx", "gy"),
            P("gy", "gx"),
        ),
        check_vma=False,
    )
```

profile of v0, /device:TPU:0, one launch (start us, length us, event | category | flops | bytes accessed | tf_op | source)
XLA Modules:
  0.0 2229.7 jit_solution(1827097208241376168)
XLA Ops:
  24.8 45.6 %all-gather.12.cloned.1.call-done = bf16[4096,512]{1,0:T(8,128)(2,1)} async-done(((bf16[512,512]{1,0:T(8,128)(2,1)}), bf16[4096,512]{1,0:T(8,128)(2,1)}) %all-gather.12.cloned.1.call-update) | async-done | bytes 4194320 | tf_op jit(solution)/shard_map/all_gather | solution.py:40
  78.0 78.9 %reduce-scatter.15.cloned.1.call-done = f32[1024,456]{0,1:T(8,128)} async-done(((f32[4096,456]{0,1:T(8,128)}), f32[1024,456]{0,1:T(8,128)}) %reduce-scatter.15.cloned.1.call-update) | async-done | bytes 1867792 | tf_op jit(solution)/shard_map/reduce_scatter | solution.py:48
  164.8 17.0 all-gather.14.cloned.1.call-done
  188.0 19.4 while.30
  208.5 35.2 %all-gather.16.cloned.1.call-done = bf16[4096,256]{1,0:T(8,128)(2,1)} async-done(((bf16[1024,256]{1,0:T(8,128)(2,1)}), bf16[4096,256]{1,0:T(8,128)(2,1)}) %all-gather.16.cloned.1.call-update) | async-done | bytes 2097168 | tf_op jit(solution)/shard_map/all_gather | solution.py:44
  249.2 49.6 %reduce-scatter.17.cloned.1.call-done = bf16[512,512]{1,0:T(8,128)(2,1)} async-done(((bf16[4096,512]{1,0:T(8,128)(2,1)}), bf16[512,512]{1,0:T(8,128)(2,1)}) %reduce-scatter.17.cloned.1.call-update) | async-done | bytes 524304 | tf_op jit(solution)/shard_map/reduce_scatter | solution.py:54
  315.4 31.9 %reduce-window.6 = s32[64,24,128]{2,1,0:T(8,128)S(1)} reduce-window(s32[64,24,128]{2,1,0:T(8,128)} %fusion.66, s32[]{:T(128)} %constant.259.clone.1), window={size=1x1x128 pad=0_0x0_0x127_0}, to_apply=%region_15.16 | reduce-window | flops 24969216 | bytes 1572868 | tf_op jit(solution)/shard_map/reduce-window
  385.2 19.8 gather_fusion.2
  416.6 126.5 %all-to-all-done.2 = bf16[8,64,8,512]{3,1,2,0:T(8,128)(2,1)} async-done(((bf16[8,64,8,512]{3,1,2,0:T(8,128)(2,1)}), bf16[8,64,8,512]{3,1,2,0:T(8,128)(2,1)}, u32[]{:S(2)}, u32[]{:S(2)}) %all-to-all-start.2) | async-done | bytes 4194336 | tf_op jit(solution)/shard_map/all_to_all | solution.py:76
  573.4 17.3 gather_fusion
  632.4 63.2 %all-to-all-done = bf16[8,64,8,512]{3,1,2,0:T(8,128)(2,1)} async-done(((bf16[8,64,8,512]{3,1,2,0:T(8,128)(2,1)}), bf16[8,64,8,512]{3,1,2,0:T(8,128)(2,1)}, u32[]{:S(2)}, u32[]{:S(2)}) %all-to-all-start) | async-done | bytes 4194336 | tf_op jit(solution)/shard_map/all_to_all | solution.py:76
  698.2 22.5 %convolution_convert_fusion = bf16[8,2816,512]{2,1,0:T(8,128)(2,1)} fusion(bf16[512,8,512]{2,0,1:T(8,128)(2,1)S(1)} %bitcast.231, bf16[8,512,1408]{1,2,0:T(8,128)(2,1)} %copy.149, bf16[8,512,1408]{1,2,0:T(8,128)(2,1)} %copy.148), kind=kOutput, calls=%fused_computation.64 | convolution fusion | flops 11868831744 | bytes 50331648 | tf_op jit(solution)/shard_map/sed,edf->sef/dot_general | solution.py:340
  720.8 28.7 %copy.185 = bf16[512,22528]{1,0:T(8,128)(2,1)} copy(bf16[512,22528]{0,1:T(8,128)(2,1)} %bitcast.227) | data formatting | bytes 46137344
  772.9 178.6 %reduce-scatter.31.cloned.1.call-done = bf16[128,22528]{1,0:T(8,128)(2,1)} async-done(((bf16[512,22528]{1,0:T(8,128)(2,1)}), bf16[128,22528]{1,0:T(8,128)(2,1)}) %reduce-scatter.31.cloned.1.call-update) | async-done | bytes 5767184
  977.8 42.6 %reduce-scatter.23.cloned.1.call-done = f32[1024,352]{0,1:T(8,128)} async-done(((f32[4096,352]{0,1:T(8,128)}), f32[1024,352]{0,1:T(8,128)}) %reduce-scatter.23.cloned.1.call-update) | async-done | bytes 1441808 | tf_op jit(solution)/shard_map/reduce_scatter | solution.py:48
  1020.3 115.7 %reduce-scatter.19.cloned.1.call-done = f32[1024,704]{0,1:T(8,128)} async-done(((f32[4096,704]{0,1:T(8,128)}), f32[1024,704]{0,1:T(8,128)}) %reduce-scatter.19.cloned.1.call-update) | async-done | bytes 2883600 | tf_op jit(solution)/shard_map/reduce_scatter | solution.py:48
  1146.8 105.4 %all-gather.18.cloned.1.call-done = bf16[512,8,1408]{2,0,1:T(8,128)(2,1)} async-done(((bf16[128,8,1408]{2,0,1:T(8,128)(2,1)}), bf16[512,8,1408]{2,0,1:T(8,128)(2,1)}) %all-gather.18.cloned.1.call-update) | async-done | bytes 11534352 | tf_op jit(solution)/shard_map/all_gather | solution.py:72
  1272.6 47.2 %all-gather.28.cloned.1.call-done = bf16[4096,704]{0,1:T(8,128)(2,1)} async-done(((bf16[1024,704]{0,1:T(8,128)(2,1)}), bf16[4096,704]{0,1:T(8,128)(2,1)}) %all-gather.28.cloned.1.call-update) | async-done | bytes 5767184 | tf_op jit(solution)/shard_map/all_gather | solution.py:44
  1327.6 204.5 %all-gather.24.cloned.1.call-done = bf16[512,8,2816]{2,0,1:T(8,128)(2,1)} async-done(((bf16[128,8,2816]{2,0,1:T(8,128)(2,1)}), bf16[512,8,2816]{2,0,1:T(8,128)(2,1)}) %all-gather.24.cloned.1.call-update) | async-done | bytes 23068688 | tf_op jit(solution)/shard_map/all_gather | solution.py:72
  1532.1 23.2 %fusion.48 = bf16[8,512,512]{1,2,0:T(8,128)(2,1)} fusion(bf16[512,8,2816]{2,0,1:T(8,128)(2,1)} %all-gather.24.cloned.1.call-done, bf16[8,512,1408]{1,2,0:T(8,128)(2,1)} %copy.149, bf16[8,512,1408]{1,2,0:T(8,128)(2,1)} %copy.148), kind=kOutput, calls=%fused_computation.87 | convolution fusion | flops 11859394560 | bytes 50331648 | tf_op jit(solution)/shard_map/sef,edf->sed/dot_general | solution.py:397
  1602.2 21.4 psum.94
  1624.0 48.9 %all-to-all-done.3 = bf16[8,64,8,512]{3,1,2,0:T(8,128)(2,1)} async-done(((bf16[8,64,8,512]{3,1,2,0:T(8,128)(2,1)}), bf16[8,64,8,512]{3,1,2,0:T(8,128)(2,1)}, u32[]{:S(2)}, u32[]{:S(2)}) %all-to-all-start.3) | async-done | bytes 4194336 | tf_op jit(solution)/shard_map/all_to_all | solution.py:76
  1723.2 44.1 %all-gather.30.cloned.1.call-done = bf16[4096,512]{1,0:T(8,128)(2,1)} async-done(((bf16[512,512]{1,0:T(8,128)(2,1)}), bf16[4096,512]{1,0:T(8,128)(2,1)}) %all-gather.30.cloned.1.call-update) | async-done | bytes 4194320 | tf_op jit(solution)/shard_map/all_gather | solution.py:40
  1774.6 49.7 %reduce-scatter.27.cloned.1.call-done = f32[1024,256]{1,0:T(8,128)} async-done(((f32[4096,256]{1,0:T(8,128)}), f32[1024,256]{1,0:T(8,128)}) %reduce-scatter.27.cloned.1.call-update) | async-done | bytes 1048592 | tf_op jit(solution)/shard_map/reduce_scatter | solution.py:48
  1826.6 67.1 %while.31 = (s32[]{:T(128)}, f32[2,512,2,192]{1,0,3,2:T(2,128)}, f32[2,1024,2,192]{1,3,2,0:T(8,128)}, f32[2,1024,2,128]{1,3,2,0:T(8,128)}, s32[2]{0:T(128)S(1)},...) while((s32[]{:T(128)}, f32[2,512,2,192]{1,0,3,2:T(2,128)}, ...), condition=%wide.region_36.37_spmd, body=%wide.region_34.36_spmd.sunk | while | flops 1763246080 | bytes 60863928 | solution.py:208
  1907.9 57.6 %all-reduce.13.cloned.1.call-done = (bf16[1024,512]{0,1:T(8,128)(2,1)}, bf16[1024,64]{0,1:T(8,128)(2,1)}, bf16[512,64]{0,1:T(8,128)(2,1)}) async-done(((bf16[1024,512]{0,1:T(8,128)(2,1)}, bf16[1024,64]{0,1:T(8,128)(2,1)}, bf16[512,64]{0,1:T(8,128)(2,1)}), (bf16[1024,512]{0,1:T(8,128)(2,1)}, bf16[1024,64]{0,1:T(8,128)(2,1)}, bf16[512,64]{0,1:T(8,128)(2,1)})) %all-reduce.13.cloned.1.call-update) | async-done | bytes 1245200 | tf_op jit(solution)/shard_map/psum | solution.py:36
  1971.3 47.2 %all-gather.32.cloned.1.call-done = bf16[4096,456]{0,1:T(8,128)(2,1)} async-done(((bf16[1024,456]{0,1:T(8,128)(2,1)}), bf16[4096,456]{0,1:T(8,128)(2,1)}) %all-gather.32.cloned.1.call-update) | async-done | bytes 3735568 | tf_op jit(solution)/shard_map/all_gather | solution.py:44
  2025.2 37.7 %all-gather.22.cloned.1.call-done = bf16[4096,352]{0,1:T(8,128)(2,1)} async-done(((bf16[1024,352]{0,1:T(8,128)(2,1)}), bf16[4096,352]{0,1:T(8,128)(2,1)}) %all-gather.22.cloned.1.call-update) | async-done | bytes 2883600 | tf_op jit(solution)/shard_map/all_gather | solution.py:44
  2097.8 27.3 %fusion.106 = f32[8,512,2816]{2,1,0:T(8,128)} fusion(bf16[512,8,512]{2,0,1:T(8,128)(2,1)} %bitcast.232, bf16[512,8,2816]{2,0,1:T(8,128)(2,1)} %all-gather.24.cloned.1.call-done), kind=kOutput, calls=%fused_computation.229 | convolution fusion | flops 11811160064 | bytes 73400320 | tf_op jit(solution)/shard_map/sed,sef->edf/dot_general | solution.py:394
  2125.1 32.2 %fusion.96 = (f32[8,512,1408]{2,1,0:T(8,128)}, f32[8,512,1408]{2,1,0:T(8,128)}) fusion(f32[8,512,2816]{2,1,0:T(8,128)} %fusion.106), kind=kLoop, calls=%fused_computation.219 | loop fusion | bytes 92274688 | tf_op jit(solution)/shard_map/slice | solution.py:401
  2173.1 16.3 all-reduce.3
  2203.2 16.9 all-reduce.11.cloned.1.call-done
  (432 shorter events, 548.7 us)
Async XLA Ops:
  7.2 177.8 %copy-start = (bf16[512,512]{1,0:T(8,128)(2,1)S(1)}, bf16[512,512]{1,0:T(8,128)(2,1)}, u32[]{:S(2)}) copy-start(bf16[512,512]{1,0:T(8,128)(2,1)} %param.28) | copy-start | bytes 1572868
  7.2 63.2 %all-gather.12.cloned.1.call-start = ((), (), s32[]{:S(2)}) async-start(), calls=%async_computation.14 | async-start | bytes 4718592 | tf_op jit(solution)/shard_map/all_gather | solution.py:40
  23.8 133.1 %reduce-scatter.15.cloned.1.call-start = ((), (), s32[]{:S(2)}) async-start(), calls=%async_computation.15 | async-start | bytes 9338880 | tf_op jit(solution)/shard_map/reduce_scatter | solution.py:48
  78.0 80.7 %copy-start.82 = (s32[1,2]{1,0:T(1,128)S(1)}, s32[1,2]{1,0:T(1,128)}, u32[]{:S(2)}) copy-start(s32[1,2]{1,0:T(1,128)} %param.24) | copy-start | bytes 28
  78.0 82.6 %copy-start.83 = (bf16[512]{0:T(512)(128)(2,1)S(1)}, bf16[512]{0:T(512)(128)(2,1)}, u32[]{:S(2)}) copy-start(bf16[512]{0:T(512)(128)(2,1)} %param.27) | copy-start | bytes 3076
  78.0 103.8 %all-gather.14.cloned.1.call-start = ((), (), s32[]{:S(2)}) async-start(), calls=%async_computation.16 | async-start | bytes 1327104 | tf_op jit(solution)/shard_map/all_gather | solution.py:289
  158.6 85.1 %all-gather.16.cloned.1.call-start = ((), (), s32[]{:S(2)}) async-start(), calls=%async_computation.17 | async-start | bytes 2621440 | tf_op jit(solution)/shard_map/all_gather | solution.py:44
  208.4 90.4 %reduce-scatter.17.cloned.1.call-start = ((), (), s32[]{:S(2)}) async-start(), calls=%async_computation.18 | async-start | bytes 4718592 | tf_op jit(solution)/shard_map/reduce_scatter | solution.py:54
  248.6 127.3 %all-reduce.9.cloned.1.call-start = ((), (), s32[]{:S(2)}) async-start(), calls=%async_computation.19 | async-start | bytes 262144 | tf_op jit(solution)/shard_map/psum | solution.py:32
  313.0 436.6 %all-gather.26.cloned.1.call-start = ((), (), s32[]{:S(2)}) async-start(), calls=%async_computation.26 | async-start | bytes 4718592 | tf_op jit(solution)/shard_map/all_gather | solution.py:40
  410.9 132.3 %all-to-all-start.2 = ((bf16[8,64,8,512]{3,1,2,0:T(8,128)(2,1)}), bf16[8,64,8,512]{3,1,2,0:T(8,128)(2,1)}, u32[]{:S(2)}, u32[]{:S(2)}) async-start(bf16[8,64,8,512]{3,1,2,0:T(8,128)(2,1)} %copy.161), calls=%async_computation.6 | async-start | bytes 8388608 | tf_op jit(solution)/shard_map/all_to_all | solution.py:76
  415.4 342.5 %all-gather.20.cloned.1.call-start = ((), (), s32[]{:S(2)}) async-start(), calls=%async_computation.21 | async-start | bytes 4718592 | tf_op jit(solution)/shard_map/all_gather | solution.py:40
  416.2 350.4 %reduce-scatter.33.cloned.1.call-start = ((), (), s32[]{:S(2)}) async-start(), calls=%async_computation.36 | async-start | bytes 14417920
  596.9 98.7 %all-to-all-start = ((bf16[8,64,8,512]{3,1,2,0:T(8,128)(2,1)}), bf16[8,64,8,512]{3,1,2,0:T(8,128)(2,1)}, u32[]{:S(2)}, u32[]{:S(2)}) async-start(bf16[8,64,8,512]{3,1,2,0:T(8,128)(2,1)} %copy.155), calls=%async_computation.2 | async-start | bytes 8388608 | tf_op jit(solution)/shard_map/all_to_all | solution.py:76
  601.6 350.0 %reduce-scatter.31.cloned.1.call-start = ((), (), s32[]{:S(2)}) async-start(), calls=%async_computation.35 | async-start | bytes 28835840
  749.5 270.8 %reduce-scatter.23.cloned.1.call-start = ((), (), s32[]{:S(2)}) async-start(), calls=%async_computation.27 | async-start | bytes 7208960 | tf_op jit(solution)/shard_map/reduce_scatter | solution.py:48
  756.8 379.2 %reduce-scatter.19.cloned.1.call-start = ((), (), s32[]{:S(2)}) async-start(), calls=%async_computation.22 | async-start | bytes 14417920 | tf_op jit(solution)/shard_map/reduce_scatter | solution.py:48
  766.5 485.7 %all-gather.18.cloned.1.call-start = ((), (), s32[]{:S(2)}) async-start(), calls=%async_computation.20 | async-start | bytes 14417920 | tf_op jit(solution)/shard_map/all_gather | solution.py:72
  977.7 342.0 %all-gather.28.cloned.1.call-start = ((), (), s32[]{:S(2)}) async-start(), calls=%async_computation.28 | async-start | bytes 7208960 | tf_op jit(solution)/shard_map/all_gather | solution.py:44
  1141.3 390.8 %all-gather.24.cloned.1.call-start = ((), (), s32[]{:S(2)}) async-start(), calls=%async_computation.25 | async-start | bytes 28835840 | tf_op jit(solution)/shard_map/all_gather | solution.py:72
  1267.6 292.5 %all-to-all-start.1 = ((bf16[8,64,8,512]{3,1,2,0:T(8,128)(2,1)}), bf16[8,64,8,512]{3,1,2,0:T(8,128)(2,1)}, u32[]{:S(2)}, u32[]{:S(2)}) async-start(bf16[8,64,8,512]{3,1,2,0:T(8,128)(2,1)} %copy.158), calls=%async_computation.3 | async-start | bytes 8388608 | tf_op jit(solution)/shard_map/all_to_all | solution.py:76
  1272.3 437.2 %reduce-scatter.25.cloned.1.call-start = ((), (), s32[]{:S(2)}) async-start(), calls=%async_computation.29 | async-start | bytes 4718592 | tf_op jit(solution)/shard_map/reduce_scatter | solution.py:54
  1560.1 112.9 %all-to-all-start.3 = ((bf16[8,64,8,512]{3,1,2,0:T(8,128)(2,1)}), bf16[8,64,8,512]{3,1,2,0:T(8,128)(2,1)}, u32[]{:S(2)}, u32[]{:S(2)}) async-start(bf16[8,64,8,512]{3,1,2,0:T(8,128)(2,1)} %copy.166), calls=%async_computation.7 | async-start | bytes 8388608 | tf_op jit(solution)/shard_map/all_to_all | solution.py:76
  1564.9 202.3 %all-gather.30.cloned.1.call-start = ((), (), s32[]{:S(2)}) async-start(), calls=%async_computation.30 | async-start | bytes 4718592 | tf_op jit(solution)/shard_map/all_gather | solution.py:40
  1723.2 101.2 %reduce-scatter.27.cloned.1.call-start = ((), (), s32[]{:S(2)}) async-start(), calls=%async_computation.31 | async-start | bytes 5242880 | tf_op jit(solution)/shard_map/reduce_scatter | solution.py:48
  1772.8 192.7 %all-reduce.13.cloned.1.call-start = ((), (), s32[]{:S(2)}) async-start(), calls=%async_computation.37 | async-start | bytes 2490368 | tf_op jit(solution)/shard_map/psum | solution.py:36
  1899.8 65.7 %copy-start.53 = (f32[1024]{0:T(1024)S(1)}, f32[1024]{0:T(1024)}, u32[]{:S(2)}) copy-start(f32[1024]{0:T(1024)} %copy-done.52) | copy-start | bytes 12292
  1905.4 113.1 %all-gather.32.cloned.1.call-start = ((), (), s32[]{:S(2)}) async-start(), calls=%async_computation.32 | async-start | bytes 4669440 | tf_op jit(solution)/shard_map/all_gather | solution.py:44
  1970.5 92.4 %all-gather.22.cloned.1.call-start = ((), (), s32[]{:S(2)}) async-start(), calls=%async_computation.23 | async-start | bytes 3604480 | tf_op jit(solution)/shard_map/all_gather | solution.py:44
  1971.2 200.3 %reduce-scatter.29.cloned.1.call-start = ((), (), s32[]{:S(2)}) async-start(), calls=%async_computation.33 | async-start | bytes 4718592 | tf_op jit(solution)/shard_map/reduce_scatter | solution.py:54
  2025.2 174.9 %reduce-scatter.21.cloned.1.call-start = ((), (), s32[]{:S(2)}) async-start(), calls=%async_computation.24 | async-start | bytes 4718592 | tf_op jit(solution)/shard_map/reduce_scatter | solution.py:54
  2069.2 150.9 %all-reduce.11.cloned.1.call-start = ((), (), s32[]{:S(2)}) async-start(), calls=%async_computation.34 | async-start | bytes 2097152 | tf_op jit(solution)/shard_map/psum | solution.py:32
  (84 other events, 1976.9 us)
Sparse Core Ops, SparseCore 0:
  23.9 46.5 all-gather.11
  78.1 78.7 reduce-scatter.14
  159.1 22.6 all-gather.13
  208.5 35.0 all-gather.15
  248.7 50.0 reduce-scatter.16
  313.1 38.4 all-reduce.8
  353.3 47.1 all-gather.25
  418.5 79.8 all-gather.19
  572.5 109.1 reduce-scatter.32
  749.6 201.8 reduce-scatter.30
  954.5 65.7 reduce-scatter.22
  1023.9 112.1 reduce-scatter.18
  1138.4 113.7 all-gather.17
  1253.9 65.7 all-gather.27
  1322.1 210.0 all-gather.23
  1534.3 62.5 reduce-scatter.24
  1723.3 43.9 all-gather.29
  1772.9 51.4 reduce-scatter.26
  1905.5 59.9 all-reduce.12
  1970.6 47.8 all-gather.31
  2021.1 41.7 all-gather.21
  2065.3 49.9 reduce-scatter.28
  2117.8 48.1 reduce-scatter.20
  2169.2 50.8 all-reduce.10
where the time goes:
time: 2250 us; the launch traced here: 2230 us
  waiting for transfers between devices  1410 us (63%)
  local copies, waits for them, and re-layouts  343 us (15%)
  matrix products  226 us (10%)
  other arithmetic  118 us (5%)
  blocking collectives  78.5 us (3%)
    all_gather x2, waiting for transfers between devices, expert_rows(): lax.all_gather(value, 'gx', axis=0, tiled=True)  310 us
    reduce_scatter x4, waiting for transfers between devices, inner_total(): lax.psum_scatter(function(jnp.int32(0), lax.axis_size('gx') * rows), 'gx'...  287 us
    all_to_all x4, waiting for transfers between devices, expert_swap(): return lax.all_to_all(value, 'gy', split_axis=0, concat_axis=0, tiled=True)  239 us
    unnamed x26, waiting for transfers between devices  181 us
    all_gather x4, waiting for transfers between devices, collect_rows(): return lax.all_gather(value, 'gx', axis=0, tiled=True)  167 us
    unnamed x181, local copies, waits for them, and re-layouts  94.8 us
    all_gather x4, waiting for transfers between devices, spread_rows(): return lax.all_gather(value, 'gy', axis=0, tiled=True)  89.7 us
    psum x5, blocking collectives, feature_total(): return lax.psum(value, 'gx')  62.2 us
  transfers between devices with their start and end apart: 28, of which 20 were waited for; matrix products, arithmetic and copies ran while one was open for 24% of the time, Pallas kernels for 0%

commit v1 on v0

v1 whole, which is shorter than its diff:
```python
import functools
import math

import jax
import jax.numpy as jnp
from jax import lax
from jax.experimental import pallas as pl
from jax.experimental.pallas import tpu as pltpu
from jax.sharding import PartitionSpec as P

D = 2048
DN = 128
DR = 64
DV = 128
L = 512
EXPERTS = 64
FF = 1408
TOPK = 6
SEQ_LEN = 1024
PIECE = 256


EPS = 1e-06
BF16 = jnp.bfloat16
F32 = jnp.float32
VMEM_LIMIT = 56 * 1024 * 1024


def params():
    return pltpu.CompilerParams(vmem_limit_bytes=VMEM_LIMIT)


def cost(flops, read, written):
    return pl.CostEstimate(flops=flops, bytes_accessed=read + written, transcendentals=0)


def after(value, *others):
    return lax.optimization_barrier((value, others))[0]


def swap(value, bit):
    return lax.ppermute(value, "gx", [(i, i ^ bit) for i in range(4)])


def square():
    return lax.axis_size("gx") == 4


def place():
    me = lax.axis_index("gx")
    return me & 1, me >> 1


def pick(value, index, axis):
    return lax.dynamic_index_in_dim(value, index, axis, keepdims=False)


def collect(block):
    if not square():
        return lax.all_gather(block, "gx", axis=0, tiled=False)
    half = block.shape[0] // 2
    from_x = swap(block, 1)
    from_y = swap(block, 2)
    across = jnp.concatenate([swap(from_y[:half], 1), swap(from_x[half:], 2)], axis=0)
    me = lax.axis_index("gx")
    whole = jnp.zeros((4,) + block.shape, block.dtype)
    for index, value in ((me, block), (me ^ 1, from_x), (me ^ 2, from_y), (me ^ 3, across)):
        whole = lax.dynamic_update_index_in_dim(whole, value, index, 0)
    return whole


def collect_rows(block):
    whole = collect(block)
    return whole.reshape((-1,) + block.shape[1:])


def feature_total(value):
    return lax.psum(value, "gx")


def square_total(value):
    if not square():
        return lax.psum(value, "gx")
    value = value + swap(value, 1)
    return value + swap(value, 2)


def spread_rows(value):
    return lax.all_gather(value, "gy", axis=0, tiled=True)


def outer_total(partial):
    total = lax.psum_scatter(partial.astype(BF16), "gy", scatter_dimension=0, tiled=True)
    return total.astype(F32)


def to_tokens(value):
    return lax.all_to_all(value, "gx", split_axis=0, concat_axis=1, tiled=True)


def to_features(value):
    return lax.all_to_all(value, "gx", split_axis=1, concat_axis=0, tiled=True)


def dot(a, b):
    return jnp.dot(a, b, preferred_element_type=F32)


def dot_nt(a, b):
    return lax.dot_general(a, b, (((1,), (1,)), ((), ())), preferred_element_type=F32)


def dot_tn(a, b):
    return lax.dot_general(a, b, (((0,), (0,)), ((), ())), preferred_element_type=F32)


def one_hot_kernel(cap, code_ref, out_ref):
    experts = code_ref.shape[1]
    tokens, slots = out_ref.shape
    column = lax.broadcasted_iota(jnp.int32, (experts, slots), 1)
    low = lax.broadcasted_iota(jnp.int32, (experts, slots), 0) * cap
    inside = (column >= low) & (column < low + cap)
    expand = jnp.where(inside, 1.0, 0.0).astype(BF16)
    offset = jnp.sum(jnp.where(inside, column - low, 0).astype(F32), axis=0, keepdims=True)
    wide = dot(code_ref[...].astype(BF16), expand)
    out_ref[...] = jnp.where(wide == offset, 1.0, 0.0).astype(BF16)


def one_hot(code, cap, blocks):
    tokens, experts = code.shape
    block = tokens // blocks
    return pl.pallas_call(
        functools.partial(one_hot_kernel, cap),
        grid=(blocks,),
        in_specs=[pl.BlockSpec((block, experts), lambda b: (b, 0))],
        out_specs=pl.BlockSpec((block, experts * cap), lambda b: (b, 0)),
        out_shape=jax.ShapeDtypeStruct((tokens, experts * cap), BF16),
        compiler_params=params(),
        name="one_hot",
    )(code)


def dispatch_kernel(chosen_ref, rows_ref, out_ref):
    moved = dot_tn(chosen_ref[...], rows_ref[...]).astype(BF16)
    out_ref[...] = moved.reshape(out_ref.shape)


def dispatch(chosen, rows, cap, blocks):
    tokens, width = rows.shape
    slots = chosen.shape[1]
    experts = slots // cap
    block = tokens // blocks
    return pl.pallas_call(
        dispatch_kernel,
        grid=(blocks,),
        in_specs=[
            pl.BlockSpec((block, slots), lambda b: (b, 0)),
            pl.BlockSpec((block, width), lambda b: (b, 0)),
        ],
        out_specs=pl.BlockSpec((experts, cap, width), lambda b: (0, b, 0)),
        out_shape=jax.ShapeDtypeStruct((experts, blocks * cap, width), BF16),
        compiler_params=params(),
        cost_estimate=cost(2 * tokens * slots * width, 4 * tokens * width, 2 * tokens * width),
        name="dispatch",
    )(chosen, rows)


def combine_kernel(groups, chosen_ref, *refs):
    out_ref = refs[-1]
    width = out_ref.shape[1]
    pieces = [ref[...].reshape(-1, width) for ref in refs[:groups]]
    slots = pieces[0] if groups == 1 else jnp.concatenate(pieces, axis=0)
    total = dot(chosen_ref[...], slots)
    for ref in refs[groups:-1]:
        total += ref[...].astype(F32)
    out_ref[...] = total.astype(out_ref.dtype)


def combine(chosen, pieces, cap, blocks, extra=()):
    tokens, slots = chosen.shape
    block = tokens // blocks
    width = pieces[0].shape[-1]
    specs = [pl.BlockSpec((block, slots), lambda b: (b, 0))]
    specs += [pl.BlockSpec((p.shape[0], cap, width), lambda b: (0, b, 0)) for p in pieces]
    specs += [pl.BlockSpec((block, width), lambda b: (b, 0)) for _ in extra]
    return pl.pallas_call(
        functools.partial(combine_kernel, len(pieces)),
        grid=(blocks,),
        in_specs=specs,
        out_specs=pl.BlockSpec((block, width), lambda b: (b, 0)),
        out_shape=jax.ShapeDtypeStruct((tokens, width), BF16),
        compiler_params=params(),
        cost_estimate=cost(2 * tokens * slots * width, 4 * tokens * width, 2 * tokens * width),
        name="combine",
    )(chosen, *pieces, *extra)


def group_kernel(parts, weights, adds, transposed, picks_ref, *refs):
    rows = [ref[0, 0] for ref in refs[:parts]]
    source = rows[0] if parts == 1 else jnp.concatenate(rows, axis=0)
    out_ref = refs[-1]
    extra = refs[parts + weights : parts + weights + adds]
    for number in range(weights):
        weight = refs[parts + number][0]
        total = dot_nt(source, weight) if transposed else dot(source, weight)
        for ref in extra:
            total += ref[0, number, 0].astype(F32)
        out_ref[0, number] = total.astype(out_ref.dtype).reshape(out_ref.shape[2:])


def group(rows, picks, parts, weights, first, count, transposed=False, adds=(), kind=BF16, by_quarter=False):
    slots, depth = rows.shape[2:]
    width = weights[0].shape[1] if transposed else weights[0].shape[2]
    many = len(weights)

    def row_spec(part):
        if by_quarter:
            return pl.BlockSpec((1, 1, slots, depth), lambda e, p: (p[part], first + e, 0, 0))
        return pl.BlockSpec((1, 1, slots, depth), lambda e, p: (first + e, p[part], 0, 0))

    def add_spec(number):
        return pl.BlockSpec((1, many, 1, slots, width), lambda e, p: (e, 0, p[parts + number], 0, 0))

    specs = [row_spec(part) for part in range(parts)]
    for weight in weights:
        if by_quarter:
            specs.append(pl.BlockSpec((1,) + weight.shape[1:], lambda e, p: (0, 0, 0)))
        else:
            specs.append(pl.BlockSpec((1,) + weight.shape[1:], lambda e, p: (first + e, 0, 0)))
    specs += [add_spec(number) for number in range(len(adds))]
    return pl.pallas_call(
        functools.partial(group_kernel, parts, many, len(adds), transposed),
        grid_spec=pltpu.PrefetchScalarGridSpec(
            num_scalar_prefetch=1,
            grid=(count,),
            in_specs=specs,
            out_specs=pl.BlockSpec((1, many, parts, slots, width), lambda e, p: (e, 0, 0, 0, 0)),
        ),
        out_shape=jax.ShapeDtypeStruct((count, many, parts, slots, width), kind),
        compiler_params=params(),
        cost_estimate=cost(
            2 * many * count * parts * slots * depth * width,
            2 * many * count * depth * width,
            2 * many * count * parts * slots * width,
        ),
        name="group",
    )(picks, *([rows] * parts), *weights, *adds)


def numbers(*values):
    return jnp.stack([jnp.asarray(value, jnp.int32) for value in values])


def halves(first, count):
    x, y = place()
    half = count // 2
    me = 2 * y + x
    return (
        (first, half, 1, numbers(1 - x, 3 - x), numbers(2 * (1 - y) + x, 1 - y), numbers(me, y, 0)),
        (first + half, half, 2, numbers(2 - 2 * y, 3 - 2 * y), numbers(2 * y + 1 - x, 1 - x), numbers(me, x, 0)),
    )


def expert_body(gate_pre, up_pre, grad_hidden, gate):
    sigma = jax.nn.sigmoid(gate_pre)
    act = gate_pre * sigma
    hidden = (act * up_pre).astype(BF16).astype(F32)
    grad_gate = jnp.sum(hidden * grad_hidden, axis=-1, keepdims=True)
    scaled = (gate * hidden).astype(BF16)
    grad = gate * grad_hidden
    grad_gate_pre = (grad * up_pre * sigma * (1.0 + gate_pre * (1.0 - sigma))).astype(BF16)
    grad_up_pre = (grad * act).astype(BF16)
    return scaled, grad_gate_pre, grad_up_pre, grad_gate


def neighbours():
    me = lax.axis_index("gx")
    x = me % 2
    y = me // 2
    return x, y, me + 1 - 2 * x, me + 2 - 4 * y


def greet(*others):
    barrier = pltpu.get_barrier_semaphore()
    for other in others:
        pl.semaphore_signal(
            barrier, inc=1, device_id={"gx": other}, device_id_type=pl.DeviceIdType.MESH
        )
    pl.semaphore_wait(barrier, len(others))


def remote(source, target, sent, received, other):
    return pltpu.make_async_remote_copy(
        src_ref=source,
        dst_ref=target,
        send_sem=sent,
        recv_sem=received,
        device_id={"gx": other},
        device_id_type=pl.DeviceIdType.MESH,
    )


def experts_kernel(
    rows,
    w_gate,
    w_up,
    grad_hidden,
    factors,
    own_out,
    x_out,
    y_out,
    d_out,
    hid_out,
    back_out,
    gate_out,
    first_sent,
    first,
    second,
    weights,
    loaded,
    first_send,
    first_recv,
    second_send,
    second_recv,
    x_send,
    x_recv,
    y_send,
    y_recv,
    d_send,
    d_recv,
    own_sem,
    weight_sem,
    load_sem,
):
    x, y, x_other, y_other = neighbours()
    me = 2 * y + x
    across = 3 - me
    pairs = rows.shape[0] // 2
    slots = rows.shape[2]
    greet(x_other, y_other)

    def side(odd):
        if odd:
            return y_other, x_other, (2 - 2 * y, 3 - 2 * y), 2 * y + 1 - x, 1 - x, x
        return x_other, y_other, (1 - x, 3 - x), 2 * (1 - y) + x, 1 - y, y

    def fetch(pair):
        for odd in range(2):
            expert = 2 * pair + odd
            pltpu.make_async_copy(w_gate.at[expert], weights.at[odd, 0], weight_sem.at[odd, 0]).start()
            pltpu.make_async_copy(w_up.at[expert], weights.at[odd, 1], weight_sem.at[odd, 1]).start()

    def fetched(pair, odd):
        expert = 2 * pair + odd
        pltpu.make_async_copy(w_gate.at[expert], weights.at[odd, 0], weight_sem.at[odd, 0]).wait()
        pltpu.make_async_copy(w_up.at[expert], weights.at[odd, 1], weight_sem.at[odd, 1]).wait()

    def first_copy(pair, odd):
        expert = 2 * pair + odd
        return remote(
            first_sent.at[pair % 2, odd],
            first.at[expert],
            first_send.at[expert],
            first_recv.at[expert],
            side(odd)[0],
        )

    def second_copy(pair, odd):
        expert = 2 * pair + odd
        return remote(
            first.at[expert, side(odd)[4]],
            second.at[expert],
            second_send.at[expert],
            second_recv.at[expert],
            side(odd)[1],
        )

    def x_copy(pair, odd):
        expert = 2 * pair + odd
        source = first.at[expert, side(odd)[5]]
        return remote(source, x_out.at[expert], x_send.at[expert], x_recv.at[expert], x_other)

    def y_copy(pair, odd):
        expert = 2 * pair + odd
        source = first.at[expert, side(odd)[5]]
        return remote(source, y_out.at[expert], y_send.at[expert], y_recv.at[expert], y_other)

    def own_copy(pair, odd):
        expert = 2 * pair + odd
        return pltpu.make_async_copy(
            first.at[expert, side(odd)[5]], own_out.at[expert], own_sem.at[expert]
        )

    def far_copy(pair, odd):
        expert = 2 * pair + odd
        source = x_out if odd else y_out
        return remote(
            source.at[expert],
            d_out.at[expert],
            d_send.at[expert],
            d_recv.at[expert],
            side(odd)[0],
        )

    def send_first(pair):
        fetch(pair)
        for odd in range(2):
            expert = 2 * pair + odd

            @pl.when(pair >= 2)
            def _(odd=odd):
                first_copy(pair - 2, odd).wait_send()

            low, high = side(odd)[2]
            source = jnp.concatenate([rows[expert, low], rows[expert, high]], axis=0)
            fetched(pair, odd)
            for number in range(2):
                out = dot(source, weights[odd, number]).astype(BF16)
                first_sent[pair % 2, odd, 0, number] = out[:slots]
                first_sent[pair % 2, odd, 1, number] = out[slots:]
            first_copy(pair, odd).start()

    def send_second(pair):
        fetch(pair)
        for odd in range(2):
            expert = 2 * pair + odd
            _, _, _, quarter, spot, _ = side(odd)
            fetched(pair, odd)
            first_copy(pair, odd).wait_recv()
            for number in range(2):
                out = dot(rows[expert, quarter], weights[odd, number])
                out += first[expert, spot, number].astype(F32)
                first[expert, spot, number] = out.astype(BF16)
            second_copy(pair, odd).start()

    def finish(pair):
        fetch(pair)
        for odd in range(2):
            expert = 2 * pair + odd
            spot = side(odd)[5]
            fetched(pair, odd)
            second_copy(pair, odd).wait_recv()
            scale = factors[expert, :, 1:2]
            source = rows[expert, me]
            gate_pre, up_pre = (
                dot(source, weights[odd, number])
                + first[expert, spot, number].astype(F32)
                + second[expert, number].astype(F32)
                for number in range(2)
            )
            scaled, grad_gate_pre, grad_up_pre, grad_gate = expert_body(
                gate_pre * scale,
                up_pre * scale,
                grad_hidden[expert].astype(F32),
                factors[expert, :, 0:1],
            )
            first[expert, spot, 0] = grad_gate_pre
            first[expert, spot, 1] = grad_up_pre
            x_copy(pair, odd).start()
            y_copy(pair, odd).start()
            own_copy(pair, odd).start()
            hid_out[expert, 0] = scaled
            gate_out[expert] = grad_gate

    def pass_on(pair):
        for odd in range(2):
            (x_copy if odd else y_copy)(pair, odd).wait_recv()
            far_copy(pair, odd).start()

    def load(pair, odd, number):
        expert = 2 * pair + odd
        source = (x_out, y_out, d_out)[number]
        return pltpu.make_async_copy(
            source.at[expert], loaded.at[odd, number], load_sem.at[odd, number]
        )

    def send_back(pair):
        fetch(pair)
        for odd in range(2):
            (y_copy if odd else x_copy)(pair, odd).wait_recv()
            load(pair, odd, 0).start()
            load(pair, odd, 1).start()
        for odd in range(2):
            far_copy(pair, odd).wait_recv()
            load(pair, odd, 2).start()
        for odd in range(2):
            expert = 2 * pair + odd
            fetched(pair, odd)
            for number in range(3):
                load(pair, odd, number).wait()
            spot = side(odd)[5]
            total = None
            for number in range(2):
                source = jnp.concatenate(
                    [first[expert, spot, number]] + [loaded[odd, part, number] for part in range(3)],
                    axis=0,
                )
                part = dot_nt(source, weights[odd, number])
                total = part if total is None else total + part
            total = total.astype(BF16)
            for number, quarter in enumerate((me, x_other, y_other, across)):
                back_out[expert, quarter] = total[number * slots : (number + 1) * slots]

    def step(number, _):
        for lag, stage in enumerate((send_first, send_second, finish, pass_on, send_back)):

            @pl.when((number >= lag) & (number < pairs + lag))
            def _(lag=lag, stage=stage):
                stage(number - lag)

        return 0

    lax.fori_loop(0, pairs + 4, step, 0)

    def drain(pair, _):
        for odd in range(2):

            @pl.when(pair >= pairs - 2)
            def _(odd=odd):
                first_copy(pair, odd).wait_send()

            second_copy(pair, odd).wait_send()
            own_copy(pair, odd).wait()
            x_copy(pair, odd).wait_send()
            y_copy(pair, odd).wait_send()
            far_copy(pair, odd).wait_send()
        return 0

    lax.fori_loop(0, pairs, drain, 0)


def routed_experts(rows, w_gate, w_up, grad_hidden, factors):
    experts, quarters, slots, depth = rows.shape
    width = w_gate.shape[2]
    vmem = pl.BlockSpec(memory_space=pltpu.VMEM)
    anywhere = pl.BlockSpec(memory_space=pl.ANY)
    block = jax.ShapeDtypeStruct((experts, 2, slots, width), BF16)
    dma = pltpu.SemaphoreType.DMA
    return pl.pallas_call(
        experts_kernel,
        in_specs=[vmem, anywhere, anywhere, vmem, vmem],
        out_specs=[anywhere] * 4 + [vmem] * 3,
        out_shape=[block] * 4
        + [
            jax.ShapeDtypeStruct((experts, 1, slots, width), BF16),
            jax.ShapeDtypeStruct((experts, quarters, slots, depth), BF16),
            jax.ShapeDtypeStruct((experts, slots, 1), F32),
        ],
        scratch_shapes=[
            pltpu.VMEM((2, 2, 2, 2, slots, width), BF16),
            pltpu.VMEM((experts, 2, 2, slots, width), BF16),
            pltpu.VMEM((experts, 2, slots, width), BF16),
            pltpu.VMEM((2, 2, depth, width), BF16),
            pltpu.VMEM((2, 3, 2, slots, width), BF16),
        ]
        + [dma((experts,))] * 11
        + [dma((2, 2)), dma((2, 3))],
        compiler_params=pltpu.CompilerParams(
            collective_id=0, has_side_effects=True, vmem_limit_bytes=VMEM_LIMIT
        ),
        cost_estimate=cost(
            12 * experts * quarters * slots * depth * width, 12 * experts * depth * width, 0
        ),
        name="routed_experts",
    )(rows, w_gate, w_up, grad_hidden, factors)


def sum_kernel(base, by_quarter, own_weights, transposed, rows, weight, out, sent, first, second, held, *sems):
    first_send, first_recv, second_send, second_recv, weight_sem = sems
    x, y, x_other, y_other = neighbours()
    me = 2 * y + x
    pairs = sent.shape[0] // 2
    slots = sent.shape[2]
    greet(x_other, y_other)

    def side(odd):
        if odd:
            return y_other, x_other, (2 - 2 * y, 3 - 2 * y), 2 * y + 1 - x, 1 - x, x
        return x_other, y_other, (1 - x, 3 - x), 2 * (1 - y) + x, 1 - y, y

    def source(item, quarter):
        return rows[quarter, item] if by_quarter else rows[base + item, quarter]

    def product(value, item):
        matrix = held[item] if own_weights else weight[...]
        return dot_nt(value, matrix) if transposed else dot(value, matrix)

    def weight_copy(item):
        return pltpu.make_async_copy(weight.at[base + item], held.at[item], weight_sem.at[item])

    def first_copy(item, odd):
        return remote(sent.at[item], first.at[item], first_send.at[item], first_recv.at[item], side(odd)[0])

    def second_copy(item, odd):
        return remote(
            first.at[item, side(odd)[4]],
            second.at[item],
            second_send.at[item],
            second_recv.at[item],
            side(odd)[1],
        )

    def send_first(pair):
        for odd in range(2):
            item = 2 * pair + odd
            low, high = side(odd)[2]
            if own_weights:
                weight_copy(item).wait()
            result = product(jnp.concatenate([source(item, low), source(item, high)], axis=0), item)
            sent[item, 0] = result[:slots].astype(BF16)
            sent[item, 1] = result[slots:].astype(BF16)
            first_copy(item, odd).start()

    def send_second(pair):
        for odd in range(2):
            item = 2 * pair + odd
            _, _, _, quarter, spot, _ = side(odd)
            result = product(source(item, quarter), item)
            first_copy(item, odd).wait_recv()
            first[item, spot] = (result + first[item, spot].astype(F32)).astype(BF16)
            second_copy(item, odd).start()

    def finish(pair):
        for odd in range(2):
            item = 2 * pair + odd
            result = product(source(item, me), item) + first[item, side(odd)[5]].astype(F32)
            second_copy(item, odd).wait_recv()
            out[item] = (result + second[item].astype(F32)).astype(out.dtype)

    def fetch(item, _):
        weight_copy(item).start()
        return 0

    if own_weights:
        lax.fori_loop(0, 2 * pairs, fetch, 0)

    def step(number, _):
        for lag, stage in enumerate((send_first, send_second, finish)):

            @pl.when((number >= lag) & (number < pairs + lag))
            def _(lag=lag, stage=stage):
                stage(number - lag)

        return 0

    lax.fori_loop(0, pairs + 2, step, 0)

    def drain(pair, _):
        for odd in range(2):
            item = 2 * pair + odd
            first_copy(item, odd).wait_send()
            second_copy(item, odd).wait_send()
        return 0

    lax.fori_loop(0, pairs, drain, 0)


def square_sum(rows, weight, base, items, number, transposed, by_quarter, kind):
    slots, depth = rows.shape[2:]
    own_weights = weight.ndim == 3
    width = weight.shape[-2] if transposed else weight.shape[-1]
    vmem = pl.BlockSpec(memory_space=pltpu.VMEM)
    dma = pltpu.SemaphoreType.DMA
    held = (items,) + weight.shape[1:] if own_weights else (8, 128)
    return pl.pallas_call(
        functools.partial(sum_kernel, base, by_quarter, own_weights, transposed),
        in_specs=[vmem, pl.BlockSpec(memory_space=pl.ANY) if own_weights else vmem],
        out_specs=vmem,
        out_shape=jax.ShapeDtypeStruct((items, slots, width), kind),
        scratch_shapes=[
            pltpu.VMEM((items, 2, slots, width), BF16),
            pltpu.VMEM((items, 2, slots, width), BF16),
            pltpu.VMEM((items, slots, width), BF16),
            pltpu.VMEM(held, BF16),
        ]
        + [dma((items,))] * 5,
        compiler_params=pltpu.CompilerParams(
            collective_id=number, has_side_effects=True, vmem_limit_bytes=VMEM_LIMIT
        ),
        cost_estimate=cost(8 * items * slots * depth * width, 2 * items * depth * width, 0),
        name="square_sum",
    )(rows, weight)


def band_total(rows, weight, number, transposed=False):
    if not square():
        whole = (dot_nt(rows, weight) if transposed else dot(rows, weight)).astype(BF16)
        return lax.psum_scatter(whole, "gx", scatter_dimension=0, tiled=True).astype(F32)
    source = rows.reshape(4, 4, rows.shape[0] // 16, rows.shape[1])
    out = square_sum(source, weight, 0, 4, number, transposed, True, F32)
    return out.reshape(-1, out.shape[2])


def hidden_kernel(base, hidden, weight, x_out, y_out, d_out, out, held, loaded, *sems):
    x_send, x_recv, y_send, y_recv, d_send, d_recv, weight_sem, load_sem = sems
    x, y, x_other, y_other = neighbours()
    me = 2 * y + x
    across = 3 - me
    pairs = out.shape[0] // 2
    slots = out.shape[2]
    greet(x_other, y_other)

    def x_copy(item):
        return remote(hidden.at[base + item], x_out.at[item], x_send.at[item], x_recv.at[item], x_other)

    def y_copy(item):
        return remote(hidden.at[base + item], y_out.at[item], y_send.at[item], y_recv.at[item], y_other)

    def far_copy(item, odd):
        source, other = (x_out, y_other) if odd else (y_out, x_other)
        return remote(source.at[item], d_out.at[item], d_send.at[item], d_recv.at[item], other)

    def weight_copy(item, odd):
        return pltpu.make_async_copy(weight.at[base + item], held.at[odd], weight_sem.at[odd])

    def load(item, odd, number):
        source = (hidden.at[base + item], x_out.at[item], y_out.at[item], d_out.at[item])[number]
        return pltpu.make_async_copy(source, loaded.at[odd, number], load_sem.at[odd, number])

    def begin(pair, _):
        for odd in range(2):
            x_copy(2 * pair + odd).start()
            y_copy(2 * pair + odd).start()
        return 0

    def pass_on(pair):
        for odd in range(2):
            item = 2 * pair + odd
            (x_copy if odd else y_copy)(item).wait_recv()
            far_copy(item, odd).start()

    def multiply(pair):
        for odd in range(2):
            item = 2 * pair + odd
            weight_copy(item, odd).start()
            (y_copy if odd else x_copy)(item).wait_recv()
            for number in range(3):
                load(item, odd, number).start()
        for odd in range(2):
            item = 2 * pair + odd
            far_copy(item, odd).wait_recv()
            load(item, odd, 3).start()
        for odd in range(2):
            item = 2 * pair + odd
            weight_copy(item, odd).wait()
            for number in range(4):
                load(item, odd, number).wait()
            source = jnp.concatenate([loaded[odd, number, 0] for number in range(4)], axis=0)
            total = dot(source, held[odd]).astype(BF16)
            for number, quarter in enumerate((me, x_other, y_other, across)):
                out[item, quarter] = total[number * slots : (number + 1) * slots]

    lax.fori_loop(0, pairs, begin, 0)

    def step(number, _):
        for lag, stage in enumerate((pass_on, multiply)):

            @pl.when((number >= lag) & (number < pairs + lag))
            def _(lag=lag, stage=stage):
                stage(number - lag)

        return 0

    lax.fori_loop(0, pairs + 1, step, 0)

    def drain(pair, _):
        for odd in range(2):
            item = 2 * pair + odd
            x_copy(item).wait_send()
            y_copy(item).wait_send()
            far_copy(item, odd).wait_send()
        return 0

    lax.fori_loop(0, pairs, drain, 0)


def hidden_products(hidden, weight, base, items, number):
    slots, width = hidden.shape[2:]
    depth = weight.shape[2]
    anywhere = pl.BlockSpec(memory_space=pl.ANY)
    block = jax.ShapeDtypeStruct((items, 1, slots, width), BF16)
    dma = pltpu.SemaphoreType.DMA
    return pl.pallas_call(
        functools.partial(hidden_kernel, base),
        in_specs=[anywhere, anywhere],
        out_specs=[anywhere] * 3 + [pl.BlockSpec(memory_space=pltpu.VMEM)],
        out_shape=[block] * 3 + [jax.ShapeDtypeStruct((items, 4, slots, depth), BF16)],
        scratch_shapes=[
            pltpu.VMEM((2,) + weight.shape[1:], BF16),
            pltpu.VMEM((2, 4, 1, slots, width), BF16),
        ]
        + [dma((items,))] * 6
        + [dma((2,)), dma((2, 4))],
        compiler_params=pltpu.CompilerParams(
            collective_id=number, has_side_effects=True, vmem_limit_bytes=VMEM_LIMIT
        ),
        cost_estimate=cost(8 * items * slots * depth * width, 2 * items * depth * width, 0),
        name="hidden_products",
    )(hidden, weight)


def group_specs(groups):
    specs, values = [], []
    base = groups[0][0]
    for first, count, blocks in groups:
        for value, start in blocks:

            def index(e, p, low=first - base, top=count - 1, start=start):
                return (jnp.clip(e - low, 0, top) + start, 0, 0, 0)

            specs.append(pl.BlockSpec((1,) + value.shape[1:], index))
            values.append(value)
    return specs, values


def for_group(groups, refs, body):
    base = groups[0][0]
    each = len(groups[0][2])
    if len(groups) == 1:
        body(refs[:each])
        return
    step = pl.program_id(0)
    for number, (first, count, _) in enumerate(groups):
        low = first - base

        @pl.when((step >= low) & (step < low + count))
        def _(number=number):
            body(refs[number * each : (number + 1) * each])


def back_kernel(groups, transposed, picks_ref, *refs):
    terms, slots = groups[0][2][0][1:3]
    out_ref = refs[-1]
    weights = refs[-1 - terms : -1]

    def body(pieces):
        total = None
        for term in range(terms):
            source = jnp.concatenate([ref[0, term] for ref in pieces], axis=0)
            part = dot_nt(source, weights[term][0]) if transposed else dot(source, weights[term][0])
            total = part if total is None else total + part
        total = total.astype(BF16)
        for quarter in range(len(pieces)):
            rows = total[quarter * slots : (quarter + 1) * slots]
            out_ref[0, pl.ds(picks_ref[quarter], 1)] = rows[None]

    for_group(groups, refs, body)


def shapes_of(groups):
    return tuple(
        (first, count, tuple(b.shape for b, _ in blocks))
        for first, count, blocks in groups
    )


def back(groups, picks, weights, transposed):
    first = groups[0][0]
    count = sum(g[1] for g in groups)
    quarters = len(groups[0][2])
    terms, slots, depth = groups[0][2][0][0].shape[1:]
    width = weights[0].shape[1] if transposed else weights[0].shape[2]
    specs, values = group_specs(groups)
    specs += [pl.BlockSpec((1,) + w.shape[1:], lambda e, p: (first + e, 0, 0)) for w in weights]
    return pl.pallas_call(
        functools.partial(back_kernel, shapes_of(groups), transposed),
        grid_spec=pltpu.PrefetchScalarGridSpec(
            num_scalar_prefetch=1,
            grid=(count,),
            in_specs=specs,
            out_specs=pl.BlockSpec((1, quarters, slots, width), lambda e, p: (e, 0, 0, 0)),
        ),
        out_shape=jax.ShapeDtypeStruct((count, quarters, slots, width), BF16),
        compiler_params=params(),
        cost_estimate=cost(
            2 * terms * count * quarters * slots * depth * width,
            2 * terms * count * (quarters * slots + width) * depth,
            2 * count * quarters * slots * width,
        ),
        name="back",
    )(picks, *values, *weights)


def weight_grad_kernel(groups, flip, picks_ref, *refs):
    terms = groups[0][2][0][1]
    quarters = len(groups[0][2])
    outs = refs[-terms:]
    rows = jnp.concatenate([ref[0, 0] for ref in refs[:quarters]], axis=0)

    def body(pieces):
        for term in range(terms):
            others = jnp.concatenate([ref[0, term] for ref in pieces], axis=0)
            outs[term][0] = dot_tn(others, rows) if flip else dot_tn(rows, others)

    for_group(groups, refs[quarters:], body)


def weight_grad(rows, groups, picks, flip):
    first = groups[0][0]
    count = sum(g[1] for g in groups)
    quarters = len(groups[0][2])
    slots, depth = rows.shape[2:]
    terms, _, width = groups[0][2][0][0].shape[1:]
    specs = [
        pl.BlockSpec((1, 1, slots, depth), lambda e, p, q=quarter: (first + e, p[q], 0, 0))
        for quarter in range(quarters)
    ]
    more, values = group_specs(groups)
    shape = (width, depth) if flip else (depth, width)
    return pl.pallas_call(
        functools.partial(weight_grad_kernel, shapes_of(groups), flip),
        grid_spec=pltpu.PrefetchScalarGridSpec(
            num_scalar_prefetch=1,
            grid=(count,),
            in_specs=specs + more,
            out_specs=[pl.BlockSpec((1,) + shape, lambda e, p: (e, 0, 0))] * terms,
        ),
        out_shape=[jax.ShapeDtypeStruct((count,) + shape, F32)] * terms,
        compiler_params=params(),
        cost_estimate=cost(
            2 * terms * count * quarters * slots * depth * width,
            2 * count * quarters * slots * (depth + terms * width),
            4 * terms * count * depth * width,
        ),
        name="weight_grad",
    )(picks, *([rows] * quarters), *values)


def silu(value):
    return value * jax.nn.sigmoid(value)


def silu_grad(value):
    sigma = jax.nn.sigmoid(value)
    return sigma * (1.0 + value * (1.0 - sigma))


def rope_tables(length):
    half = DR // 2
    position = jnp.arange(length).astype(F32)
    inverse = jnp.exp(-math.log(10000.0) * jnp.arange(half).astype(F32) / half)
    angle = position[:, None] * inverse[None, :]
    cosine, sine = jnp.cos(angle), jnp.sin(angle)
    return jnp.concatenate([cosine, cosine], axis=1), jnp.concatenate([-sine, sine], axis=1)


def turn(value, cosine, sine):
    half = DR // 2
    other = jnp.concatenate([value[:, half:], value[:, :half]], axis=1)
    return value * cosine + other * sine


def visible(starts_ref, sequence):
    length = SEQ_LEN
    query = lax.broadcasted_iota(jnp.int32, (length, 1), 0)
    key = lax.broadcasted_iota(jnp.int32, (1, length), 1)
    seen = key <= query
    for number in range(2):
        low = starts_ref[sequence, number]
        seen |= ((query >= low) & (query < low + PIECE)) & ((key >= low) & (key < low + PIECE))
    return seen


def attention_kernel(heads, starts_ref, proj, latent, gain, w_expand, cos, sin, out, logs, q_out, k_out, v_out, n_out):
    scale = (DN + DR) ** (-0.5)
    cosine, sine = cos[...], sin[...]
    lat = latent[...].astype(F32)
    compressed = lat[:, :L]
    root = lax.rsqrt(jnp.mean(compressed * compressed, axis=1, keepdims=True) + EPS)
    normed = (compressed * root * gain[...].astype(F32)).astype(BF16)
    n_out[...] = normed
    key_rope = turn(lat[:, L:], cosine, sine).astype(BF16)
    expanded = dot(normed, w_expand[...]).astype(BF16)
    seen = visible(starts_ref, pl.program_id(0))
    for head in range(heads):
        plain = proj[:, head * DN : (head + 1) * DN].astype(BF16)
        start = heads * DN + head * DR
        query = jnp.concatenate([plain, turn(proj[:, start : start + DR], cosine, sine).astype(BF16)], axis=1)
        start = head * (DN + DV)
        key = jnp.concatenate([expanded[:, start : start + DN], key_rope], axis=1)
        value = expanded[:, start + DN : start + DN + DV]
        q_out[0, head] = query
        k_out[0, head] = key
        v_out[0, head] = value
        scores = jnp.where(seen, dot_nt(query, key) * scale, -1e30)
        peak = jnp.max(scores, axis=1, keepdims=True)
        expo = jnp.exp(scores - peak)
        total = jnp.sum(expo, axis=1, keepdims=True)
        weights = (expo / total).astype(BF16)
        out[:, head * DV : (head + 1) * DV] = dot(weights, value).astype(BF16)
        logs[0, head] = peak + jnp.log(total)


def attention_forward(starts, proj, latent, gain, w_expand, cosine, sine, heads):
    band = proj.shape[0]
    seqs = band // SEQ_LEN

    def rows(width):
        return pl.BlockSpec((SEQ_LEN, width), lambda s, p: (s, 0))

    def whole(shape):
        return pl.BlockSpec(shape, lambda s, p: (0, 0))

    def by_head(width):
        return pl.BlockSpec((1, heads, SEQ_LEN, width), lambda s, p: (s, 0, 0, 0))

    def head_shape(width, kind=BF16):
        return jax.ShapeDtypeStruct((seqs, heads, SEQ_LEN, width), kind)

    return pl.pallas_call(
        functools.partial(attention_kernel, heads),
        grid_spec=pltpu.PrefetchScalarGridSpec(
            num_scalar_prefetch=1,
            grid=(seqs,),
            in_specs=[
                rows(proj.shape[1]),
                rows(L + DR),
                whole((1, L)),
                whole(w_expand.shape),
                whole((SEQ_LEN, DR)),
                whole((SEQ_LEN, DR)),
            ],
            out_specs=[rows(heads * DV), by_head(1), by_head(DN + DR), by_head(DN + DR), by_head(DV), rows(L)],
        ),
        out_shape=[
            jax.ShapeDtypeStruct((band, heads * DV), BF16),
            head_shape(1, F32),
            head_shape(DN + DR),
            head_shape(DN + DR),
            head_shape(DV),
            jax.ShapeDtypeStruct((band, L), BF16),
        ],
        compiler_params=params(),
        name="attention",
    )(starts, proj, latent, gain[None], w_expand, cosine, sine)


def attention_back_kernel(heads, starts_ref, q_ref, k_ref, v_ref, logs, grad, w_expand, cos, sin, dq_out, de_out, dl_out):
    scale = (DN + DR) ** (-0.5)
    cosine, sine = cos[...], -sin[...]
    seen = visible(starts_ref, pl.program_id(0))
    rope = None
    latent = None
    for head in range(heads):
        query, key, value = q_ref[0, head], k_ref[0, head], v_ref[0, head]
        grad_here = grad[:, head * DV : (head + 1) * DV]
        scores = jnp.where(seen, dot_nt(query, key) * scale, -1e30)
        weights = jnp.exp(scores - logs[0, head])
        grad_weights = dot_nt(grad_here, value)
        centre = jnp.sum(weights * grad_weights, axis=1, keepdims=True)
        grad_scores = (weights * (grad_weights - centre)).astype(BF16)
        grad_query = dot(grad_scores, key) * scale
        grad_key = dot_tn(grad_scores, query) * scale
        grad_value = dot_tn(weights.astype(BF16), grad_here)
        dq_out[:, head * DN : (head + 1) * DN] = grad_query[:, :DN].astype(BF16)
        start = heads * DN + head * DR
        dq_out[:, start : start + DR] = turn(grad_query[:, DN:], cosine, sine).astype(BF16)
        part = turn(grad_key[:, DN:], cosine, sine)
        rope = part if rope is None else rope + part
        both = jnp.concatenate([grad_key[:, :DN].astype(BF16), grad_value.astype(BF16)], axis=1)
        start = head * (DN + DV)
        de_out[:, start : start + DN + DV] = both
        part = dot_nt(both, w_expand[:, start : start + DN + DV])
        latent = part if latent is None else latent + part
    dl_out[:, :L] = latent.astype(BF16)
    dl_out[:, L:] = rope.astype(BF16)


def attention_backward(starts, query, key, value, logs, grad, w_expand, cosine, sine):
    seqs, heads = query.shape[:2]
    band = seqs * SEQ_LEN

    def rows(width):
        return pl.BlockSpec((SEQ_LEN, width), lambda s, p: (s, 0))

    def whole(shape):
        return pl.BlockSpec(shape, lambda s, p: (0, 0))

    def by_head(width):
        return pl.BlockSpec((1, heads, SEQ_LEN, width), lambda s, p: (s, 0, 0, 0))

    widths = (heads * (DN + DR), heads * (DN + DV), L + DR)
    return pl.pallas_call(
        functools.partial(attention_back_kernel, heads),
        grid_spec=pltpu.PrefetchScalarGridSpec(
            num_scalar_prefetch=1,
            grid=(seqs,),
            in_specs=[
                by_head(DN + DR),
                by_head(DN + DR),
                by_head(DV),
                by_head(1),
                rows(heads * DV),
                whole(w_expand.shape),
                whole((SEQ_LEN, DR)),
                whole((SEQ_LEN, DR)),
            ],
            out_specs=[rows(width) for width in widths],
        ),
        out_shape=[jax.ShapeDtypeStruct((band, width), BF16) for width in widths],
        compiler_params=params(),
        name="attention_back",
    )(starts, query, key, value, logs, grad, w_expand, cosine, sine)


def norm_backward(value, scale, gain, grad_norm, row_total, width):
    return (
        scale[:, None] * gain * grad_norm - value * (scale**3 / width)[:, None] * row_total[:, None]
    )


def widen(value, width):
    return jnp.pad(value, ((0, 0), (0, width - value.shape[1])))


def up_to(width):
    return 128 * ((width + 127) // 128)


def per_device(
    hidden_in,
    expert_routes,
    piece_starts,
    query_weight,
    latent_weight,
    latent_gain,
    expand_weight,
    output_weight,
    attention_gain,
    ffn_gain,
    router_weight,
    gate_weight,
    up_weight,
    down_weight,
    shared_gate,
    shared_up,
    shared_down,
    grad_out,
):
    row_parts = lax.axis_size("gx")
    column_parts = lax.axis_size("gy")
    here_x = lax.axis_index("gx")
    here_y = lax.axis_index("gy")
    local_rows = hidden_in.shape[0]
    all_tokens = local_rows * column_parts
    band_rows = all_tokens // row_parts
    head_width = query_weight.shape[1]
    heads_here = head_width // (DN + DR)
    latent_width = latent_weight.shape[1]
    experts_here = gate_weight.shape[0]
    shared_width = shared_gate.shape[1]
    cap = 16 * ((local_rows * TOPK * 5 + 64 * EXPERTS - 1) // (64 * EXPERTS))
    blocks = column_parts
    quarter_blocks = blocks // row_parts
    quarter_slots = quarter_blocks * cap
    on_square = square()

    hidden_all = spread_rows(hidden_in)
    hidden = hidden_in.astype(F32)
    grad_top = grad_out.astype(F32)
    wide = up_to(shared_width)
    shared_weight = jnp.concatenate(
        [widen(shared_gate, wide), widen(shared_up, wide), widen(shared_down.T, wide)], axis=1
    )
    scale_one = lax.rsqrt(feature_total(jnp.sum(hidden * hidden, axis=1)) / D + EPS)
    grad_top_tokens = to_tokens(after(grad_out, scale_one))
    shared_weight = collect_rows(after(shared_weight, scale_one))
    sent = jnp.concatenate([expert_routes.T.astype(F32), scale_one[None]], axis=0)
    gathered = lax.all_gather(sent, "gy", axis=1, tiled=True)
    routes_all = gathered[:TOPK].astype(jnp.int32)
    scale_one_all = gathered[TOPK]
    mine = here_y * experts_here + jnp.arange(experts_here, dtype=jnp.int32)
    named = jnp.any(routes_all[:, :, None] == mine[None, None, :], axis=0)
    named_blocks = named.astype(BF16).reshape(blocks, local_rows, experts_here)
    order = jnp.arange(local_rows, dtype=jnp.int32)
    earlier = (order[None, :] < order[:, None]).astype(BF16)
    slot = jnp.einsum("ts,bse->bte", earlier, named_blocks, preferred_element_type=F32)
    code = jnp.where(named, slot.reshape(all_tokens, experts_here), -1.0)
    chosen = one_hot(code, cap, blocks)
    code_here = pick(code.reshape(row_parts, quarter_blocks, local_rows, experts_here), here_x, 0)
    spots = jnp.arange(cap, dtype=jnp.int32).astype(F32)
    at_slot = code_here[:, :, :, None] == spots
    hidden_all = after(hidden_all, chosen, grad_top_tokens)

    norm_one_all = (hidden_all.astype(F32) * scale_one_all[:, None] * attention_gain).astype(BF16)
    by_head = query_weight.reshape(-1, heads_here, DN + DR)
    used = head_width + latent_width
    in_weight = jnp.concatenate(
        [
            by_head[:, :, :DN].reshape(-1, heads_here * DN),
            by_head[:, :, DN:].reshape(-1, heads_here * DR),
            widen(latent_weight, up_to(used) - head_width),
        ],
        axis=1,
    )
    projected = band_total(norm_one_all, in_weight, 1)
    latent_part = projected[:, head_width:used].astype(BF16)
    latent_all = lax.all_gather(latent_part, "gy", axis=1, tiled=True)

    grad_top_all = spread_rows(after(grad_out, hidden_all))
    grad_rows = dispatch(after(chosen, latent_part), grad_top_all, cap, blocks)
    grad_rows = grad_rows.reshape(experts_here, row_parts, quarter_slots, -1)

    if on_square:
        late = experts_here - 2
        grad_hidden_pre = [square_sum(grad_rows, down_weight, 0, 2, 2, True, False, BF16)]
        latent_all = after(latent_all, grad_hidden_pre[0])
    grad_top_band = spread_rows(after(grad_top_tokens, latent_all))

    cosine, sine = rope_tables(SEQ_LEN)
    attended, logs, query_seq, key_seq, value_seq, latent_norm = attention_forward(
        piece_starts, projected, latent_all, latent_gain, expand_weight, cosine, sine, heads_here
    )
    attended_all = collect_rows(attended)
    attended_all = after(attended_all, shared_weight)
    attention_part = dot(attended_all, output_weight).astype(BF16)
    after_attention = hidden + outer_total(attention_part)

    if on_square:
        rows = after(grad_rows, attention_part)
        grad_hidden_pre.append(square_sum(rows, down_weight, 2, late - 2, 3, True, False, BF16))
        after_attention, rows = lax.optimization_barrier((after_attention, rows, grad_hidden_pre[1]))[:2]
        last_steps = halves(late, 2)
        last_sent = [
            group(rows, away, 2, (down_weight,), start, half, True)
            for start, half, bit, away, _, _ in last_steps
        ]
        last_ones = [swap(value, step[2]) for value, step in zip(last_sent, last_steps)]

    gained = (after_attention * ffn_gain).astype(BF16)
    gained_all = spread_rows(gained)
    squares = jnp.sum(after_attention * after_attention, axis=1, keepdims=True)
    logits = dot(after(gained, squares), router_weight)
    totals = square_total(widen(jnp.concatenate([logits, squares], axis=1), 128))
    scale_two = lax.rsqrt(totals[:, EXPERTS] / D + EPS)
    probs = jax.nn.softmax(totals[:, :EXPERTS] * scale_two[:, None], axis=-1)
    norm_two = (after_attention * scale_two[:, None] * ffn_gain).astype(BF16)
    sent = jnp.concatenate(
        [
            probs.reshape(local_rows, column_parts, experts_here),
            jnp.broadcast_to(scale_two[:, None, None], (local_rows, column_parts, 1)),
        ],
        axis=2,
    ).transpose(1, 0, 2)
    received = lax.all_to_all(sent, "gy", split_axis=0, concat_axis=0, tiled=True)
    scale_two_all = received[:, :, experts_here].reshape(all_tokens)
    received = pick(received.reshape(row_parts, quarter_blocks, local_rows, experts_here + 1), here_x, 0)
    factors = jnp.stack(
        [
            jnp.sum(jnp.where(at_slot, value[:, :, :, None], 0.0), axis=1)
            .transpose(1, 0, 2)
            .reshape(experts_here, quarter_slots)
            for value in (received[:, :, :experts_here], received[:, :, experts_here:])
        ],
        axis=2,
    )
    norm_two_tokens = to_tokens(norm_two)
    if on_square:
        rows = after(grad_rows, factors)
        last_twos = [
            swap(group(rows, second, 1, (down_weight,), start, half, True, (one,)), 3 - bit)
            for (start, half, bit, _, second, _), one in zip(last_steps, last_ones)
        ]
        gained_all = after(gained_all, norm_two_tokens)
    rows_two = dispatch(chosen, gained_all, cap, blocks)
    rows_two = rows_two.reshape(experts_here, row_parts, quarter_slots, -1)
    norm_two_band = spread_rows(after(norm_two_tokens, gained_all))

    both_weights = (gate_weight, up_weight)
    if on_square:
        rows = after(grad_rows, rows_two)
        grad_hidden_pre += [
            group(rows, third, 1, (down_weight,), start, half, True, (one, two)).reshape(1, quarter_slots, -1)
            for (start, half, _, _, _, third), one, two in zip(last_steps, last_ones, last_twos)
        ]
        grad_hidden_pre = jnp.concatenate(grad_hidden_pre, axis=0)
        order_of = numbers(here_x, here_x ^ 1, here_x ^ 2, here_x ^ 3)
        own, from_x, from_y, across, scaled, back_rows, slot_grad = routed_experts(
            rows_two, gate_weight, up_weight, grad_hidden_pre, factors
        )
        whole = [(own, 0), (from_x, 0), (from_y, 0), (across, 0)]
        grad_groups = [(0, experts_here, whole)]
    else:
        everything = jnp.arange(row_parts, dtype=jnp.int32)
        order_of = everything

        def whole_total(rows, weight, transposed):
            out = group(rows, everything, row_parts, (weight,), 0, experts_here, transposed)
            out = out.reshape((experts_here,) + out.shape[2:])
            return lax.psum_scatter(out, "gx", scatter_dimension=1, tiled=True)[:, 0].astype(F32)

        scale = factors[:, :, 1:2]
        scaled, grad_gate_pre, grad_up_pre, slot_grad = expert_body(
            whole_total(rows_two, gate_weight, False) * scale,
            whole_total(rows_two, up_weight, False) * scale,
            whole_total(grad_rows, down_weight, True),
            factors[:, :, 0:1],
        )
        grads = jnp.stack([grad_gate_pre, grad_up_pre], axis=1)
        whole = lax.all_gather(grads, "gx", axis=0, tiled=False)
        grad_groups = [(0, experts_here, [(whole[q], 0) for q in range(row_parts)])]
        whole = lax.all_gather(scaled[:, None], "gx", axis=0, tiled=False)
        hidden_groups = [(0, experts_here, [(whole[q], 0) for q in range(row_parts)])]

        back_rows = back(grad_groups, order_of, both_weights, True)

    back_rows = back_rows.reshape(experts_here, blocks * cap, -1)
    grad_norm_part = combine(chosen, [back_rows], cap, blocks)
    grad_norm_routed = outer_total(grad_norm_part)

    shared_gate_all = shared_weight[:, :wide]
    shared_up_all = shared_weight[:, wide : 2 * wide]
    shared_down_all = shared_weight[:, 2 * wide :]
    norm_two_band = after(norm_two_band, grad_norm_part)
    shared_gate_pre = dot(norm_two_band, shared_gate_all)
    shared_up_pre = dot(norm_two_band, shared_up_all)
    shared_hidden = (silu(shared_gate_pre) * shared_up_pre).astype(BF16)
    grad_shared_hidden = dot(grad_top_band, shared_down_all)
    grad_shared_gate_pre = (
        grad_shared_hidden * shared_up_pre * silu_grad(shared_gate_pre)
    ).astype(BF16)
    grad_shared_up_pre = (grad_shared_hidden * silu(shared_gate_pre)).astype(BF16)
    grad_shared_both = jnp.concatenate([grad_shared_gate_pre, grad_shared_up_pre], axis=1)
    grad_shared_part = dot_nt(grad_shared_both, shared_weight[:, : 2 * wide]).astype(BF16)
    grad_norm_shared = outer_total(grad_shared_part)
    grad_shared = dot_tn(after(norm_two_band, grad_shared_part), grad_shared_both).astype(BF16)
    grad_shared = lax.psum_scatter(
        after(grad_shared, grad_norm_shared), "gx", scatter_dimension=0, tiled=True
    ).astype(F32)

    slot_grad = after(slot_grad, grad_norm_part)
    slot_grad = slot_grad.reshape(experts_here, quarter_blocks, cap).transpose(1, 0, 2)
    grad_probs = jnp.sum(jnp.where(at_slot, slot_grad[:, None], 0.0), axis=3)
    grad_probs = grad_probs.reshape(band_rows, experts_here)
    grad_probs = collect(grad_probs.T).transpose(0, 2, 1).reshape(blocks, local_rows, experts_here)
    grad_probs = lax.all_to_all(grad_probs, "gy", split_axis=0, concat_axis=2, tiled=True)
    grad_probs = grad_probs.reshape(local_rows, EXPERTS)
    centre = jnp.sum(probs * grad_probs, axis=1, keepdims=True)
    grad_logits = (probs * (grad_probs - centre)).astype(BF16)
    grad_norm_router = dot_nt(grad_logits, router_weight)
    grad_router_part = dot_tn(norm_two, grad_logits)
    waits = [grad_norm_router]
    if on_square:
        half = experts_here // 2
        hidden_x, hidden_y, hidden_d, out_low = hidden_products(
            after(scaled, grad_shared_part), down_weight, 0, half, 4
        )
        hidden_groups = [(0, half, [(scaled, 0), (hidden_x, 0), (hidden_y, 0), (hidden_d, 0)])]
        waits.append(out_low)
    grad_norm_shared = to_features(grad_norm_shared.astype(BF16)).astype(F32)
    grad_norm_routed = after(grad_norm_routed, *waits)
    grad_norm_two = grad_norm_routed + grad_norm_shared + grad_norm_router

    scaled_after = after_attention * ffn_gain
    row_two = feature_total(jnp.sum(scaled_after * grad_norm_two, axis=1))
    grad_after = grad_top + norm_backward(
        after_attention, scale_two, ffn_gain, grad_norm_two, row_two, D
    )
    grad_ffn_part = jnp.sum(grad_norm_two * after_attention * scale_two[:, None], axis=0)
    grad_after_sent = grad_after.astype(BF16)
    grad_after_all = spread_rows(grad_after_sent)

    if on_square:
        hidden_x, hidden_y, hidden_d, out_high = hidden_products(
            after(scaled, grad_after_sent), down_weight, half, half, 5
        )
        hidden_groups.append((half, half, [(scaled, half), (hidden_x, 0), (hidden_y, 0), (hidden_d, 0)]))
        out = [out_low, out_high]
        grad_after_all = after(grad_after_all, out_high)
    else:
        out = [back(hidden_groups, order_of, (down_weight,), False)]
    out = [value.reshape(value.shape[0], blocks * cap, -1) for value in out]

    grad_attended = band_total(grad_after_all, output_weight, 6, True).astype(BF16)
    shared_hidden_all = collect(after(shared_hidden, grad_attended)).reshape(row_parts, blocks, -1, wide)
    shared_hidden_all = shared_hidden_all.transpose(1, 0, 2, 3).reshape(all_tokens, wide)
    shared_down_wide = jnp.pad(shared_down, ((0, wide - shared_width), (0, 0)))
    shared_out = dot(shared_hidden_all, shared_down_wide).astype(BF16)
    routed_part = combine(chosen, out, cap, blocks, (shared_out,))
    routed = outer_total(routed_part)
    mixed = (after_attention + routed).astype(BF16)
    grad_query_pre, grad_expanded, latent_grads = attention_backward(
        piece_starts, query_seq, key_seq, value_seq, logs, grad_attended, expand_weight, cosine, sine
    )
    latent_sums = lax.psum(latent_grads, "gy").astype(F32)
    norm_two_all = (gained_all.astype(F32) * scale_two_all[:, None]).astype(BF16)
    rows_norm = dispatch(after(chosen, latent_grads), norm_two_all, cap, blocks)
    rows_norm = rows_norm.reshape(experts_here, row_parts, quarter_slots, -1)
    grad_gate, grad_up = weight_grad(rows_norm, grad_groups, order_of, False)
    latent_grads = after(latent_sums, grad_gate, grad_up)
    grad_query_all = collect_rows(grad_query_pre)
    latent_f32 = latent_all.astype(F32)
    compressed = latent_f32[:, :L]
    latent_scale = lax.rsqrt(jnp.mean(compressed * compressed, axis=1) + EPS)
    grad_latent_norm, grad_rope_key = latent_grads[:, :L], latent_grads[:, L:]
    latent_row = jnp.sum(compressed * latent_gain * grad_latent_norm, axis=1)
    grad_compressed = norm_backward(
        compressed, latent_scale, latent_gain, grad_latent_norm, latent_row, L
    )
    grad_gain_part = jnp.sum(grad_latent_norm * compressed * latent_scale[:, None], axis=0)
    grad_latent_pre = jnp.concatenate([grad_compressed, grad_rope_key], axis=1)
    grad_latent_own = lax.dynamic_slice_in_dim(
        grad_latent_pre, here_y * latent_width, latent_width, 1
    ).astype(BF16)
    grad_latent_own = widen(grad_latent_own, up_to(used) - head_width)
    grad_latent_all = collect_rows(grad_latent_own)
    grad_norm_part = (
        dot_nt(grad_query_all, in_weight[:, :head_width])
        + dot_nt(grad_latent_all, in_weight[:, head_width:])
    ).astype(BF16)
    grad_norm_one = outer_total(grad_norm_part)

    norm_one_all = after(norm_one_all, grad_norm_part)
    grad_query = dot_tn(norm_one_all, grad_query_all)
    grad_query = jnp.concatenate(
        [
            grad_query[:, : heads_here * DN].reshape(-1, heads_here, DN),
            grad_query[:, heads_here * DN :].reshape(-1, heads_here, DR),
        ],
        axis=2,
    ).reshape(-1, head_width)
    grad_latent = dot_tn(norm_one_all, grad_latent_all)[:, :latent_width]
    grad_output = dot_tn(attended_all, after(grad_after_all, grad_norm_part))
    (grad_down,) = weight_grad(after(grad_rows, grad_norm_part), hidden_groups, order_of, True)
    grad_expand = square_total(dot_tn(latent_norm, grad_expanded).astype(BF16)).astype(F32)
    grad_shared_down = dot_tn(shared_hidden_all, grad_top_all)[:shared_width]
    pieces = grad_router_part.reshape(column_parts, -1, EXPERTS)
    pieces = lax.all_to_all(pieces, "gy", split_axis=0, concat_axis=0, tiled=True)
    grad_router = lax.all_gather(jnp.sum(pieces, axis=0), "gy", axis=0, tiled=True)
    (
        grad_norm_one,
        grad_query,
        grad_latent,
        grad_output,
        grad_down,
        grad_expand,
        grad_router,
        grad_shared_down,
    ) = lax.optimization_barrier(
        (
            grad_norm_one,
            grad_query,
            grad_latent,
            grad_output,
            grad_down,
            grad_expand,
            grad_router,
            grad_shared_down,
        )
    )
    row_one, grad_latent_gain = feature_total(
        (jnp.sum(hidden * attention_gain * grad_norm_one, axis=1), grad_gain_part)
    )
    grad_hidden = grad_after + norm_backward(
        hidden, scale_one, attention_gain, grad_norm_one, row_one, D
    )
    grad_attention_part = jnp.sum(grad_norm_one * hidden * scale_one[:, None], axis=0)
    grad_attention_gain, grad_ffn_gain = lax.psum((grad_attention_part, grad_ffn_part), "gy")
    grad_shared_gate = grad_shared[:, :shared_width]
    grad_shared_up = grad_shared[:, wide : wide + shared_width]
    return (
        mixed,
        grad_hidden,
        grad_query,
        grad_latent,
        grad_latent_gain,
        grad_expand,
        grad_output,
        grad_attention_gain,
        grad_ffn_gain,
        grad_router,
        grad_gate,
        grad_up,
        grad_down,
        grad_shared_gate,
        grad_shared_up,
        grad_shared_down,
    )


def solution(mesh):
    return jax.shard_map(
        per_device,
        mesh=mesh,
        in_specs=(
            P("gy", "gx"),
            P("gy", None),
            P("gx", None),
            P("gx", "gy"),
            P("gx", "gy"),
            P(),
            P(None, "gy"),
            P("gy", "gx"),
            P("gx"),
            P("gx"),
            P("gx", None),
            P("gy", "gx", None),
            P("gy", "gx", None),
            P("gy", None, "gx"),
            P("gx", "gy"),
            P("gx", "gy"),
            P("gy", "gx"),
            P("gy", "gx"),
        ),
        out_specs=(
            P("gy", "gx"),
            P("gy", "gx"),
            P("gx", "gy"),
            P("gx", "gy"),
            P(),
            P(None, "gy"),
            P("gy", "gx"),
            P("gx"),
            P("gx"),
            P("gx", None),
            P("gy", "gx", None),
            P("gy", "gx", None),
            P("gy", None, "gx"),
            P("gx", "gy"),
            P("gx", "gy"),
            P("gy", "gx"),
        ),
        check_vma=False,
    )
```

time: 2250 us -> 1340 us (0.60)
  waiting for transfers between devices: 1410 us -> 161 us
  Pallas kernels: 0 us -> 799 us
  local copies, waits for them, and re-layouts: 343 us -> 74.3 us
  matrix products: 226 us -> 62.3 us
  other arithmetic: 118 us -> 60.8 us
  starting transfers between devices: 21.2 us -> 52.2 us
    pallas_call x0 -> x23, Pallas kernels: none -> 799 us  [the longest x1 390 us: routed_experts(): pl.pallas_call(experts_kernel, in_specs=[vmem, anywhere, anywhere, vmem,...]
    all_gather x7 -> x1, waiting for transfers between devices: 494 us -> 0.02 us  [per_device(): latent_all = lax.all_gather(latent_part, 'gy', axis=1, tiled=True)]
    reduce_scatter x8 -> x6, waiting for transfers between devices: 336 us -> 28.5 us  [the longest x5 28.5 us: outer_total(): lax.psum_scatter(partial.astype(BF16), 'gy', scatter_dimension=0, tiled=T...]
    all_to_all x4, waiting for transfers between devices: 239 us -> 7.98 us  [the longest x1 6.59 us: per_device(): lax.all_to_all(sent, 'gy', split_axis=0, concat_axis=0, tiled=True)]
    unnamed x26 -> x14, waiting for transfers between devices: 181 us -> 2.06 us
    dot_general x38 -> x18, matrix products: 226 us -> 62.3 us  [the longest x6 23.9 us: dot(): return jnp.dot(a, b, preferred_element_type=F32)]
    ppermute x0 -> x32, waiting for transfers between devices: none -> 80 us  [swap(): return lax.ppermute(value, 'gx', [(i, i ^ bit) for i in range(4)])]
    unnamed x181 -> x117, local copies, waits for them, and re-layouts: 94.8 us -> 19.5 us
  transfers between devices with their start and end apart: 28 -> 50, of which waited for: 20 -> 24; matrix products, arithmetic and copies ran while one was open for 24% -> 12% of each run, Pallas kernels for 0% -> 58%
where the time goes in v1:
time: 1340 us; the launch traced here: 1320 us
  Pallas kernels  799 us (60%)
  waiting for transfers between devices  161 us (12%)
  blocking collectives  98.4 us (7%)
  local copies, waits for them, and re-layouts  74.3 us (6%)
  matrix products  62.3 us (5%)
  other arithmetic  60.8 us (5%)
  starting transfers between devices  52.2 us (4%)
  between operations  15.5 us (1%)
    pallas_call x1, Pallas kernels, routed_experts(): pl.pallas_call(experts_kernel, in_specs=[vmem, anywhere, anywhere, vmem,...  390 us
    pallas_call x4, Pallas kernels, square_sum(): pl.pallas_call(functools.partial(sum_kernel, base, by_quarter, own_weight...  155 us
    pallas_call x2, Pallas kernels, hidden_products(): pl.pallas_call(functools.partial(hidden_kernel, base), in_specs=[anywhere...  107 us
    ppermute x32, waiting for transfers between devices, swap(): return lax.ppermute(value, 'gx', [(i, i ^ bit) for i in range(4)])  80 us
    pallas_call x2, Pallas kernels, weight_grad(): pl.pallas_call(functools.partial(weight_grad_kernel, shapes_of(groups), f...  46.9 us
    all_gather x6, waiting for transfers between devices, spread_rows(): return lax.all_gather(value, 'gy', axis=0, tiled=True)  37.7 us
    ppermute x32, starting transfers between devices, swap(): return lax.ppermute(value, 'gx', [(i, i ^ bit) for i in range(4)])  34.8 us
    psum x3, blocking collectives, feature_total(): return lax.psum(value, 'gx')  29.8 us
  transfers between devices with their start and end apart: 50, of which 24 were waited for; matrix products, arithmetic and copies ran while one was open for 12% of the time, Pallas kernels for 58%

profile of v1, /device:TPU:0, one launch (start us, length us, event | category | flops | bytes accessed | tf_op | source)
XLA Modules:
  0.0 1323.3 jit_solution(13998628889222467706)
XLA Ops:
  9.1 11.4 psum.49
  25.4 14.7 %all_gather.28 = f32[7,4096]{1,0:T(8,128)S(1)} all-gather(f32[7,512]{1,0:T(8,128)S(1)} %pad_maximum_fusion.8), channel_id=1, replica_groups=mesh['gx'=4,'gy'=8] {'gy'}, dimensions={1}, use_global_device_ids=true | all-gather | bytes 129024 | tf_op jit(solution)/shard_map/all_gather | solution.py:1169
  52.2 8.3 all-gather.8.cloned.1.call-done
  75.7 50.3 %square_sum.4 = f32[4,256,512]{2,1,0:T(8,128)} custom-call(bf16[4,4,256,512]{3,2,1,0:T(8,128)(2,1)} %bitcast.223, bf16[512,512]{1,0:T(8,128)(2,1)} %pad_maximum_fusion.5.weight), custom_call_target="tpu_custom_call" | custom-call | flops 2147483648 | bytes 2097152 | tf_op jit(solution)/shard_map/square_sum/pallas_call | solution.py:665
  142.5 8.9 dispatch.3
  151.4 31.1 %square_sum.5 = bf16[2,128,1408]{2,1,0:T(8,128)(2,1)} custom-call(bf16[8,4,128,512]{3,2,1,0:T(8,128)(2,1)} %bitcast.197, bf16[8,1408,512]{2,1,0:T(8,128)(2,1)} %weight.8), custom_call_target="tpu_custom_call" | custom-call | flops 1476395008 | bytes 2883584 | tf_op jit(solution)/shard_map/square_sum/pallas_call | solution.py:665
  185.3 12.1 attention.1
  223.5 51.0 %square_sum.6 = bf16[4,128,1408]{2,1,0:T(8,128)(2,1)} custom-call(bf16[8,4,128,512]{3,2,1,0:T(8,128)(2,1)} %bitcast.198, bf16[8,1408,512]{2,1,0:T(8,128)(2,1)} %weight.8), custom_call_target="tpu_custom_call" | custom-call | flops 2952790016 | bytes 5767168 | tf_op jit(solution)/shard_map/square_sum/pallas_call | solution.py:665
  285.5 8.8 collective-permute-done.9
  294.7 10.2 all_to_all.76
  305.0 17.0 %all-gather.14.cloned.1.call-done.rows_ref = bf16[4096,512]{1,0:T(8,128)(2,1)} async-done(((bf16[512,512]{1,0:T(8,128)(2,1)}), bf16[4096,512]{1,0:T(8,128)(2,1)}) %all-gather.14.cloned.1.call-update) | async-done | bytes 4194320 | tf_op jit(solution)/shard_map/all_gather | solution.py:89
  365.3 12.4 all-gather.16.cloned.1.call-done
  384.4 9.2 dispatch.4
  405.1 389.6 %routed_experts.1 = (bf16[8,2,128,1408]{3,2,1,0:T(8,128)(2,1)}, bf16[8,2,128,1408]{3,2,1,0:T(8,128)(2,1)}, bf16[8,2,128,1408]{3,2,1,0:T(8,128)(2,1)}, bf16[8,2,1...) custom-call(bf16[8,4,128,512]{3,2,1,0:T(8,128)(2,1)} %bitcast.217, ...), custom_call_target="tpu_custom_call" | custom-call | flops 35433480192 | bytes 69206016 | tf_op jit(solution)/shard_map/routed_experts/pallas_call | solution.py:539
  794.7 9.0 combine.2
  831.1 13.0 all_to_all.77
  844.2 28.4 %reduce-scatter.11.cloned.1.call-done = bf16[128,2048]{1,0:T(8,128)(2,1)} async-done(((bf16[1024,2048]{1,0:T(8,128)(2,1)}), bf16[128,2048]{1,0:T(8,128)(2,1)}) %reduce-scatter.11.cloned.1.call-update) | async-done | bytes 524304 | tf_op jit(solution)/shard_map/reduce_scatter | solution.py:93
  878.5 57.2 %hidden_products.2 = (bf16[4,1,128,1408]{3,2,1,0:T(8,128)(2,1)}, bf16[4,1,128,1408]{3,2,1,0:T(8,128)(2,1)}, bf16[4,1,128,1408]{3,2,1,0:T(8,128)(2,1)}, bf16[4,4,128,512]{3,2,1,0:T(8,128)(2,1)}) custom-call(bf16[8,1,128,1408]{3,2,1,0:T(8,128)(2,1)} %get-tuple-element.104.hidden.refs_4_.refs_8_, bf16[8,1408,512]{2,1,0:T(8,128)(2,1)} %weight.8), custom_call_target="tpu_custom_call" | custom-call | flops 2952790016 | bytes 5767168 | tf_op jit(solution)/shard_map/hidden_products/pallas_call | solution.py:783
  940.4 8.9 psum.50
  952.7 49.6 %hidden_products.3 = (bf16[4,1,128,1408]{3,2,1,0:T(8,128)(2,1)}, bf16[4,1,128,1408]{3,2,1,0:T(8,128)(2,1)}, bf16[4,1,128,1408]{3,2,1,0:T(8,128)(2,1)}, bf16[4,4,128,512]{3,2,1,0:T(8,128)(2,1)}) custom-call(bf16[8,1,128,1408]{3,2,1,0:T(8,128)(2,1)} %get-tuple-element.104.hidden.refs_4_.refs_8_, bf16[8,1408,512]{2,1,0:T(8,128)(2,1)} %weight.8), custom_call_target="tpu_custom_call" | custom-call | flops 2952790016 | bytes 5767168 | tf_op jit(solution)/shard_map/hidden_products/pallas_call | solution.py:783
  1002.3 22.1 %square_sum.7 = f32[4,256,256]{2,1,0:T(8,128)} custom-call(bf16[4,4,256,512]{3,2,1,0:T(8,128)(2,1)} %bitcast.224, bf16[256,512]{1,0:T(8,128)(2,1)} %weight.9), custom_call_target="tpu_custom_call" | custom-call | flops 1073741824 | bytes 1048576 | tf_op jit(solution)/shard_map/square_sum/pallas_call | solution.py:665
  1026.5 14.2 %attention_back.1 = (bf16[1024,384]{1,0:T(8,128)(2,1)}, bf16[1024,512]{1,0:T(8,128)(2,1)}, bf16[1024,576]{1,0:T(8,128)(2,1)}) custom-call(s32[1,2]{1,0:T(1,128)} %starts_ref.3, bf16[1,2,1024,192]{3,2,1,0:T(8,128)(2,1)} %get-tuple-element.108.q_ref, bf16[1,2,1024,192]{3,2,1,0:T(8,128)(2,1)} %get-tuple-element.109.k_ref, ...), custom_call_target="tpu_custom_call" | custom-call | tf_op jit(solution)/shard_map/attention_back/pallas_call | solution.py:1083
  1040.9 7.3 convolution_convert_fusion.3
  1056.9 8.9 dispatch.5
  1069.9 27.3 %weight_grad.2 = (f32[8,512,1408]{2,1,0:T(8,128)}, f32[8,512,1408]{2,1,0:T(8,128)}) custom-call(s32[4]{0:T(128)} %pad_add_fusion.6.picks_ref, bf16[8,4,128,512]{3,2,1,0:T(8,128)(2,1)} %bitcast.218, bf16[8,4,128,512]{3,2,1,0:T(8,128)(2,1)} %bitcast.219, bf16[8,4,128,512]{3,2,1,0:T(8,128)(2,1)} %bitcast.220, bf16[8,4,128,512]{3,2,1,0:T(8,128)(2,1)} %bitcast.221, ...), custom_call_target="tpu_custom_call" | custom-call | flops 11811160064 | bytes 73400320 | tf_op jit(solution)/shard_map/weight_grad/pallas_call | solution.py:910
  1121.6 18.5 %collective-permute-done.29 = bf16[512,128]{1,0:T(8,128)(2,1)S(1)} collective-permute-done((bf16[512,128]{1,0:T(8,128)(2,1)S(1)}, bf16[512,128]{1,0:T(8,128)(2,1)S(1)}, u32[]{:S(2)}, u32[]{:S(2)}) %collective-permute-start.29) | collective-permute-done | bytes 131104 | tf_op jit(solution)/shard_map/ppermute | solution.py:42
  1153.3 15.8 %collective-permute-done.19 = bf16[1024,384]{0,1:T(8,128)(2,1)} collective-permute-done((bf16[1024,384]{0,1:T(8,128)(2,1)}, bf16[1024,384]{0,1:T(8,128)(2,1)}, u32[]{:S(2)}, u32[]{:S(2)}) %collective-permute-start.19) | collective-permute-done | bytes 786464 | tf_op jit(solution)/shard_map/ppermute | solution.py:42
  1196.7 9.9 combine.3
  1224.9 16.7 %all_gather.35 = f32[512,64]{1,0:T(8,128)} all-gather(f32[64,64]{1,0:T(8,128)S(1)} %copy.224), channel_id=1, replica_groups=mesh['gx'=4,'gy'=8] {'gy'}, dimensions={0}, use_global_device_ids=true | all-gather | bytes 147456 | tf_op jit(solution)/shard_map/all_gather | solution.py:1429
  1259.5 19.6 %weight_grad.3 = f32[8,1408,512]{2,1,0:T(8,128)} custom-call(s32[4]{0:T(128)} %pad_add_fusion.6.picks_ref, bf16[8,4,128,512]{3,2,1,0:T(8,128)(2,1)} %bitcast.207, bf16[8,4,128,512]{3,2,1,0:T(8,128)(2,1)} %bitcast.208, bf16[8,4,128,512]{3,2,1,0:T(8,128)(2,1)} %bitcast.209, bf16[8,4,128,512]{3,2,1,0:T(8,128)(2,1)} %bitcast.210, ...), custom_call_target="tpu_custom_call" | custom-call | flops 5905580032 | bytes 38797312 | tf_op jit(solution)/shard_map/weight_grad/pallas_call | solution.py:910
  1288.1 9.5 all-reduce.8
  1297.6 14.1 %all-reduce.7 = (f32[512]{0:T(512)}, f32[512]{0:T(512)}) all-reduce(f32[512]{0:T(512)S(1)} %get-tuple-element.258, f32[512]{0:T(512)S(1)} %get-tuple-element.256), channel_id=1, replica_groups=mesh['gx'=4,'gy'=8] {'gy'}, use_global_device_ids=true, to_apply=%region_26.27 | all-reduce | flops 1024 | bytes 8192 | tf_op jit(solution)/shard_map/psum | solution.py:1458
  (398 shorter events, 322.9 us)
Async XLA Ops:
  7.2 53.3 %all-gather.8.cloned.1.call-start = ((), (), s32[]{:S(2)}) async-start(), calls=%async_computation.12 | async-start | bytes 4718592 | tf_op jit(solution)/shard_map/all_gather | solution.py:89
  21.1 30.1 %all-to-all-start = ((bf16[4,128,512]{2,1,0:T(8,128)(2,1)}), bf16[4,128,512]{2,1,0:T(8,128)(2,1)S(1)}, u32[]{:S(2)}, u32[]{:S(2)}) async-start(bf16[4,128,512]{2,1,0:T(8,128)(2,1)} %bitcast.216), calls=%async_computation | async-start | bytes 1048576 | tf_op jit(solution)/shard_map/all_to_all | solution.py:98
  24.6 118.0 %all-gather.12.cloned.1.call-start = ((), (), s32[]{:S(2)}) async-start(), calls=%async_computation.14 | async-start | bytes 4718592 | tf_op jit(solution)/shard_map/all_gather | solution.py:89
  60.5 122.1 %all-gather.10.cloned.1.call-start = ((), (), s32[]{:S(2)}) async-start(), calls=%async_computation.13 | async-start | bytes 1327104 | tf_op jit(solution)/shard_map/all_gather | solution.py:1198
  61.4 73.5 %collective-permute-start.5 = (bf16[512,1152]{1,0:T(8,128)(2,1)S(1)}, bf16[512,1152]{1,0:T(8,128)(2,1)S(1)}, u32[]{:S(2)}, u32[]{:S(2)}) collective-permute-start(bf16[512,1152]{1,0:T(8,128)(2,1)S(1)} %fusion.25), channel_id=1, source_target_pairs={{0,16},{8,24},{16,0},{24,8},{1,17},{9,25},{17,1},{25,9},{2,18},{10... | collective-permute-start | bytes 3538952 | tf_op jit(solution)/shard_map/ppermute | solution.py:42
  62.9 74.3 %collective-permute-start.4 = (bf16[512,1152]{1,0:T(8,128)(2,1)S(1)}, bf16[512,1152]{1,0:T(8,128)(2,1)}, u32[]{:S(2)}, u32[]{:S(2)}) collective-permute-start(bf16[512,1152]{1,0:T(8,128)(2,1)S(1)} %fusion.25), channel_id=1, source_target_pairs={{0,8},{8,0},{16,24},{24,16},{1,9},{9,1},{17,25},{25,17},{2,10},{10... | collective-permute-start | bytes 3538952 | tf_op jit(solution)/shard_map/ppermute | solution.py:42
  128.0 146.5 %reduce-scatter.7.cloned.1.call-start = ((), (), s32[]{:S(2)}) async-start(), calls=%async_computation.15 | async-start | bytes 4718592 | tf_op jit(solution)/shard_map/reduce_scatter | solution.py:93
  135.8 63.7 %collective-permute-start.6 = (bf16[256,1152]{1,0:T(8,128)(2,1)}, bf16[256,1152]{1,0:T(8,128)(2,1)}, u32[]{:S(2)}, u32[]{:S(2)}) collective-permute-start(bf16[256,1152]{1,0:T(8,128)(2,1)} %slice.156), channel_id=1, source_target_pairs={{0,8},{8,0},{16,24},{24,16},{1,9},{9,1},{17,25},{25,17},{2,10},{10... | collective-permute-start | bytes 1769480 | tf_op jit(solution)/shard_map/ppermute | solution.py:42
  138.4 61.1 %collective-permute-start.7 = (bf16[256,1152]{1,0:T(8,128)(2,1)S(1)}, bf16[256,1152]{1,0:T(8,128)(2,1)S(1)}, u32[]{:S(2)}, u32[]{:S(2)}) collective-permute-start(bf16[256,1152]{1,0:T(8,128)(2,1)S(1)} %slice.157), channel_id=1, source_target_pairs={{0,16},{8,24},{16,0},{24,8},{1,17},{9,25},{17,1},{25,9},{2,18},{10... | collective-permute-start | bytes 1769480 | tf_op jit(solution)/shard_map/ppermute | solution.py:42
  222.8 99.1 %all-gather.14.cloned.1.call-start = ((), (), s32[]{:S(2)}) async-start(), calls=%async_computation.16 | async-start | bytes 4718592 | tf_op jit(solution)/shard_map/all_gather | solution.py:89
  276.7 101.0 %all-gather.16.cloned.1.call-start = ((), (), s32[]{:S(2)}) async-start(), calls=%async_computation.17 | async-start | bytes 4718592 | tf_op jit(solution)/shard_map/all_gather | solution.py:89
  277.2 526.5 %all-gather.18.cloned.1.call-start = ((), (), s32[]{:S(2)}) async-start(), calls=%async_computation.18 | async-start | bytes 4718592 | tf_op jit(solution)/shard_map/all_gather | solution.py:89
  325.9 22.3 %all-to-all-start.2 = ((f32[8,512,9]{1,2,0:T(8,128)}), f32[8,512,9]{1,2,0:T(8,128)}, u32[]{:S(2)}, u32[]{:S(2)}) async-start(f32[8,512,9]{1,2,0:T(8,128)} %maximum_bitcast_fusion.4), calls=%async_computation.3 | async-start | bytes 524288 | tf_op jit(solution)/shard_map/all_to_all | solution.py:1245
  330.0 542.6 %reduce-scatter.11.cloned.1.call-start = ((), (), s32[]{:S(2)}) async-start(), calls=%async_computation.20 | async-start | bytes 4718592 | tf_op jit(solution)/shard_map/reduce_scatter | solution.py:93
  358.0 39.9 %collective-permute-start.11 = (bf16[1,1,1,128,1408]{4,3,2,1,0:T(8,128)(2,1)}, bf16[1,1,1,128,1408]{4,3,2,1,0:T(8,128)(2,1)S(1)}, u32[]{:S(2)}, u32[]{:S(2)}) collective-permute-start(bf16[1,1,1,128,1408]{4,3,2,1,0:T(8,128)(2,1)} %group.7), channel_id=1, source_target_pairs={{0,16},{8,24},{16,0},{24,8},{1,17},{9,25},{17,1},{25,9},{2,18},{10... | collective-permute-start | bytes 1081352 | tf_op jit(solution)/shard_map/ppermute | solution.py:42
  363.8 29.8 %collective-permute-start.13 = (bf16[1,1,1,128,1408]{4,3,2,1,0:T(8,128)(2,1)}, bf16[1,1,1,128,1408]{4,3,2,1,0:T(8,128)(2,1)S(1)}, u32[]{:S(2)}, u32[]{:S(2)}) collective-permute-start(bf16[1,1,1,128,1408]{4,3,2,1,0:T(8,128)(2,1)} %group.10), channel_id=1, source_target_pairs={{0,8},{8,0},{16,24},{24,16},{1,9},{9,1},{17,25},{25,17},{2,10},{10... | collective-permute-start | bytes 1081352 | tf_op jit(solution)/shard_map/ppermute | solution.py:42
  821.0 114.7 %reduce-scatter.9.cloned.1.call-start = ((), (), s32[]{:S(2)}) async-start(), calls=%async_computation.19 | async-start | bytes 4718592 | tf_op jit(solution)/shard_map/reduce_scatter | solution.py:93
  874.5 63.4 %all-to-all-start.4 = ((bf16[128,4,512]{2,0,1:T(8,128)(2,1)}), bf16[128,4,512]{2,0,1:T(8,128)(2,1)S(1)}, u32[]{:S(2)}, u32[]{:S(2)}) async-start(bf16[128,4,512]{2,0,1:T(8,128)(2,1)} %bitcast.194), calls=%async_computation.7 | async-start | bytes 1048576 | tf_op jit(solution)/shard_map/all_to_all | solution.py:102
  878.1 124.2 %all-gather.20.cloned.1.call-start = ((), (), s32[]{:S(2)}) async-start(), calls=%async_computation.21 | async-start | bytes 4718592 | tf_op jit(solution)/shard_map/all_gather | solution.py:89
  952.1 150.1 %all-reduce.11.cloned.1.call-start = ((), (), s32[]{:S(2)}) async-start(), calls=%async_computation.23 | async-start | bytes 2621440 | tf_op jit(solution)/shard_map/psum | solution.py:1385
  1040.7 200.9 %reduce-scatter.17.cloned.1.call-start = ((), (), s32[]{:S(2)}) async-start(), calls=%async_computation.25 | async-start | bytes 3932160 | tf_op jit(solution)/shard_map/reduce_scatter | solution.py:1327
  1048.3 235.3 %reduce-scatter.15.cloned.1.call-start = ((), (), s32[]{:S(2)}) async-start(), calls=%async_computation.24 | async-start | bytes 4718592 | tf_op jit(solution)/shard_map/reduce_scatter | solution.py:93
  1054.9 54.1 %collective-permute-start.23 = (bf16[1024,384]{1,0:T(8,128)(2,1)}, bf16[1024,384]{1,0:T(8,128)(2,1)S(1)}, u32[]{:S(2)}, u32[]{:S(2)}) collective-permute-start(bf16[1024,384]{1,0:T(8,128)(2,1)} %get-tuple-element.112), channel_id=1, source_target_pairs={{0,16},{8,24},{16,0},{24,8},{1,17},{9,25},{17,1},{25,9},{2,18},{10... | collective-permute-start | bytes 2359304 | tf_op jit(solution)/shard_map/ppermute | solution.py:42
  1056.3 53.3 %collective-permute-start.22 = (bf16[1024,384]{1,0:T(8,128)(2,1)}, bf16[1024,384]{1,0:T(8,128)(2,1)}, u32[]{:S(2)}, u32[]{:S(2)}) collective-permute-start(bf16[1024,384]{1,0:T(8,128)(2,1)} %get-tuple-element.112), channel_id=1, source_target_pairs={{0,8},{8,0},{16,24},{24,16},{1,9},{9,1},{17,25},{25,17},{2,10},{10... | collective-permute-start | bytes 2359304 | tf_op jit(solution)/shard_map/ppermute | solution.py:42
  1109.1 32.4 %collective-permute-start.24 = (bf16[512,384]{1,0:T(8,128)(2,1)S(1)}, bf16[512,384]{1,0:T(8,128)(2,1)S(1)}, u32[]{:S(2)}, u32[]{:S(2)}) collective-permute-start(bf16[512,384]{1,0:T(8,128)(2,1)S(1)} %slice.170), channel_id=1, source_target_pairs={{0,8},{8,0},{16,24},{24,16},{1,9},{9,1},{17,25},{25,17},{2,10},{10... | collective-permute-start | bytes 1179656 | tf_op jit(solution)/shard_map/ppermute | solution.py:42
  1110.8 30.6 %collective-permute-start.25 = (bf16[512,384]{1,0:T(8,128)(2,1)S(1)}, bf16[512,384]{1,0:T(8,128)(2,1)S(1)}, u32[]{:S(2)}, u32[]{:S(2)}) collective-permute-start(bf16[512,384]{1,0:T(8,128)(2,1)S(1)} %slice.171), channel_id=1, source_target_pairs={{0,16},{8,24},{16,0},{24,8},{1,17},{9,25},{17,1},{25,9},{2,18},{10... | collective-permute-start | bytes 1179656 | tf_op jit(solution)/shard_map/ppermute | solution.py:42
  1117.6 22.4 %collective-permute-start.29 = (bf16[512,128]{1,0:T(8,128)(2,1)S(1)}, bf16[512,128]{1,0:T(8,128)(2,1)S(1)}, u32[]{:S(2)}, u32[]{:S(2)}) collective-permute-start(bf16[512,128]{1,0:T(8,128)(2,1)S(1)} %slice.175), channel_id=1, source_target_pairs={{0,16},{8,24},{16,0},{24,8},{1,17},{9,25},{17,1},{25,9},{2,18},{10... | collective-permute-start | bytes 393224 | tf_op jit(solution)/shard_map/ppermute | solution.py:42
  1120.7 19.4 %collective-permute-start.28 = (bf16[512,128]{1,0:T(8,128)(2,1)S(1)}, bf16[512,128]{1,0:T(8,128)(2,1)S(1)}, u32[]{:S(2)}, u32[]{:S(2)}) collective-permute-start(bf16[512,128]{1,0:T(8,128)(2,1)S(1)} %slice.174), channel_id=1, source_target_pairs={{0,8},{8,0},{16,24},{24,16},{1,9},{9,1},{17,25},{25,17},{2,10},{10... | collective-permute-start | bytes 393224 | tf_op jit(solution)/shard_map/ppermute | solution.py:42
  1149.0 165.4 %reduce-scatter.13.cloned.1.call-start = ((), (), s32[]{:S(2)}) async-start(), calls=%async_computation.22 | async-start | bytes 4718592 | tf_op jit(solution)/shard_map/reduce_scatter | solution.py:93
  1149.2 19.9 %collective-permute-start.19 = (bf16[1024,384]{0,1:T(8,128)(2,1)}, bf16[1024,384]{0,1:T(8,128)(2,1)}, u32[]{:S(2)}, u32[]{:S(2)}) collective-permute-start(bf16[1024,384]{0,1:T(8,128)(2,1)} %get-tuple-element.107), channel_id=1, source_target_pairs={{0,16},{8,24},{16,0},{24,8},{1,17},{9,25},{17,1},{25,9},{2,18},{10... | collective-permute-start | bytes 2359304 | tf_op jit(solution)/shard_map/ppermute | solution.py:42
  1151.7 22.1 %collective-permute-start.18 = (bf16[1024,384]{0,1:T(8,128)(2,1)}, bf16[1024,384]{0,1:T(8,128)(2,1)}, u32[]{:S(2)}, u32[]{:S(2)}) collective-permute-start(bf16[1024,384]{0,1:T(8,128)(2,1)} %get-tuple-element.107), channel_id=1, source_target_pairs={{0,8},{8,0},{16,24},{24,16},{1,9},{9,1},{17,25},{25,17},{2,10},{10... | collective-permute-start | bytes 2359304 | tf_op jit(solution)/shard_map/ppermute | solution.py:42
  1219.7 27.4 %collective-permute-start.31 = (bf16[512,512]{1,0:T(8,128)(2,1)S(1)}, bf16[512,512]{1,0:T(8,128)(2,1)}, u32[]{:S(2)}, u32[]{:S(2)}) collective-permute-start(bf16[512,512]{1,0:T(8,128)(2,1)S(1)} %add.194), channel_id=1, source_target_pairs={{0,16},{8,24},{16,0},{24,8},{1,17},{9,25},{17,1},{25,9},{2,18},{10... | collective-permute-start | bytes 1572872 | tf_op jit(solution)/shard_map/ppermute | solution.py:42
  (70 other events, 857.1 us)
Sparse Core Ops, SparseCore 0:
  9.6 50.8 all-gather.7
  62.1 45.8 all-gather.11
  128.1 20.5 all-gather.9
  222.9 48.0 reduce-scatter.6
  276.8 45.1 all-gather.13
  324.0 53.6 all-gather.15
  379.3 48.0 all-gather.17
  821.1 51.4 reduce-scatter.10
  875.5 48.1 reduce-scatter.8
  952.2 46.2 all-gather.19
  1040.8 61.2 all-reduce.10
  1105.0 59.9 reduce-scatter.16
  1167.3 50.2 reduce-scatter.14
  1219.7 50.2 reduce-scatter.12

commit v2 on v1

--- a/solution.py
+++ b/solution.py
@@ -30,12 +30,37 @@
     return pltpu.CompilerParams(vmem_limit_bytes=VMEM_LIMIT)
 
 
-def cost(flops, read, written):
-    return pl.CostEstimate(flops=flops, bytes_accessed=read + written, transcendentals=0)
+def cost(microseconds):
+    return pl.CostEstimate(flops=int(microseconds * 0.575e9), bytes_accessed=0, transcendentals=0)
+
+
+waited = []
 
 
 def after(value, *others):
-    return lax.optimization_barrier((value, others))[0]
+    value, others = lax.optimization_barrier((value, others))
+    waited.extend(jax.tree.leaves(others))
+    return value
+
+
+def together(*values):
+    return lax.optimization_barrier(values)
+
+
+def settle_kernel(value, *refs):
+    refs[-1][...] = value[...]
+
+
+def settle(value):
+    vmem = pl.BlockSpec(memory_space=pltpu.VMEM)
+    return pl.pallas_call(
+        settle_kernel,
+        in_specs=[vmem] + [pl.BlockSpec(memory_space=pl.ANY)] * len(waited),
+        out_specs=vmem,
+        out_shape=jax.ShapeDtypeStruct(value.shape, value.dtype),
+        cost_estimate=cost(1),
+        name="settle",
+    )(value, *waited)
 
 
 def swap(value, bit):
@@ -55,13 +80,21 @@
     return lax.dynamic_index_in_dim(value, index, axis, keepdims=False)
 
 
+def from_others(block):
+    half = block.shape[0] // 2
+    from_x = swap(block, 1)
+    from_y = swap(block, 2)
+    return from_x, from_y, swap(from_y[:half], 1), swap(from_x[half:], 2)
+
+
 def collect(block):
     if not square():
         return lax.all_gather(block, "gx", axis=0, tiled=False)
-    half = block.shape[0] // 2
-    from_x = swap(block, 1)
-    from_y = swap(block, 2)
-    across = jnp.concatenate([swap(from_y[:half], 1), swap(from_x[half:], 2)], axis=0)
+    return stacked(block, *from_others(block))
+
+
+def stacked(block, from_x, from_y, low, high):
+    across = jnp.concatenate([low, high], axis=0)
     me = lax.axis_index("gx")
     whole = jnp.zeros((4,) + block.shape, block.dtype)
     for index, value in ((me, block), (me ^ 1, from_x), (me ^ 2, from_y), (me ^ 3, across)):
@@ -85,13 +118,25 @@
     return value + swap(value, 2)
 
 
+def inner_rows(value):
+    parts = lax.axis_size("gx")
+    value = value.reshape(parts, -1, value.shape[1])
+    return lax.all_to_all(value, "gx", split_axis=0, concat_axis=0, tiled=True)
+
+
+def tower_step(value, step):
+    size, bit = lax.axis_size("gy"), 2**step
+    if bit >= size:
+        return value
+    return value + lax.ppermute(value, "gy", [(i, i ^ bit) for i in range(size)])
+
+
 def spread_rows(value):
     return lax.all_gather(value, "gy", axis=0, tiled=True)
 
 
 def outer_total(partial):
-    total = lax.psum_scatter(partial.astype(BF16), "gy", scatter_dimension=0, tiled=True)
-    return total.astype(F32)
+    return lax.psum_scatter(partial.astype(BF16), "gy", scatter_dimension=0, tiled=True)
 
 
 def to_tokens(value):
@@ -136,6 +181,7 @@
         out_specs=pl.BlockSpec((block, experts * cap), lambda b: (b, 0)),
         out_shape=jax.ShapeDtypeStruct((tokens, experts * cap), BF16),
         compiler_params=params(),
+        cost_estimate=cost(7),
         name="one_hot",
     )(code)
 
@@ -145,24 +191,50 @@
     out_ref[...] = moved.reshape(out_ref.shape)
 
 
-def dispatch(chosen, rows, cap, blocks):
+def dispatch_scaled_kernel(chosen_ref, rows_ref, scale_ref, out_ref, scale_out_ref):
+    dispatch_kernel(chosen_ref, rows_ref, out_ref)
+    high, middle, low = thirds(scale_ref[...])
+    parts = jnp.concatenate([high, middle, low], axis=1)
+    moved = dot_tn(chosen_ref[...], parts)
+    moved = moved[:, 0:1] + moved[:, 1:2] + moved[:, 2:3]
+    scale_out_ref[...] = moved.reshape(scale_out_ref.shape)
+
+
+def thirds(value):
+    high = value.astype(BF16)
+    rest = value - high.astype(F32)
+    middle = rest.astype(BF16)
+    return high, middle, (rest - middle.astype(F32)).astype(BF16)
+
+
+def dispatch(chosen, rows, cap, blocks, scale=None):
     tokens, width = rows.shape
     slots = chosen.shape[1]
     experts = slots // cap
     block = tokens // blocks
-    return pl.pallas_call(
-        dispatch_kernel,
+    specs = [
+        pl.BlockSpec((block, slots), lambda b: (b, 0)),
+        pl.BlockSpec((block, width), lambda b: (b, 0)),
+    ]
+    out_specs = [pl.BlockSpec((experts, cap, width), lambda b: (0, b, 0))]
+    shapes = [jax.ShapeDtypeStruct((experts, blocks * cap, width), BF16)]
+    values = [chosen, rows]
+    if scale is not None:
+        specs.append(pl.BlockSpec((block, 1), lambda b: (b, 0)))
+        out_specs.append(pl.BlockSpec((experts, cap, 1), lambda b: (0, b, 0)))
+        shapes.append(jax.ShapeDtypeStruct((experts, blocks * cap, 1), F32))
+        values.append(scale)
+    outs = pl.pallas_call(
+        dispatch_kernel if scale is None else dispatch_scaled_kernel,
         grid=(blocks,),
-        in_specs=[
-            pl.BlockSpec((block, slots), lambda b: (b, 0)),
-            pl.BlockSpec((block, width), lambda b: (b, 0)),
-        ],
-        out_specs=pl.BlockSpec((experts, cap, width), lambda b: (0, b, 0)),
-        out_shape=jax.ShapeDtypeStruct((experts, blocks * cap, width), BF16),
+        in_specs=specs,
+        out_specs=out_specs,
+        out_shape=shapes,
         compiler_params=params(),
-        cost_estimate=cost(2 * tokens * slots * width, 4 * tokens * width, 2 * tokens * width),
+        cost_estimate=cost(10),
         name="dispatch",
-    )(chosen, rows)
+    )(*values)
+    return outs[0] if scale is None else outs
 
 
 def combine_kernel(groups, chosen_ref, *refs):
@@ -190,7 +262,7 @@
         out_specs=pl.BlockSpec((block, width), lambda b: (b, 0)),
         out_shape=jax.ShapeDtypeStruct((tokens, width), BF16),
         compiler_params=params(),
-        cost_estimate=cost(2 * tokens * slots * width, 4 * tokens * width, 2 * tokens * width),
+        cost_estimate=cost(9),
         name="combine",
     )(chosen, *pieces, *extra)
 
@@ -238,11 +310,7 @@
         ),
         out_shape=jax.ShapeDtypeStruct((count, many, parts, slots, width), kind),
         compiler_params=params(),
-        cost_estimate=cost(
-            2 * many * count * parts * slots * depth * width,
-            2 * many * count * depth * width,
-            2 * many * count * parts * slots * width,
-        ),
+        cost_estimate=cost(4),
         name="group",
     )(picks, *([rows] * parts), *weights, *adds)
 
@@ -304,7 +372,8 @@
     rows,
     w_gate,
     w_up,
-    grad_hidden,
+    grad_low,
+    grad_high,
     factors,
     own_out,
     x_out,
@@ -433,6 +502,12 @@
                 first[expert, spot, number] = out.astype(BF16)
             second_copy(pair, odd).start()
 
+    def hidden_gradient(expert):
+        half = grad_low.shape[0]
+        low = grad_low[jnp.minimum(expert, half - 1)].astype(F32)
+        high = grad_high[jnp.maximum(expert - half, 0)].astype(F32)
+        return jnp.where(expert < half, low, high)
+
     def finish(pair):
         fetch(pair)
         for odd in range(2):
@@ -451,7 +526,7 @@
             scaled, grad_gate_pre, grad_up_pre, grad_gate = expert_body(
                 gate_pre * scale,
                 up_pre * scale,
-                grad_hidden[expert].astype(F32),
+                hidden_gradient(expert),
                 factors[expert, :, 0:1],
             )
             first[expert, spot, 0] = grad_gate_pre
@@ -529,7 +604,7 @@
     lax.fori_loop(0, pairs, drain, 0)
 
 
-def routed_experts(rows, w_gate, w_up, grad_hidden, factors):
+def routed_experts(rows, w_gate, w_up, grad_low, grad_high, factors):
     experts, quarters, slots, depth = rows.shape
     width = w_gate.shape[2]
     vmem = pl.BlockSpec(memory_space=pltpu.VMEM)
@@ -538,7 +613,7 @@
     dma = pltpu.SemaphoreType.DMA
     return pl.pallas_call(
         experts_kernel,
-        in_specs=[vmem, anywhere, anywhere, vmem, vmem],
+        in_specs=[vmem, anywhere, anywhere, vmem, vmem, vmem],
         out_specs=[anywhere] * 4 + [vmem] * 3,
         out_shape=[block] * 4
         + [
@@ -558,11 +633,9 @@
         compiler_params=pltpu.CompilerParams(
             collective_id=0, has_side_effects=True, vmem_limit_bytes=VMEM_LIMIT
         ),
-        cost_estimate=cost(
-            12 * experts * quarters * slots * depth * width, 12 * experts * depth * width, 0
-        ),
+        cost_estimate=cost(390),
         name="routed_experts",
-    )(rows, w_gate, w_up, grad_hidden, factors)
+    )(rows, w_gate, w_up, grad_low, grad_high, factors)
 
 
 def sum_kernel(base, by_quarter, own_weights, transposed, rows, weight, out, sent, first, second, held, *sems):
@@ -677,126 +750,129 @@
         compiler_params=pltpu.CompilerParams(
             collective_id=number, has_side_effects=True, vmem_limit_bytes=VMEM_LIMIT
         ),
-        cost_estimate=cost(8 * items * slots * depth * width, 2 * items * depth * width, 0),
+        cost_estimate=cost(13.5 * items if own_weights else 20 + 25 * width // 512),
         name="square_sum",
     )(rows, weight)
 
 
-def band_total(rows, weight, number, transposed=False):
+def band_total(rows, weight, number, transposed=False, kind=F32):
     if not square():
         whole = (dot_nt(rows, weight) if transposed else dot(rows, weight)).astype(BF16)
-        return lax.psum_scatter(whole, "gx", scatter_dimension=0, tiled=True).astype(F32)
+        return lax.psum_scatter(whole, "gx", scatter_dimension=0, tiled=True).astype(kind)
     source = rows.reshape(4, 4, rows.shape[0] // 16, rows.shape[1])
-    out = square_sum(source, weight, 0, 4, number, transposed, True, F32)
+    out = square_sum(source, weight, 0, 4, number, transposed, True, kind)
     return out.reshape(-1, out.shape[2])
 
 
-def hidden_kernel(base, hidden, weight, x_out, y_out, d_out, out, held, loaded, *sems):
-    x_send, x_recv, y_send, y_recv, d_send, d_recv, weight_sem, load_sem = sems
+def small_kernel(both, inner_ref, outer_ref, inner_out, outer_out, inner_land, outer_land, send, recv, far_send, far_recv):
     x, y, x_other, y_other = neighbours()
     me = 2 * y + x
-    across = 3 - me
-    pairs = out.shape[0] // 2
-    slots = out.shape[2]
-    greet(x_other, y_other)
-
-    def x_copy(item):
-        return remote(hidden.at[base + item], x_out.at[item], x_send.at[item], x_recv.at[item], x_other)
-
-    def y_copy(item):
-        return remote(hidden.at[base + item], y_out.at[item], y_send.at[item], y_recv.at[item], y_other)
-
-    def far_copy(item, odd):
-        source, other = (x_out, y_other) if odd else (y_out, x_other)
-        return remote(source.at[item], d_out.at[item], d_send.at[item], d_recv.at[item], other)
-
-    def weight_copy(item, odd):
-        return pltpu.make_async_copy(weight.at[base + item], held.at[odd], weight_sem.at[odd])
-
-    def load(item, odd, number):
-        source = (hidden.at[base + item], x_out.at[item], y_out.at[item], d_out.at[item])[number]
-        return pltpu.make_async_copy(source, loaded.at[odd, number], load_sem.at[odd, number])
-
-    def begin(pair, _):
-        for odd in range(2):
-            x_copy(2 * pair + odd).start()
-            y_copy(2 * pair + odd).start()
-        return 0
-
-    def pass_on(pair):
-        for odd in range(2):
-            item = 2 * pair + odd
-            (x_copy if odd else y_copy)(item).wait_recv()
-            far_copy(item, odd).start()
-
-    def multiply(pair):
-        for odd in range(2):
-            item = 2 * pair + odd
-            weight_copy(item, odd).start()
-            (y_copy if odd else x_copy)(item).wait_recv()
-            for number in range(3):
-                load(item, odd, number).start()
-        for odd in range(2):
-            item = 2 * pair + odd
-            far_copy(item, odd).wait_recv()
-            load(item, odd, 3).start()
-        for odd in range(2):
-            item = 2 * pair + odd
-            weight_copy(item, odd).wait()
-            for number in range(4):
-                load(item, odd, number).wait()
-            source = jnp.concatenate([loaded[odd, number, 0] for number in range(4)], axis=0)
-            total = dot(source, held[odd]).astype(BF16)
-            for number, quarter in enumerate((me, x_other, y_other, across)):
-                out[item, quarter] = total[number * slots : (number + 1) * slots]
-
-    lax.fori_loop(0, pairs, begin, 0)
-
-    def step(number, _):
-        for lag, stage in enumerate((pass_on, multiply)):
-
-            @pl.when((number >= lag) & (number < pairs + lag))
-            def _(lag=lag, stage=stage):
-                stage(number - lag)
-
-        return 0
-
-    lax.fori_loop(0, pairs + 1, step, 0)
-
-    def drain(pair, _):
-        for odd in range(2):
-            item = 2 * pair + odd
-            x_copy(item).wait_send()
-            y_copy(item).wait_send()
-            far_copy(item, odd).wait_send()
-        return 0
-
-    lax.fori_loop(0, pairs, drain, 0)
-
-
-def hidden_products(hidden, weight, base, items, number):
-    slots, width = hidden.shape[2:]
-    depth = weight.shape[2]
-    anywhere = pl.BlockSpec(memory_space=pl.ANY)
-    block = jax.ShapeDtypeStruct((items, 1, slots, width), BF16)
+    peers = (x_other, y_other, 3 - me)
+    here = lax.axis_index("gy")
+    size = outer_land.shape[0]
+    barrier = pltpu.get_barrier_semaphore()
+    for other in peers:
+        pl.semaphore_signal(barrier, inc=1, device_id={"gx": other}, device_id_type=pl.DeviceIdType.MESH)
+    for step in range(1, size if both else 1):
+        pl.semaphore_signal(
+            barrier, inc=1, device_id={"gy": (here + step) % size}, device_id_type=pl.DeviceIdType.MESH
+        )
+    pl.semaphore_wait(barrier, 3 + (size - 1 if both else 0))
+
+    inner_land[me] = inner_ref[...]
+
+    def inner_copy(number):
+        return remote(inner_ref, inner_land.at[me], send.at[number], recv.at[number], peers[number])
+
+    for number in range(3):
+        inner_copy(number).start()
+    for number in range(3):
+        inner_copy(number).wait()
+    total = inner_land[0]
+    for number in range(1, 4):
+        total = total + inner_land[number]
+    inner_out[...] = total
+    if not both:
+        outer_out[...] = outer_ref[...]
+        return
+    outer_land[here, 0:8] = outer_ref[...]
+    outer_land[here, 8:16] = total
+
+    def outer_copy(step):
+        return pltpu.make_async_remote_copy(
+            src_ref=outer_land.at[here],
+            dst_ref=outer_land.at[here],
+            send_sem=far_send.at[step - 1],
+            recv_sem=far_recv.at[step - 1],
+            device_id={"gy": (here + step) % size},
+            device_id_type=pl.DeviceIdType.MESH,
+        )
+
+    for step in range(1, size):
+        outer_copy(step).start()
+    for step in range(1, size):
+        outer_copy(step).wait()
+    total = outer_land[0]
+    for number in range(1, size):
+        total = total + outer_land[number]
+    outer_out[...] = total
+
+
+def small_totals(inner, outer, number):
+    both = outer is not None
+    size = lax.axis_size("gy")
     dma = pltpu.SemaphoreType.DMA
+    vmem = pl.BlockSpec(memory_space=pltpu.VMEM)
     return pl.pallas_call(
-        functools.partial(hidden_kernel, base),
-        in_specs=[anywhere, anywhere],
-        out_specs=[anywhere] * 3 + [pl.BlockSpec(memory_space=pltpu.VMEM)],
-        out_shape=[block] * 3 + [jax.ShapeDtypeStruct((items, 4, slots, depth), BF16)],
+        functools.partial(small_kernel, both),
+        in_specs=[vmem, vmem],
+        out_specs=[vmem, vmem],
+        out_shape=[
+            jax.ShapeDtypeStruct((8, 128), F32),
+            jax.ShapeDtypeStruct((16, 128) if both else (8, 128), F32),
+        ],
         scratch_shapes=[
-            pltpu.VMEM((2,) + weight.shape[1:], BF16),
-            pltpu.VMEM((2, 4, 1, slots, width), BF16),
-        ]
-        + [dma((items,))] * 6
-        + [dma((2,)), dma((2, 4))],
+            pltpu.VMEM((4, 8, 128), F32),
+            pltpu.VMEM((size, 16, 128), F32),
+            dma((3,)),
+            dma((3,)),
+            dma((size - 1,)),
+            dma((size - 1,)),
+        ],
         compiler_params=pltpu.CompilerParams(
             collective_id=number, has_side_effects=True, vmem_limit_bytes=VMEM_LIMIT
         ),
-        cost_estimate=cost(8 * items * slots * depth * width, 2 * items * depth * width, 0),
-        name="hidden_products",
-    )(hidden, weight)
+        cost_estimate=cost(6),
+        name="small_totals",
+    )(inner, outer if both else jnp.zeros((8, 128), F32))
+
+
+def shared_sums_kernel(parts, gate, up, down):
+    width = gate.shape[0]
+    wide = parts.shape[2] // 3
+    total = parts[0].astype(F32)
+    for number in range(1, parts.shape[0]):
+        total = total + parts[number].astype(F32)
+    total = total.T
+    gate[...] = total[:width]
+    up[...] = total[wide : wide + width]
+    down[...] = total[2 * wide : 2 * wide + width]
+
+
+def shared_sums(parts, width):
+    rows = parts.shape[1]
+    block = 128
+    many = parts.shape[0]
+    return pl.pallas_call(
+        shared_sums_kernel,
+        grid=(rows // block,),
+        in_specs=[pl.BlockSpec((many, block, parts.shape[2]), lambda i: (0, i, 0))],
+        out_specs=[pl.BlockSpec((width, block), lambda i: (0, i))] * 3,
+        out_shape=[jax.ShapeDtypeStruct((width, rows), F32)] * 3,
+        compiler_params=params(),
+        cost_estimate=cost(5),
+        name="shared_sums",
+    )(parts)
 
 
 def group_specs(groups):
@@ -872,20 +948,21 @@
         ),
         out_shape=jax.ShapeDtypeStruct((count, quarters, slots, width), BF16),
         compiler_params=params(),
-        cost_estimate=cost(
-            2 * terms * count * quarters * slots * depth * width,
-            2 * terms * count * (quarters * slots + width) * depth,
-            2 * count * quarters * slots * width,
-        ),
+        cost_estimate=cost(4 * count),
         name="back",
     )(picks, *values, *weights)
 
 
-def weight_grad_kernel(groups, flip, picks_ref, *refs):
+def weight_grad_kernel(groups, flip, scaled, picks_ref, *refs):
     terms = groups[0][2][0][1]
     quarters = len(groups[0][2])
     outs = refs[-terms:]
-    rows = jnp.concatenate([ref[0, 0] for ref in refs[:quarters]], axis=0)
+    rows = [ref[0, 0] for ref in refs[:quarters]]
+    if scaled:
+        scales = refs[quarters : 2 * quarters]
+        rows = [(row.astype(F32) * ref[0, 0]).astype(BF16) for row, ref in zip(rows, scales)]
+        refs = refs[quarters:]
+    rows = jnp.concatenate(rows, axis=0)
 
     def body(pieces):
         for term in range(terms):
@@ -895,7 +972,7 @@
     for_group(groups, refs[quarters:], body)
 
 
-def weight_grad(rows, groups, picks, flip):
+def weight_grad(rows, groups, picks, flip, scale=None):
     first = groups[0][0]
     count = sum(g[1] for g in groups)
     quarters = len(groups[0][2])
@@ -905,10 +982,17 @@
         pl.BlockSpec((1, 1, slots, depth), lambda e, p, q=quarter: (first + e, p[q], 0, 0))
         for quarter in range(quarters)
     ]
-    more, values = group_specs(groups)
+    values = [rows] * quarters
+    if scale is not None:
+        specs += [
+            pl.BlockSpec((1, 1, slots, 1), lambda e, p, q=quarter: (first + e, p[q], 0, 0))
+            for quarter in range(quarters)
+        ]
+        values += [scale] * quarters
+    more, others = group_specs(groups)
     shape = (width, depth) if flip else (depth, width)
     return pl.pallas_call(
-        functools.partial(weight_grad_kernel, shapes_of(groups), flip),
+        functools.partial(weight_grad_kernel, shapes_of(groups), flip, scale is not None),
         grid_spec=pltpu.PrefetchScalarGridSpec(
             num_scalar_prefetch=1,
             grid=(count,),
@@ -917,22 +1001,127 @@
         ),
         out_shape=[jax.ShapeDtypeStruct((count,) + shape, F32)] * terms,
         compiler_params=params(),
-        cost_estimate=cost(
-            2 * terms * count * quarters * slots * depth * width,
-            2 * count * quarters * slots * (depth + terms * width),
-            4 * terms * count * depth * width,
+        cost_estimate=cost(1),
+        name="weight_grad",
+    )(picks, *values, *others)
+
+
+def side_by_side_kernel(gate, up, down, out):
+    width = gate.shape[1]
+    wide = out.shape[1] // 3
+    out[...] = jnp.zeros_like(out)
+    out[:, :width] = gate[...]
+    out[:, wide : wide + width] = up[...]
+    out[:, 2 * wide : 2 * wide + width] = down[...].T
+
+
+def side_by_side(gate, up, down, wide):
+    return pl.pallas_call(
+        side_by_side_kernel,
+        out_shape=jax.ShapeDtypeStruct((gate.shape[0], 3 * wide), BF16),
+        compiler_params=params(),
+        cost_estimate=cost(3),
+        name="side_by_side",
+    )(gate, up, down)
+
+
+def shared_kernel(picks_ref, norm, scale, grad, *refs):
+    blocks, (hidden_out, grads_out, part_out, forward_out, weight) = refs[:-5], refs[-5:]
+    wide = hidden_out.shape[1]
+
+    @pl.when(pl.program_id(0) == 0)
+    def _():
+        rows = blocks[0].shape[0]
+        if len(blocks) == 1:
+            weight[...] = blocks[0][...]
+        else:
+            half = rows // 2
+            for number in range(3):
+                start = pl.multiple_of(picks_ref[number] * rows, rows)
+                weight[pl.ds(start, rows)] = blocks[number][...]
+            start = pl.multiple_of(picks_ref[3] * rows, rows)
+            weight[pl.ds(start, half)] = blocks[3][...]
+            weight[pl.ds(start + half, half)] = blocks[4][...]
+
+    both = dot(norm[...], weight[:, : 2 * wide]) * scale[...]
+    gate_pre, up_pre = both[:, :wide], both[:, wide:]
+    grad_hidden = dot(grad[...], weight[:, 2 * wide :])
+    sigma = jax.nn.sigmoid(gate_pre)
+    act = gate_pre * sigma
+    hidden = (act * up_pre).astype(BF16)
+    hidden_out[...] = hidden
+    forward_out[...] = dot_nt(hidden, weight[:, 2 * wide :]).astype(BF16)
+    grads = jnp.concatenate(
+        [
+            (grad_hidden * up_pre * sigma * (1.0 + gate_pre * (1.0 - sigma))).astype(BF16),
+            (grad_hidden * act).astype(BF16),
+        ],
+        axis=1,
+    )
+    grads_out[...] = (grads.astype(F32) * scale[...]).astype(BF16)
+    part_out[...] = dot_nt(grads, weight[:, : 2 * wide]).astype(BF16)
+
+
+def shared_experts(norm, scale, grad, weights, picks):
+    rows, depth = norm.shape
+    wide = weights[0].shape[1] // 3
+    block = 256
+    return pl.pallas_call(
+        shared_kernel,
+        grid_spec=pltpu.PrefetchScalarGridSpec(
+            num_scalar_prefetch=1,
+            grid=(rows // block,),
+            in_specs=[
+                pl.BlockSpec((block, depth), lambda i, p: (i, 0)),
+                pl.BlockSpec((block, 1), lambda i, p: (i, 0)),
+                pl.BlockSpec((block, depth), lambda i, p: (i, 0)),
+            ]
+            + [pl.BlockSpec(weight.shape, lambda i, p: (0, 0)) for weight in weights],
+            out_specs=[
+                pl.BlockSpec((block, wide), lambda i, p: (i, 0)),
+                pl.BlockSpec((block, 2 * wide), lambda i, p: (i, 0)),
+                pl.BlockSpec((block, depth), lambda i, p: (i, 0)),
+                pl.BlockSpec((block, depth), lambda i, p: (i, 0)),
+            ],
+            scratch_shapes=[pltpu.VMEM((depth, 3 * wide), BF16)],
         ),
-        name="weight_grad",
-    )(picks, *([rows] * quarters), *values)
-
-
-def silu(value):
-    return value * jax.nn.sigmoid(value)
-
-
-def silu_grad(value):
-    sigma = jax.nn.sigmoid(value)
-    return sigma * (1.0 + value * (1.0 - sigma))
+        out_shape=[
+            jax.ShapeDtypeStruct((rows, wide), BF16),
+            jax.ShapeDtypeStruct((rows, 2 * wide), BF16),
+            jax.ShapeDtypeStruct((rows, depth), BF16),
+            jax.ShapeDtypeStruct((rows, depth), BF16),
+        ],
+        compiler_params=params(),
+        cost_estimate=cost(16),
+        name="shared_experts",
+    )(picks, norm, scale, grad, *weights)
+
+
+def shared_weights_kernel(norm, grads, grad, hidden, out):
+    both = grads.shape[1]
+    out[:, :both] = dot_tn(norm[...], grads[...]).astype(BF16)
+    out[:, both:] = dot_tn(grad[...], hidden[...]).astype(BF16)
+
+
+def shared_weights(norm, grads, grad, hidden):
+    rows, depth = norm.shape
+    block = 256
+    width = grads.shape[1] + hidden.shape[1]
+    return pl.pallas_call(
+        shared_weights_kernel,
+        grid=(depth // block,),
+        in_specs=[
+            pl.BlockSpec((rows, block), lambda i: (0, i)),
+            pl.BlockSpec(grads.shape, lambda i: (0, 0)),
+            pl.BlockSpec((rows, block), lambda i: (0, i)),
+            pl.BlockSpec(hidden.shape, lambda i: (0, 0)),
+        ],
+        out_specs=pl.BlockSpec((block, width), lambda i: (i, 0)),
+        out_shape=jax.ShapeDtypeStruct((depth, width), BF16),
+        compiler_params=params(),
+        cost_estimate=cost(10),
+        name="shared_weights",
+    )(norm, grads, grad, hidden)
 
 
 def rope_tables(length):
@@ -961,9 +1150,10 @@
     return seen
 
 
-def attention_kernel(heads, starts_ref, proj, latent, gain, w_expand, cos, sin, out, logs, q_out, k_out, v_out, n_out):
+def attention_kernel(heads, starts_ref, proj_ref, rows_scale, latent, gain, w_expand, cos, sin, out, logs, q_out, k_out, v_out, n_out):
     scale = (DN + DR) ** (-0.5)
     cosine, sine = cos[...], sin[...]
+    proj = proj_ref[...] * rows_scale[...]
     lat = latent[...].astype(F32)
     compressed = lat[:, :L]
     root = lax.rsqrt(jnp.mean(compressed * compressed, axis=1, keepdims=True) + EPS)
@@ -991,7 +1181,7 @@
         logs[0, head] = peak + jnp.log(total)
 
 
-def attention_forward(starts, proj, latent, gain, w_expand, cosine, sine, heads):
+def attention_forward(starts, proj, rows_scale, latent, gain, w_expand, cosine, sine, heads):
     band = proj.shape[0]
     seqs = band // SEQ_LEN
 
@@ -1014,6 +1204,7 @@
             grid=(seqs,),
             in_specs=[
                 rows(proj.shape[1]),
+                rows(1),
                 rows(L + DR),
                 whole((1, L)),
                 whole(w_expand.shape),
@@ -1031,8 +1222,9 @@
             jax.ShapeDtypeStruct((band, L), BF16),
         ],
         compiler_params=params(),
+        cost_estimate=cost(12),
         name="attention",
-    )(starts, proj, latent, gain[None], w_expand, cosine, sine)
+    )(starts, proj, rows_scale, latent, gain[None], w_expand, cosine, sine)
 
 
 def attention_back_kernel(heads, starts_ref, q_ref, k_ref, v_ref, logs, grad, w_expand, cos, sin, dq_out, de_out, dl_out):
@@ -1099,8 +1291,46 @@
         ),
         out_shape=[jax.ShapeDtypeStruct((band, width), BF16) for width in widths],
         compiler_params=params(),
+        cost_estimate=cost(14),
         name="attention_back",
     )(starts, query, key, value, logs, grad, w_expand, cosine, sine)
+
+
+def norm_products_kernel(picks_ref, *refs):
+    query, latent = refs[:5], refs[5:10]
+    weight, whole_out, part_out = refs[10:]
+    half = query[3].shape[0]
+
+    def write(number, start, query_rows, latent_rows):
+        both = jnp.concatenate([query_rows, latent_rows], axis=1)
+        place_of = pl.ds(picks_ref[number], 1)
+        whole_out[place_of, start : start + half] = both[None]
+        part_out[place_of, start : start + half] = dot_nt(both, weight[...]).astype(BF16)[None]
+
+    for number in range(3):
+        for start in (0, half):
+            rows = slice(start, start + half)
+            write(number, start, query[number][rows], latent[number][rows])
+    write(3, 0, query[3][...], latent[3][...])
+    write(3, half, query[4][...], latent[4][...])
+
+
+def norm_products(query, latent, weight, picks):
+    rows = query[0].shape[0]
+    width = weight.shape[1]
+    vmem = pl.BlockSpec(memory_space=pltpu.VMEM)
+    return pl.pallas_call(
+        norm_products_kernel,
+        in_specs=[pl.BlockSpec(memory_space=pltpu.SMEM)] + [vmem] * 11,
+        out_specs=[vmem, vmem],
+        out_shape=[
+            jax.ShapeDtypeStruct((4, rows, width), BF16),
+            jax.ShapeDtypeStruct((4, rows, weight.shape[0]), BF16),
+        ],
+        compiler_params=params(),
+        cost_estimate=cost(8),
+        name="norm_products",
+    )(picks, *query, *latent, weight)
 
 
 def norm_backward(value, scale, gain, grad_norm, row_total, width):
@@ -1141,7 +1371,7 @@
     column_parts = lax.axis_size("gy")
     here_x = lax.axis_index("gx")
     here_y = lax.axis_index("gy")
-    local_rows = hidden_in.shape[0]
+    local_rows, local_width = hidden_in.shape
     all_tokens = local_rows * column_parts
     band_rows = all_tokens // row_parts
     head_width = query_weight.shape[1]
@@ -1154,19 +1384,23 @@
     quarter_blocks = blocks // row_parts
     quarter_slots = quarter_blocks * cap
     on_square = square()
-
+    if on_square:
+        order_of = numbers(here_x, here_x ^ 1, here_x ^ 2, here_x ^ 3)
+    else:
+        order_of = jnp.arange(row_parts, dtype=jnp.int32)
+
+    waited.clear()
     hidden_all = spread_rows(hidden_in)
     hidden = hidden_in.astype(F32)
     grad_top = grad_out.astype(F32)
     wide = up_to(shared_width)
-    shared_weight = jnp.concatenate(
-        [widen(shared_gate, wide), widen(shared_up, wide), widen(shared_down.T, wide)], axis=1
-    )
+    shared_weight = side_by_side(shared_gate, shared_up, shared_down, wide)
     scale_one = lax.rsqrt(feature_total(jnp.sum(hidden * hidden, axis=1)) / D + EPS)
-    grad_top_tokens = to_tokens(after(grad_out, scale_one))
-    shared_weight = collect_rows(after(shared_weight, scale_one))
     sent = jnp.concatenate([expert_routes.T.astype(F32), scale_one[None]], axis=0)
-    gathered = lax.all_gather(sent, "gy", axis=1, tiled=True)
+    gathered = jnp.broadcast_to(sent[None], (column_parts,) + sent.shape)
+    gathered = lax.all_to_all(gathered, "gy", split_axis=0, concat_axis=0, tiled=True)
+    grad_top_tokens = to_tokens(after(grad_out, gathered))
+    gathered = gathered.transpose(1, 0, 2).reshape(TOPK + 1, all_tokens)
     routes_all = gathered[:TOPK].astype(jnp.int32)
     scale_one_all = gathered[TOPK]
     mine = here_y * experts_here + jnp.arange(experts_here, dtype=jnp.int32)
@@ -1180,9 +1414,6 @@
     code_here = pick(code.reshape(row_parts, quarter_blocks, local_rows, experts_here), here_x, 0)
     spots = jnp.arange(cap, dtype=jnp.int32).astype(F32)
     at_slot = code_here[:, :, :, None] == spots
-    hidden_all = after(hidden_all, chosen, grad_top_tokens)
-
-    norm_one_all = (hidden_all.astype(F32) * scale_one_all[:, None] * attention_gain).astype(BF16)
     by_head = query_weight.reshape(-1, heads_here, DN + DR)
     used = head_width + latent_width
     in_weight = jnp.concatenate(
@@ -1193,45 +1424,61 @@
         ],
         axis=1,
     )
-    projected = band_total(norm_one_all, in_weight, 1)
-    latent_part = projected[:, head_width:used].astype(BF16)
+    cosine, sine = rope_tables(SEQ_LEN)
+    if on_square:
+        shared_weight = after(shared_weight, gathered)
+        shared_x, shared_y = swap(shared_weight, 1), swap(shared_weight, 2)
+        hidden_all, shared_x, shared_y, chosen = together(hidden_all, shared_x, shared_y, chosen)
+    hidden_all, in_weight, cosine, sine = together(hidden_all, in_weight, cosine, sine)
+
+    gained_one_all = (hidden_all.astype(F32) * attention_gain).astype(BF16)
+    projected = band_total(gained_one_all, in_weight, 1)
+    band_one = pick(scale_one_all.reshape(row_parts, band_rows), here_x, 0)[:, None]
+    grad_top_all = spread_rows(after(grad_out, hidden_all))
+    latent_part = (projected[:, head_width:used] * band_one).astype(BF16)
+    latent_part = after(latent_part, grad_top_all)
     latent_all = lax.all_gather(latent_part, "gy", axis=1, tiled=True)
 
-    grad_top_all = spread_rows(after(grad_out, hidden_all))
-    grad_rows = dispatch(after(chosen, latent_part), grad_top_all, cap, blocks)
+
+    if on_square:
+        middle = shared_weight.shape[0] // 2
+        shared_x, shared_y = after((shared_x, shared_y), latent_part)
+        far = swap(shared_y[:middle], 1), swap(shared_x[middle:], 2)
+    else:
+        weights_of_shared = (lax.all_gather(shared_weight, "gx", axis=0, tiled=True),)
+    grad_top_band = spread_rows(after(grad_top_tokens, latent_all))
+
+    attended, logs, query_seq, key_seq, value_seq, latent_norm = attention_forward(
+        piece_starts, projected, band_one, latent_all, latent_gain, expand_weight, cosine, sine, heads_here
+    )
+    if on_square:
+        attended, *far = together(attended, *far)
+        weights_of_shared = (shared_weight, shared_x, shared_y, *far)
+    grad_rows = dispatch(after(chosen, attended), grad_top_all, cap, blocks)
     grad_rows = grad_rows.reshape(experts_here, row_parts, quarter_slots, -1)
+    attended_all = after(collect_rows(attended), grad_rows)
+    attention_part = dot(attended_all, output_weight).astype(BF16)
+    after_attention = hidden + outer_total(attention_part).astype(F32)
 
     if on_square:
-        late = experts_here - 2
-        grad_hidden_pre = [square_sum(grad_rows, down_weight, 0, 2, 2, True, False, BF16)]
-        latent_all = after(latent_all, grad_hidden_pre[0])
-    grad_top_band = spread_rows(after(grad_top_tokens, latent_all))
-
-    cosine, sine = rope_tables(SEQ_LEN)
-    attended, logs, query_seq, key_seq, value_seq, latent_norm = attention_forward(
-        piece_starts, projected, latent_all, latent_gain, expand_weight, cosine, sine, heads_here
-    )
-    attended_all = collect_rows(attended)
-    attended_all = after(attended_all, shared_weight)
-    attention_part = dot(attended_all, output_weight).astype(BF16)
-    after_attention = hidden + outer_total(attention_part)
-
-    if on_square:
-        rows = after(grad_rows, attention_part)
-        grad_hidden_pre.append(square_sum(rows, down_weight, 2, late - 2, 3, True, False, BF16))
-        after_attention, rows = lax.optimization_barrier((after_attention, rows, grad_hidden_pre[1]))[:2]
-        last_steps = halves(late, 2)
-        last_sent = [
-            group(rows, away, 2, (down_weight,), start, half, True)
-            for start, half, bit, away, _, _ in last_steps
-        ]
-        last_ones = [swap(value, step[2]) for value, step in zip(last_sent, last_steps)]
+        half = experts_here // 2
+        rows = after(grad_rows, attention_part, grad_top_band)
+        grad_hidden_low = square_sum(rows, down_weight, 0, half, 2, True, False, BF16)
+        after_attention = after(after_attention, grad_hidden_low)
 
     gained = (after_attention * ffn_gain).astype(BF16)
     gained_all = spread_rows(gained)
+    gained_tokens = to_tokens(gained)
+    gained_band = spread_rows(gained_tokens)
     squares = jnp.sum(after_attention * after_attention, axis=1, keepdims=True)
-    logits = dot(after(gained, squares), router_weight)
-    totals = square_total(widen(jnp.concatenate([logits, squares], axis=1), 128))
+    logits = dot(gained, router_weight)
+    totals = widen(jnp.concatenate([logits, squares], axis=1), 128)
+    if on_square:
+        norm_one_all = hidden_all.astype(F32) * scale_one_all[:, None] * attention_gain
+        norm_one_all = after(norm_one_all.astype(BF16), totals)
+        rows, norm_one_all = together(after(grad_rows, totals), norm_one_all)
+        grad_hidden_high = square_sum(rows, down_weight, half, half, 3, True, False, BF16)
+    totals = square_total(totals)
     scale_two = lax.rsqrt(totals[:, EXPERTS] / D + EPS)
     probs = jax.nn.softmax(totals[:, :EXPERTS] * scale_two[:, None], axis=-1)
     norm_two = (after_attention * scale_two[:, None] * ffn_gain).astype(BF16)
@@ -1254,35 +1501,29 @@
         ],
         axis=2,
     )
-    norm_two_tokens = to_tokens(norm_two)
     if on_square:
-        rows = after(grad_rows, factors)
-        last_twos = [
-            swap(group(rows, second, 1, (down_weight,), start, half, True, (one,)), 3 - bit)
-            for (start, half, bit, _, second, _), one in zip(last_steps, last_ones)
-        ]
-        gained_all = after(gained_all, norm_two_tokens)
-    rows_two = dispatch(chosen, gained_all, cap, blocks)
+        gained_all, factors = lax.optimization_barrier((gained_all, factors, grad_hidden_high))[:2]
+    rows_two, slot_scale = dispatch(chosen, gained_all, cap, blocks, scale_two_all[:, None])
     rows_two = rows_two.reshape(experts_here, row_parts, quarter_slots, -1)
-    norm_two_band = spread_rows(after(norm_two_tokens, gained_all))
+    slot_scale = slot_scale.reshape(experts_here, row_parts, quarter_slots, 1)
+
+    band_scale = scale_two_all.reshape(blocks, row_parts, -1)
+    band_scale = pick(band_scale, here_x, 1).reshape(-1, 1)
+    shared_hidden, grad_shared_both, grad_shared_part, shared_part = shared_experts(
+        after(gained_band, rows_two), band_scale, grad_top_band, weights_of_shared, order_of
+    )
+    grad_norm_shared = outer_total(grad_shared_part)
+    shared_out = outer_total(shared_part)
 
     both_weights = (gate_weight, up_weight)
     if on_square:
-        rows = after(grad_rows, rows_two)
-        grad_hidden_pre += [
-            group(rows, third, 1, (down_weight,), start, half, True, (one, two)).reshape(1, quarter_slots, -1)
-            for (start, half, _, _, _, third), one, two in zip(last_steps, last_ones, last_twos)
-        ]
-        grad_hidden_pre = jnp.concatenate(grad_hidden_pre, axis=0)
-        order_of = numbers(here_x, here_x ^ 1, here_x ^ 2, here_x ^ 3)
         own, from_x, from_y, across, scaled, back_rows, slot_grad = routed_experts(
-            rows_two, gate_weight, up_weight, grad_hidden_pre, factors
+            after(rows_two, shared_part), gate_weight, up_weight, grad_hidden_low, grad_hidden_high, factors
         )
         whole = [(own, 0), (from_x, 0), (from_y, 0), (across, 0)]
         grad_groups = [(0, experts_here, whole)]
     else:
-        everything = jnp.arange(row_parts, dtype=jnp.int32)
-        order_of = everything
+        everything = order_of
 
         def whole_total(rows, weight, transposed):
             out = group(rows, everything, row_parts, (weight,), 0, experts_here, transposed)
@@ -1305,29 +1546,16 @@
         back_rows = back(grad_groups, order_of, both_weights, True)
 
     back_rows = back_rows.reshape(experts_here, blocks * cap, -1)
-    grad_norm_part = combine(chosen, [back_rows], cap, blocks)
+    grad_norm_part = combine(after(chosen, shared_out), [back_rows], cap, blocks)
     grad_norm_routed = outer_total(grad_norm_part)
 
-    shared_gate_all = shared_weight[:, :wide]
-    shared_up_all = shared_weight[:, wide : 2 * wide]
-    shared_down_all = shared_weight[:, 2 * wide :]
-    norm_two_band = after(norm_two_band, grad_norm_part)
-    shared_gate_pre = dot(norm_two_band, shared_gate_all)
-    shared_up_pre = dot(norm_two_band, shared_up_all)
-    shared_hidden = (silu(shared_gate_pre) * shared_up_pre).astype(BF16)
-    grad_shared_hidden = dot(grad_top_band, shared_down_all)
-    grad_shared_gate_pre = (
-        grad_shared_hidden * shared_up_pre * silu_grad(shared_gate_pre)
-    ).astype(BF16)
-    grad_shared_up_pre = (grad_shared_hidden * silu(shared_gate_pre)).astype(BF16)
-    grad_shared_both = jnp.concatenate([grad_shared_gate_pre, grad_shared_up_pre], axis=1)
-    grad_shared_part = dot_nt(grad_shared_both, shared_weight[:, : 2 * wide]).astype(BF16)
-    grad_norm_shared = outer_total(grad_shared_part)
-    grad_shared = dot_tn(after(norm_two_band, grad_shared_part), grad_shared_both).astype(BF16)
-    grad_shared = lax.psum_scatter(
-        after(grad_shared, grad_norm_shared), "gx", scatter_dimension=0, tiled=True
-    ).astype(F32)
-
+    both_shared = after(jnp.stack([grad_norm_shared, shared_out]), grad_norm_part)
+    both_shared = lax.all_to_all(both_shared, "gx", split_axis=2, concat_axis=1, tiled=True)
+    grad_norm_shared, shared_out = both_shared[0].astype(F32), both_shared[1].astype(F32)
+    if on_square:
+        scaled = after(scaled, grad_norm_shared)
+        low, high = scaled[:half], scaled[half:]
+        low_x, low_y, high_x, high_y = swap(low, 1), swap(low, 2), swap(high, 1), swap(high, 2)
     slot_grad = after(slot_grad, grad_norm_part)
     slot_grad = slot_grad.reshape(experts_here, quarter_blocks, cap).transpose(1, 0, 2)
     grad_probs = jnp.sum(jnp.where(at_slot, slot_grad[:, None], 0.0), axis=3)
@@ -1339,20 +1567,20 @@
     grad_logits = (probs * (grad_probs - centre)).astype(BF16)
     grad_norm_router = dot_nt(grad_logits, router_weight)
     grad_router_part = dot_tn(norm_two, grad_logits)
-    waits = [grad_norm_router]
-    if on_square:
-        half = experts_here // 2
-        hidden_x, hidden_y, hidden_d, out_low = hidden_products(
-            after(scaled, grad_shared_part), down_weight, 0, half, 4
-        )
-        hidden_groups = [(0, half, [(scaled, 0), (hidden_x, 0), (hidden_y, 0), (hidden_d, 0)])]
-        waits.append(out_low)
-    grad_norm_shared = to_features(grad_norm_shared.astype(BF16)).astype(F32)
-    grad_norm_routed = after(grad_norm_routed, *waits)
-    grad_norm_two = grad_norm_routed + grad_norm_shared + grad_norm_router
+    grad_shared = shared_weights(
+        after(gained_band, grad_norm_shared), grad_shared_both, grad_top_band, shared_hidden
+    )
+    grad_norm_routed, grad_norm_router, grad_shared = lax.optimization_barrier(
+        (grad_norm_routed, grad_norm_router, grad_shared)
+    )
+    grad_norm_two = grad_norm_routed.astype(F32) + grad_norm_shared + grad_norm_router
 
     scaled_after = after_attention * ffn_gain
-    row_two = feature_total(jnp.sum(scaled_after * grad_norm_two, axis=1))
+    row_two = jnp.sum(scaled_after * grad_norm_two, axis=1)
+    if on_square and local_rows == 512:
+        row_two = small_totals(jnp.pad(row_two.reshape(4, 128), ((0, 4), (0, 0))), None, 4)[0][:4].reshape(-1)
+    else:
+        row_two = feature_total(row_two)
     grad_after = grad_top + norm_backward(
         after_attention, scale_two, ffn_gain, grad_norm_two, row_two, D
     )
@@ -1360,58 +1588,90 @@
     grad_after_sent = grad_after.astype(BF16)
     grad_after_all = spread_rows(grad_after_sent)
 
+    grad_router = tower_step(after(grad_router_part, grad_after_sent), 0)
+    grad_after_all, grad_router = together(grad_after_all, grad_router)
+    waiting = after(rows_two, grad_after_sent)
+    grad_gate, grad_up = weight_grad(waiting, grad_groups, order_of, False, slot_scale)
+    grad_after_all, grad_gate, grad_up = lax.optimization_barrier(
+        (grad_after_all, grad_gate, grad_up)
+    )
     if on_square:
-        hidden_x, hidden_y, hidden_d, out_high = hidden_products(
-            after(scaled, grad_after_sent), down_weight, half, half, 5
+        grad_after_all, low_x, low_y, high_x, high_y = together(
+            grad_after_all, low_x, low_y, high_x, high_y
         )
-        hidden_groups.append((half, half, [(scaled, half), (hidden_x, 0), (hidden_y, 0), (hidden_d, 0)]))
-        out = [out_low, out_high]
-        grad_after_all = after(grad_after_all, out_high)
-    else:
-        out = [back(hidden_groups, order_of, (down_weight,), False)]
-    out = [value.reshape(value.shape[0], blocks * cap, -1) for value in out]
-
-    grad_attended = band_total(grad_after_all, output_weight, 6, True).astype(BF16)
-    shared_hidden_all = collect(after(shared_hidden, grad_attended)).reshape(row_parts, blocks, -1, wide)
-    shared_hidden_all = shared_hidden_all.transpose(1, 0, 2, 3).reshape(all_tokens, wide)
-    shared_down_wide = jnp.pad(shared_down, ((0, wide - shared_width), (0, 0)))
-    shared_out = dot(shared_hidden_all, shared_down_wide).astype(BF16)
-    routed_part = combine(chosen, out, cap, blocks, (shared_out,))
-    routed = outer_total(routed_part)
-    mixed = (after_attention + routed).astype(BF16)
+
+    grad_attended = band_total(grad_after_all, output_weight, 6, True, BF16)
+    if on_square:
+        low_y, high_x = after((low_y, high_x), grad_attended)
+        low_far, high_far = swap(low_y, 1), swap(high_x, 2)
+        hidden_groups = [
+            (0, half, [(low, 0), (low_x, 0), (low_y, 0), (low_far, 0)]),
+            (half, half, [(high, 0), (high_x, 0), (high_y, 0), (high_far, 0)]),
+        ]
     grad_query_pre, grad_expanded, latent_grads = attention_backward(
         piece_starts, query_seq, key_seq, value_seq, logs, grad_attended, expand_weight, cosine, sine
     )
-    latent_sums = lax.psum(latent_grads, "gy").astype(F32)
-    norm_two_all = (gained_all.astype(F32) * scale_two_all[:, None]).astype(BF16)
-    rows_norm = dispatch(after(chosen, latent_grads), norm_two_all, cap, blocks)
-    rows_norm = rows_norm.reshape(experts_here, row_parts, quarter_slots, -1)
-    grad_gate, grad_up = weight_grad(rows_norm, grad_groups, order_of, False)
-    latent_grads = after(latent_sums, grad_gate, grad_up)
-    grad_query_all = collect_rows(grad_query_pre)
-    latent_f32 = latent_all.astype(F32)
+    own_rows = band_rows // column_parts
+    latent_sums = outer_total(latent_grads).astype(F32)
+    grad_router = tower_step(after(grad_router, latent_grads), 1)
+    expand_part = dot_tn(latent_norm, grad_expanded).astype(BF16)
+    if on_square:
+        expand_away = swap(expand_part, 1)
+
+    if on_square:
+        query_x, query_y = swap(grad_query_pre, 1), swap(grad_query_pre, 2)
+    waiting = after(down_weight, latent_grads)
+    out = back(hidden_groups, order_of, (waiting,), False)
+    if on_square:
+        out, query_x, query_y = together(out, query_x, query_y)
+        middle = band_rows // 2
+        far = swap(query_y[:middle], 1), swap(query_x[middle:], 2)
+        query_blocks = (grad_query_pre, query_x, query_y, *far)
+    out = out.reshape(experts_here, blocks * cap, -1)
+    routed_part = combine(chosen, [out], cap, blocks)
+    if on_square:
+        routed_part, expand_away = together(routed_part, expand_away)
+        expand_x = expand_part + expand_away
+    routed_part, grad_router = together(routed_part, grad_router)
+    latent_sums, routed_part = together(latent_sums, routed_part)
+    routed = outer_total(routed_part)
+    latent_f32 = lax.dynamic_slice_in_dim(latent_all, here_y * own_rows, own_rows, 0).astype(F32)
     compressed = latent_f32[:, :L]
     latent_scale = lax.rsqrt(jnp.mean(compressed * compressed, axis=1) + EPS)
-    grad_latent_norm, grad_rope_key = latent_grads[:, :L], latent_grads[:, L:]
+    grad_latent_norm, grad_rope_key = latent_sums[:, :L], latent_sums[:, L:]
     latent_row = jnp.sum(compressed * latent_gain * grad_latent_norm, axis=1)
     grad_compressed = norm_backward(
         compressed, latent_scale, latent_gain, grad_latent_norm, latent_row, L
     )
     grad_gain_part = jnp.sum(grad_latent_norm * compressed * latent_scale[:, None], axis=0)
-    grad_latent_pre = jnp.concatenate([grad_compressed, grad_rope_key], axis=1)
-    grad_latent_own = lax.dynamic_slice_in_dim(
-        grad_latent_pre, here_y * latent_width, latent_width, 1
-    ).astype(BF16)
+    grad_latent_pre = jnp.concatenate([grad_compressed, grad_rope_key], axis=1).astype(BF16)
+    grad_latent_own = grad_latent_pre.reshape(own_rows, column_parts, latent_width).transpose(1, 0, 2)
+    grad_latent_own = lax.all_to_all(grad_latent_own, "gy", split_axis=0, concat_axis=0, tiled=True)
+    if on_square:
+        expand_y = swap(after(expand_x, grad_latent_pre), 2)
+        grad_latent_own, expand_y = together(grad_latent_own, expand_y)
+    grad_latent_own = grad_latent_own.reshape(band_rows, latent_width)
     grad_latent_own = widen(grad_latent_own, up_to(used) - head_width)
-    grad_latent_all = collect_rows(grad_latent_own)
-    grad_norm_part = (
-        dot_nt(grad_query_all, in_weight[:, :head_width])
-        + dot_nt(grad_latent_all, in_weight[:, head_width:])
-    ).astype(BF16)
-    grad_norm_one = outer_total(grad_norm_part)
-
+    if on_square:
+        latent_blocks = (grad_latent_own, *from_others(grad_latent_own))
+        grad_projected_all, grad_norm_part = norm_products(
+            query_blocks, latent_blocks, in_weight, order_of
+        )
+        grad_projected_all = grad_projected_all.reshape(all_tokens, -1)
+        grad_norm_part = grad_norm_part.reshape(all_tokens, -1)
+    else:
+        grad_projected = jnp.concatenate([grad_query_pre, grad_latent_own], axis=1)
+        grad_projected_all = collect_rows(grad_projected)
+        grad_norm_part = dot_nt(grad_projected_all, in_weight).astype(BF16)
+    grad_norm_one = outer_total(grad_norm_part).astype(F32)
+
+    mixed = (after_attention + routed.astype(F32) + shared_out).astype(BF16)
+    if not on_square:
+        norm_one_all = hidden_all.astype(F32) * scale_one_all[:, None] * attention_gain
+        norm_one_all = norm_one_all.astype(BF16)
     norm_one_all = after(norm_one_all, grad_norm_part)
-    grad_query = dot_tn(norm_one_all, grad_query_all)
+    grad_projected = dot_tn(norm_one_all, grad_projected_all)
+    grad_query = grad_projected[:, :head_width]
     grad_query = jnp.concatenate(
         [
             grad_query[:, : heads_here * DN].reshape(-1, heads_here, DN),
@@ -1419,45 +1679,41 @@
         ],
         axis=2,
     ).reshape(-1, head_width)
-    grad_latent = dot_tn(norm_one_all, grad_latent_all)[:, :latent_width]
+    grad_latent = grad_projected[:, head_width:used]
     grad_output = dot_tn(attended_all, after(grad_after_all, grad_norm_part))
+    if on_square:
+        grad_expand = expand_x.astype(F32) + expand_y.astype(F32)
+    else:
+        grad_expand = lax.psum(expand_part, "gx").astype(F32)
+    grad_router = tower_step(tower_step(after(grad_router, grad_norm_part), 2), 3)
+    grad_shared = inner_rows(after(grad_shared, grad_norm_part))
     (grad_down,) = weight_grad(after(grad_rows, grad_norm_part), hidden_groups, order_of, True)
-    grad_expand = square_total(dot_tn(latent_norm, grad_expanded).astype(BF16)).astype(F32)
-    grad_shared_down = dot_tn(shared_hidden_all, grad_top_all)[:shared_width]
-    pieces = grad_router_part.reshape(column_parts, -1, EXPERTS)
-    pieces = lax.all_to_all(pieces, "gy", split_axis=0, concat_axis=0, tiled=True)
-    grad_router = lax.all_gather(jnp.sum(pieces, axis=0), "gy", axis=0, tiled=True)
-    (
-        grad_norm_one,
-        grad_query,
-        grad_latent,
-        grad_output,
-        grad_down,
-        grad_expand,
-        grad_router,
-        grad_shared_down,
-    ) = lax.optimization_barrier(
-        (
-            grad_norm_one,
-            grad_query,
-            grad_latent,
-            grad_output,
-            grad_down,
-            grad_expand,
-            grad_router,
-            grad_shared_down,
+    grad_norm_one, grad_query, grad_latent, grad_output, grad_expand, grad_down = together(
+        grad_norm_one, grad_query, grad_latent, grad_output, grad_expand, grad_down
+    )
+    row_one = jnp.sum(hidden * attention_gain * grad_norm_one, axis=1)
+    grad_attention_part = jnp.sum(grad_norm_one * hidden * scale_one[:, None], axis=0)
+    if on_square and local_rows == 512 and local_width == 512:
+        inner = jnp.concatenate([row_one, grad_gain_part]).reshape(8, 128)
+        outer = jnp.concatenate([grad_attention_part, grad_ffn_part]).reshape(8, 128)
+        inner, outer = small_totals(inner, outer, 5)
+        row_one = inner[:4].reshape(-1)
+        grad_attention_gain = outer[:4].reshape(-1)
+        grad_ffn_gain = outer[4:8].reshape(-1)
+        grad_latent_gain = outer[12:].reshape(-1)
+    else:
+        row_one, grad_latent_gain = feature_total((row_one, grad_gain_part))
+        grad_attention_gain, grad_ffn_gain, grad_latent_gain = lax.psum(
+            (grad_attention_part, grad_ffn_part, grad_latent_gain), "gy"
         )
-    )
-    row_one, grad_latent_gain = feature_total(
-        (jnp.sum(hidden * attention_gain * grad_norm_one, axis=1), grad_gain_part)
-    )
     grad_hidden = grad_after + norm_backward(
         hidden, scale_one, attention_gain, grad_norm_one, row_one, D
     )
-    grad_attention_part = jnp.sum(grad_norm_one * hidden * scale_one[:, None], axis=0)
-    grad_attention_gain, grad_ffn_gain = lax.psum((grad_attention_part, grad_ffn_part), "gy")
-    grad_shared_gate = grad_shared[:, :shared_width]
-    grad_shared_up = grad_shared[:, wide : wide + shared_width]
+    grad_shared_gate, grad_shared_up, grad_shared_down = shared_sums(
+        after(grad_shared, row_one), shared_width
+    )
+    grad_shared_gate, grad_shared_up = grad_shared_gate.T, grad_shared_up.T
+    grad_latent_gain = settle(grad_latent_gain)
     return (
         mixed,
         grad_hidden,

time: 1340 us -> 1130 us (0.84)
  blocking collectives: 98.4 us -> 35.1 us
  matrix products: 62.3 us -> 17.6 us
  Pallas kernels: 799 us -> 763 us
  local copies, waits for them, and re-layouts: 74.3 us -> 45.6 us
  waiting for transfers between devices: 161 us -> 143 us
  other arithmetic: 60.8 us -> 43.3 us
    pallas_call x11, Pallas kernels: 155 us -> 98.5 us  [the longest x2 19.7 us: dispatch(): pl.pallas_call(dispatch_kernel if scale is None else dispatch_scaled_kern...]
    all_gather x2 -> x0, blocking collectives: 31.4 us -> none  [the longest x1 16.7 us: per_device(): lax.all_gather(jnp.sum(pieces, axis=0), 'gy', axis=0, tiled=True)]
    all_gather x6, waiting for transfers between devices: 37.7 us -> 10.5 us  [spread_rows(): return lax.all_gather(value, 'gy', axis=0, tiled=True)]
    all_to_all x3 -> x5, waiting for transfers between devices: 1.38 us -> 25.3 us  [the longest x1 12.1 us: per_device(): lax.all_to_all(both_shared, 'gx', split_axis=2, concat_axis=1, tiled=True)]
    pallas_call x4, Pallas kernels: 155 us -> 177 us  [square_sum(): pl.pallas_call(functools.partial(sum_kernel, base, by_quarter, own_weight...]
    dot_general x6 -> x2, matrix products: 23.9 us -> 3.45 us  [dot(): return jnp.dot(a, b, preferred_element_type=F32)]
    psum x3 -> x1, blocking collectives: 29.8 us -> 11.4 us  [feature_total(): return lax.psum(value, 'gx')]
    dot_general x4 -> x1, matrix products: 15 us -> 0.27 us  [dot_nt(): lax.dot_general(a, b, (((1,), (1,)), ((), ())), preferred_element_type=F32)]
  transfers between devices with their start and end apart: 50 -> 53, of which waited for: 24 -> 27; matrix products, arithmetic and copies ran while one was open for 12% -> 8% of each run, Pallas kernels for 58% -> 63%
where the time goes in v2:
time: 1130 us; the launch traced here: 1120 us
  Pallas kernels  763 us (68%)
  waiting for transfers between devices  143 us (13%)
  starting transfers between devices  60.9 us (5%)
  local copies, waits for them, and re-layouts  45.6 us (4%)
  other arithmetic  43.3 us (4%)
  blocking collectives  35.1 us (3%)
  matrix products  17.6 us (2%)
  between operations  15.6 us (1%)
    pallas_call x1, Pallas kernels, routed_experts(): pl.pallas_call(experts_kernel, in_specs=[vmem, anywhere, anywhere, vmem,...  388 us
    pallas_call x4, Pallas kernels, square_sum(): pl.pallas_call(functools.partial(sum_kernel, base, by_quarter, own_weight...  177 us
    ppermute x30, waiting for transfers between devices, swap(): return lax.ppermute(value, 'gx', [(i, i ^ bit) for i in range(4)])  81 us
    pallas_call x2, Pallas kernels, weight_grad(): pl.pallas_call(functools.partial(weight_grad_kernel, shapes_of(groups), f...  48.1 us
    ppermute x30, starting transfers between devices, swap(): return lax.ppermute(value, 'gx', [(i, i ^ bit) for i in range(4)])  32.2 us
    all_to_all x2, blocking collectives, to_tokens(): return lax.all_to_all(value, 'gx', split_axis=0, concat_axis=1, tiled=True)  23.7 us
  transfers between devices with their start and end apart: 53, of which 27 were waited for; matrix products, arithmetic and copies ran while one was open for 8% of the time, Pallas kernels for 63%

profile of v2, /device:TPU:0, one launch (start us, length us, event | category | flops | bytes accessed | tf_op | source)
XLA Modules:
  0.0 1123.7 jit_solution(9158244550631908982)
XLA Ops:
  9.2 11.4 %psum.7 = f32[512]{0:T(512)S(1)} all-reduce(f32[512]{0:T(512)S(1)} %fusion.6), channel_id=1, replica_groups=mesh['gx'=4,'gy'=8] {'gx'}, use_global_device_ids=true, to_apply=%region_1.0 | all-reduce | flops 512 | bytes 4096 | tf_op jit(solution)/shard_map/psum | solution.py:111
  43.4 7.0 one_hot.1.chosen_ref
  50.4 15.7 %collective-permute-done.refs_1_ = bf16[512,1152]{1,0:T(8,128)(2,1)} collective-permute-done((bf16[512,1152]{1,0:T(8,128)(2,1)}, bf16[512,1152]{1,0:T(8,128)(2,1)}, u32[]{:S(2)}, u32[]{:S(2)}) %collective-permute-start) | collective-permute-done | bytes 1179680 | tf_op jit(solution)/shard_map/ppermute | solution.py:67
  72.1 41.1 %square_sum.4 = f32[4,256,512]{2,1,0:T(8,128)} custom-call(bf16[4,4,256,512]{3,2,1,0:T(8,128)(2,1)} %bitcast.187, bf16[512,512]{1,0:T(8,128)(2,1)} %fusion.19.weight.refs_10_), custom_call_target="tpu_custom_call" | custom-call | flops 25874999296 | tf_op jit(solution)/shard_map/square_sum/pallas_call | solution.py:738
  115.4 11.8 %all_to_all.88 = bf16[4,128,512]{2,1,0:T(8,128)(2,1)S(1)} all-to-all(bf16[4,128,512]{2,1,0:T(8,128)(2,1)S(1)} %bitcast.183), channel_id=1, replica_groups=mesh['gx'=4,'gy'=8] {'gx'}, dimensions={0} | all-to-all | bytes 1048576 | tf_op jit(solution)/shard_map/all_to_all | solution.py:143
  128.0 10.0 all-gather.12.cloned.1.call-done
  146.7 12.4 %attention.1 = (bf16[1024,256]{1,0:T(8,128)(2,1)}, f32[1,2,1024,1]{3,2,1,0:T(8,128)}, bf16[1,2,1024,192]{3,2,1,0:T(8,128)(2,1)}, bf16[1,2,1024,192]{3,2,1,0:T(8,...) custom-call(s32[1,2]{1,0:T(1,128)} %starts_ref.3, f32[1024,512]{1,0:T(8,128)} %bitcast.219, ...), custom_call_target="tpu_custom_call" | custom-call | flops 6899999744 | tf_op jit(solution)/shard_map/attention/pallas_call | solution.py:1200
  161.3 9.0 dispatch.2
  187.0 57.0 %square_sum.5.grad_low.refs_10_ = bf16[4,128,1408]{2,1,0:T(8,128)(2,1)} custom-call(bf16[8,4,128,512]{3,2,1,0:T(8,128)(2,1)} %bitcast.169, bf16[8,1408,512]{2,1,0:T(8,128)(2,1)} %refs_8_), custom_call_target="tpu_custom_call" | custom-call | flops 31050000384 | tf_op jit(solution)/shard_map/square_sum/pallas_call | solution.py:738
  247.3 12.0 %all_to_all.89 = bf16[4,128,512]{2,1,0:T(8,128)(2,1)S(1)} all-to-all(bf16[4,128,512]{2,1,0:T(8,128)(2,1)} %bitcast.182), channel_id=1, replica_groups=mesh['gx'=4,'gy'=8] {'gx'}, dimensions={0} | all-to-all | bytes 1048576 | tf_op jit(solution)/shard_map/all_to_all | solution.py:143
  281.2 56.2 %square_sum.6.grad_high = bf16[4,128,1408]{2,1,0:T(8,128)(2,1)} custom-call(bf16[8,4,128,512]{3,2,1,0:T(8,128)(2,1)} %bitcast.170, bf16[8,1408,512]{2,1,0:T(8,128)(2,1)} %refs_8_), custom_call_target="tpu_custom_call" | custom-call | flops 31050000384 | tf_op jit(solution)/shard_map/square_sum/pallas_call | solution.py:738
  341.3 10.8 dispatch.3
  352.1 17.1 %shared_experts.1 = (bf16[1024,384]{1,0:T(8,128)(2,1)}, bf16[1024,768]{1,0:T(8,128)(2,1)}, bf16[1024,2048]{1,0:T(8,128)(2,1)}, bf16[1024,2048]{1,0:T(8,128)(2,1)}) custom-call(s32[4]{0:T(128)} %pad_add_fusion.picks_ref, bf16[1024,2048]{1,0:T(8,128)(2,1)} %all-gather.16.cloned.1.call-done.norm, f32[1024,1]{1,0:T(8,128)} %copy.170.scale, ...), custom_call_target="tpu_custom_call" | custom-call | flops 9200000000 | tf_op jit(solution)/shard_map/shared_experts/pallas_call | solution.py:1069
  370.7 387.9 %routed_experts.1 = (bf16[8,2,128,1408]{3,2,1,0:T(8,128)(2,1)}, bf16[8,2,128,1408]{3,2,1,0:T(8,128)(2,1)}, bf16[8,2,128,1408]{3,2,1,0:T(8,128)(2,1)}, bf16[8,2,1...) custom-call(bf16[8,4,128,512]{3,2,1,0:T(8,128)(2,1)} %bitcast.163, ...), custom_call_target="tpu_custom_call" | custom-call | flops 224250003456 | tf_op jit(solution)/shard_map/routed_experts/pallas_call | solution.py:614
  758.7 8.8 combine.2.refs_16_.refs_18_
  787.0 6.0 all-to-all-done.4
  797.9 12.1 %all-to-all-done.5 = bf16[2,128,2048]{1,0,2:T(2,128)(2,1)S(1)} async-done(((bf16[2,128,2048]{1,0,2:T(2,128)(2,1)}), bf16[2,128,2048]{1,0,2:T(2,128)(2,1)S(1)}, u32[]{:S(2)}, u32[]{:S(2)}) %all-to-all-start.5) | async-done | bytes 1048608 | tf_op jit(solution)/shard_map/all_to_all | solution.py:1553
  812.1 11.9 %shared_weights.1 = bf16[2048,1152]{1,0:T(8,128)(2,1)} custom-call(bf16[1024,2048]{1,0:T(8,128)(2,1)} %all-gather.16.cloned.1.call-done.norm, bf16[1024,768]{1,0:T(8,128)(2,1)} %get-tuple-element.201.grads, bf16[1024,2048]{1,0:T(8,128)(2,1)} %all-gather.14.cloned.1.call-done.grad.refs_9_, bf16[1024,384]{1,0:T(8,128)(2,1)} %get-tuple-element.202.hidden), custom_call_target="tpu_custom_call" | custom-call | flops 5750000128 | tf_op jit(solution)/shard_map/shared_weights/pallas_call | solution.py:1110
  826.8 6.1 small_totals.2
  842.9 29.0 %weight_grad.2 = (f32[8,512,1408]{2,1,0:T(8,128)}, f32[8,512,1408]{2,1,0:T(8,128)}) custom-call(s32[4]{0:T(128)} %pad_add_fusion.picks_ref, bf16[8,4,128,512]{3,2,1,0:T(8,128)(2,1)} %bitcast.164, bf16[8,4,128,512]{3,2,1,0:T(8,128)(2,1)} %bitcast.165, bf16[8,4,128,512]{3,2,1,0:T(8,128)(2,1)} %bitcast.166, bf16[8,4,128,512]{3,2,1,0:T(8,128)(2,1)} %bitcast.167, ...), custom_call_target="tpu_custom_call" | custom-call | flops 575000000 | tf_op jit(solution)/shard_map/weight_grad/pallas_call | solution.py:994
  872.0 9.1 all-gather.20.cloned.1.call-done
  881.1 20.0 %collective-permute-done.17.refs_5_.refs_9_ = bf16[4,1,128,1408]{3,2,1,0:T(8,128)(2,1)} collective-permute-done((bf16[4,1,128,1408]{3,2,1,0:T(8,128)(2,1)S(1)}, bf16[4,1,128,1408]{3,2,1,0:T(8,128)(2,1)}, u32[]{:S(2)}, u32[]{:S(2)}) %collective-permute-start.17) | collective-permute-done | bytes 1441824 | tf_op jit(solution)/shard_map/ppermute | solution.py:67
  901.8 23.2 %square_sum.7 = bf16[4,256,256]{2,1,0:T(8,128)(2,1)} custom-call(bf16[4,4,256,512]{3,2,1,0:T(8,128)(2,1)} %bitcast.237, bf16[256,512]{1,0:T(8,128)(2,1)} %weight.5), custom_call_target="tpu_custom_call" | custom-call | flops 18400000000 | tf_op jit(solution)/shard_map/square_sum/pallas_call | solution.py:738
  927.0 14.0 %attention_back.1 = (bf16[1024,384]{1,0:T(8,128)(2,1)}, bf16[1024,512]{1,0:T(8,128)(2,1)}, bf16[1024,576]{1,0:T(8,128)(2,1)}) custom-call(s32[1,2]{1,0:T(1,128)} %starts_ref.3, bf16[1,2,1024,192]{3,2,1,0:T(8,128)(2,1)} %get-tuple-element.179.q_ref, bf16[1,2,1024,192]{3,2,1,0:T(8,128)(2,1)} %get-tuple-element.180.k_ref, ...), custom_call_target="tpu_custom_call" | custom-call | flops 8049999872 | tf_op jit(solution)/shard_map/attention_back/pallas_call | solution.py:1275
  949.0 10.8 collective-permute-done.19.refs_3_.refs_7_
  960.9 15.5 %back.1 = bf16[8,4,128,512]{3,2,1,0:T(8,128)(2,1)} custom-call(s32[4]{0:T(128)} %pad_add_fusion.picks_ref, bf16[4,1,128,1408]{3,2,1,0:T(8,128)(2,1)} %get-tuple-element.379.refs_0_.refs_4_, bf16[4,1,128,1408]{3,2,1,0:T(8,128)(2,1)} %collective-permute-done.15.refs_1_.refs_5_, bf16[4,1,128,1408]{3,2,1,0:T(8,128)(2,1)} %collective-permute-done.16.refs_2_.refs_6_, ...), custom_call_target="tpu_custom_call" | custom-call | flops 18400000000 | tf_op jit(solution)/shard_map/back/pallas_call | solution.py:941
  976.3 8.8 combine.3
  1000.5 7.0 all-to-all-done.6
  1027.5 7.9 norm_products.1
  1051.0 19.1 %weight_grad.3 = f32[8,1408,512]{2,1,0:T(8,128)} custom-call(s32[4]{0:T(128)} %pad_add_fusion.picks_ref, bf16[8,4,128,512]{3,2,1,0:T(8,128)(2,1)} %bitcast.171, bf16[8,4,128,512]{3,2,1,0:T(8,128)(2,1)} %bitcast.172, bf16[8,4,128,512]{3,2,1,0:T(8,128)(2,1)} %bitcast.173, bf16[8,4,128,512]{3,2,1,0:T(8,128)(2,1)} %bitcast.174, ...), custom_call_target="tpu_custom_call" | custom-call | flops 575000000 | tf_op jit(solution)/shard_map/weight_grad/pallas_call | solution.py:994
  1077.2 14.4 %reduce-scatter.20.cloned.1.call-done = bf16[512,512]{1,0:T(8,128)(2,1)} async-done(((bf16[4096,512]{1,0:T(8,128)(2,1)}), bf16[512,512]{1,0:T(8,128)(2,1)}) %reduce-scatter.20.cloned.1.call-update) | async-done | bytes 524304 | tf_op jit(solution)/shard_map/reduce_scatter | solution.py:139
  1095.6 12.0 %small_totals.3 = (f32[8,128]{1,0:T(8,128)}, f32[16,128]{1,0:T(8,128)}) custom-call(f32[8,128]{1,0:T(8,128)} %pad_maximum_fusion.6.inner_ref, f32[8,128]{1,0:T(8,128)} %pad_maximum_fusion.7.outer_ref), custom_call_target="tpu_custom_call" | custom-call | flops 3449999872 | tf_op jit(solution)/shard_map/small_totals/pallas_call | solution.py:826
  (381 shorter events, 213.4 us)
Async XLA Ops:
  7.2 59.0 %all-gather.8.cloned.1.call-start = ((), (), s32[]{:S(2)}) async-start(), calls=%async_computation.15 | async-start | bytes 4718592 | tf_op jit(solution)/shard_map/all_gather | solution.py:135
  27.4 87.1 %all-gather.10.cloned.1.call-start = ((), (), s32[]{:S(2)}) async-start(), calls=%async_computation.16 | async-start | bytes 4718592 | tf_op jit(solution)/shard_map/all_gather | solution.py:135
  37.6 28.5 %collective-permute-start = (bf16[512,1152]{1,0:T(8,128)(2,1)}, bf16[512,1152]{1,0:T(8,128)(2,1)}, u32[]{:S(2)}, u32[]{:S(2)}) collective-permute-start(bf16[512,1152]{1,0:T(8,128)(2,1)} %side_by_side.1.refs_0_), channel_id=1, source_target_pairs={{0,8},{8,0},{16,24},{24,16},{1,9},{9,1},{17,25},{25,17},{2,10},{10... | collective-permute-start | bytes 3538952 | tf_op jit(solution)/shard_map/ppermute | solution.py:67
  38.6 27.6 %collective-permute-start.1 = (bf16[512,1152]{1,0:T(8,128)(2,1)}, bf16[512,1152]{1,0:T(8,128)(2,1)}, u32[]{:S(2)}, u32[]{:S(2)}) collective-permute-start(bf16[512,1152]{1,0:T(8,128)(2,1)} %side_by_side.1.refs_0_), channel_id=1, source_target_pairs={{0,16},{8,24},{16,0},{24,8},{1,17},{9,25},{17,1},{25,9},{2,18},{10... | collective-permute-start | bytes 3538952 | tf_op jit(solution)/shard_map/ppermute | solution.py:67
  66.2 71.8 %all-gather.12.cloned.1.call-start = ((), (), s32[]{:S(2)}) async-start(), calls=%async_computation.17 | async-start | bytes 1327104 | tf_op jit(solution)/shard_map/all_gather | solution.py:1440
  115.4 71.7 %all-gather.14.cloned.1.call-start = ((), (), s32[]{:S(2)}) async-start(), calls=%async_computation.19 | async-start | bytes 4718592 | tf_op jit(solution)/shard_map/all_gather | solution.py:135
  138.1 105.9 %reduce-scatter.8.cloned.1.call-start = ((), (), s32[]{:S(2)}) async-start(), calls=%async_computation.18 | async-start | bytes 4718592 | tf_op jit(solution)/shard_map/reduce_scatter | solution.py:139
  141.1 18.0 %collective-permute-start.2 = (bf16[256,1152]{1,0:T(8,128)(2,1)S(1)}, bf16[256,1152]{1,0:T(8,128)(2,1)}, u32[]{:S(2)}, u32[]{:S(2)}) collective-permute-start(bf16[256,1152]{1,0:T(8,128)(2,1)S(1)} %slice.120), channel_id=1, source_target_pairs={{0,8},{8,0},{16,24},{24,16},{1,9},{9,1},{17,25},{25,17},{2,10},{10... | collective-permute-start | bytes 1769480 | tf_op jit(solution)/shard_map/ppermute | solution.py:67
  185.0 156.3 %all-gather.18.cloned.1.call-start = ((), (), s32[]{:S(2)}) async-start(), calls=%async_computation.21 | async-start | bytes 4718592 | tf_op jit(solution)/shard_map/all_gather | solution.py:135
  247.2 104.8 %all-gather.16.cloned.1.call-start = ((), (), s32[]{:S(2)}) async-start(), calls=%async_computation.20 | async-start | bytes 4718592 | tf_op jit(solution)/shard_map/all_gather | solution.py:135
  277.8 59.7 %all-to-all-start.3 = ((f32[8,512,9]{1,2,0:T(8,128)}), f32[8,512,9]{1,2,0:T(8,128)S(1)}, u32[]{:S(2)}, u32[]{:S(2)}) async-start(f32[8,512,9]{1,2,0:T(8,128)} %maximum_bitcast_fusion.1), calls=%async_computation.4 | async-start | bytes 524288 | tf_op jit(solution)/shard_map/all_to_all | solution.py:1492
  281.2 477.5 %reduce-scatter.10.cloned.1.call-start = ((), (), s32[]{:S(2)}) async-start(), calls=%async_computation.22 | async-start | bytes 4718592 | tf_op jit(solution)/shard_map/reduce_scatter | solution.py:139
  369.2 414.6 %reduce-scatter.14.cloned.1.call-start = ((), (), s32[]{:S(2)}) async-start(), calls=%async_computation.24 | async-start | bytes 4718592 | tf_op jit(solution)/shard_map/reduce_scatter | solution.py:139
  370.3 453.7 %reduce-scatter.12.cloned.1.call-start = ((), (), s32[]{:S(2)}) async-start(), calls=%async_computation.23 | async-start | bytes 4718592 | tf_op jit(solution)/shard_map/reduce_scatter | solution.py:139
  793.0 17.1 %all-to-all-start.5 = ((bf16[2,128,2048]{1,0,2:T(2,128)(2,1)}), bf16[2,128,2048]{1,0,2:T(2,128)(2,1)S(1)}, u32[]{:S(2)}, u32[]{:S(2)}) async-start(bf16[2,128,2048]{1,0,2:T(2,128)(2,1)} %copy.175), calls=%async_computation.9 | async-start | bytes 2097152 | tf_op jit(solution)/shard_map/all_to_all | solution.py:1553
  796.5 84.6 %all-gather.20.cloned.1.call-start = ((), (), s32[]{:S(2)}) async-start(), calls=%async_computation.25 | async-start | bytes 4718592 | tf_op jit(solution)/shard_map/all_gather | solution.py:135
  835.2 150.0 %reduce-scatter.16.cloned.1.call-start = ((), (), s32[]{:S(2)}) async-start(), calls=%async_computation.26 | async-start | bytes 1474560 | tf_op jit(solution)/shard_map/reduce_scatter | solution.py:139
  838.5 42.6 %collective-permute-start.15 = (bf16[4,1,128,1408]{3,2,1,0:T(8,128)(2,1)}, bf16[4,1,128,1408]{3,2,1,0:T(8,128)(2,1)}, u32[]{:S(2)}, u32[]{:S(2)}) collective-permute-start(bf16[4,1,128,1408]{3,2,1,0:T(8,128)(2,1)} %get-tuple-element.379.refs_0_.refs_4_), channel_id=1, source_target_pairs={{0,8},{8,0},{16,24},{24,16},{1,9},{9,1},{17,25},{25,17},{2,10},{10... | collective-permute-start | bytes 4325384 | tf_op jit(solution)/shard_map/ppermute | solution.py:67
  839.9 41.2 %collective-permute-start.16 = (bf16[4,1,128,1408]{3,2,1,0:T(8,128)(2,1)}, bf16[4,1,128,1408]{3,2,1,0:T(8,128)(2,1)}, u32[]{:S(2)}, u32[]{:S(2)}) collective-permute-start(bf16[4,1,128,1408]{3,2,1,0:T(8,128)(2,1)} %get-tuple-element.379.refs_0_.refs_4_), channel_id=1, source_target_pairs={{0,16},{8,24},{16,0},{24,8},{1,17},{9,25},{17,1},{25,9},{2,18},{10... | collective-permute-start | bytes 4325384 | tf_op jit(solution)/shard_map/ppermute | solution.py:67
  840.5 60.6 %collective-permute-start.17 = (bf16[4,1,128,1408]{3,2,1,0:T(8,128)(2,1)S(1)}, bf16[4,1,128,1408]{3,2,1,0:T(8,128)(2,1)}, u32[]{:S(2)}, u32[]{:S(2)}) collective-permute-start(bf16[4,1,128,1408]{3,2,1,0:T(8,128)(2,1)S(1)} %get-tuple-element.378.refs_4_.refs_8_), channel_id=1, source_target_pairs={{0,8},{8,0},{16,24},{24,16},{1,9},{9,1},{17,25},{25,17},{2,10},{10... | collective-permute-start | bytes 4325384 | tf_op jit(solution)/shard_map/ppermute | solution.py:67
  842.0 59.8 %collective-permute-start.18 = (bf16[4,1,128,1408]{3,2,1,0:T(8,128)(2,1)S(1)}, bf16[4,1,128,1408]{3,2,1,0:T(8,128)(2,1)}, u32[]{:S(2)}, u32[]{:S(2)}) collective-permute-start(bf16[4,1,128,1408]{3,2,1,0:T(8,128)(2,1)S(1)} %get-tuple-element.378.refs_4_.refs_8_), channel_id=1, source_target_pairs={{0,16},{8,24},{16,0},{24,8},{1,17},{9,25},{17,1},{25,9},{2,18},{10... | collective-permute-start | bytes 4325384 | tf_op jit(solution)/shard_map/ppermute | solution.py:67
  842.9 29.1 %collective-permute-start.14 = (f32[512,64]{0,1:T(8,128)S(1)}, f32[512,64]{0,1:T(8,128)S(1)}, u32[]{:S(2)}, u32[]{:S(2)}) collective-permute-start(f32[512,64]{0,1:T(8,128)S(1)} %fusion.20), channel_id=1, source_target_pairs={{0,1},{1,0},{2,3},{3,2},{4,5},{5,4},{6,7},{7,6},{8,9},{9,8},{10,11... | collective-permute-start | bytes 393224 | tf_op jit(solution)/shard_map/ppermute | solution.py:131
  925.0 34.8 %collective-permute-start.19 = (bf16[4,1,128,1408]{3,2,1,0:T(8,128)(2,1)}, bf16[4,1,128,1408]{3,2,1,0:T(8,128)(2,1)S(1)}, u32[]{:S(2)}, u32[]{:S(2)}) collective-permute-start(bf16[4,1,128,1408]{3,2,1,0:T(8,128)(2,1)} %collective-permute-done.16.refs_2_.refs_6_), channel_id=1, source_target_pairs={{0,8},{8,0},{16,24},{24,16},{1,9},{9,1},{17,25},{25,17},{2,10},{10... | collective-permute-start | bytes 4325384 | tf_op jit(solution)/shard_map/ppermute | solution.py:67
  925.4 34.8 %collective-permute-start.20 = (bf16[4,1,128,1408]{3,2,1,0:T(8,128)(2,1)}, bf16[4,1,128,1408]{3,2,1,0:T(8,128)(2,1)}, u32[]{:S(2)}, u32[]{:S(2)}) collective-permute-start(bf16[4,1,128,1408]{3,2,1,0:T(8,128)(2,1)} %collective-permute-done.17.refs_5_.refs_9_), channel_id=1, source_target_pairs={{0,16},{8,24},{16,0},{24,8},{1,17},{9,25},{17,1},{25,9},{2,18},{10... | collective-permute-start | bytes 4325384 | tf_op jit(solution)/shard_map/ppermute | solution.py:67
  941.0 35.3 %collective-permute-start.21 = (bf16[1024,384]{1,0:T(8,128)(2,1)}, bf16[1024,384]{1,0:T(8,128)(2,1)}, u32[]{:S(2)}, u32[]{:S(2)}) collective-permute-start(bf16[1024,384]{1,0:T(8,128)(2,1)} %get-tuple-element.228.refs_0_), channel_id=1, source_target_pairs={{0,8},{8,0},{16,24},{24,16},{1,9},{9,1},{17,25},{25,17},{2,10},{10... | collective-permute-start | bytes 2359304 | tf_op jit(solution)/shard_map/ppermute | solution.py:67
  941.4 34.9 %collective-permute-start.22 = (bf16[1024,384]{1,0:T(8,128)(2,1)}, bf16[1024,384]{1,0:T(8,128)(2,1)}, u32[]{:S(2)}, u32[]{:S(2)}) collective-permute-start(bf16[1024,384]{1,0:T(8,128)(2,1)} %get-tuple-element.228.refs_0_), channel_id=1, source_target_pairs={{0,16},{8,24},{16,0},{24,8},{1,17},{9,25},{17,1},{25,9},{2,18},{10... | collective-permute-start | bytes 2359304 | tf_op jit(solution)/shard_map/ppermute | solution.py:67
  943.1 132.1 %reduce-scatter.18.cloned.1.call-start = ((), (), s32[]{:S(2)}) async-start(), calls=%async_computation.27 | async-start | bytes 4718592 | tf_op jit(solution)/shard_map/reduce_scatter | solution.py:139
  948.2 37.0 %collective-permute-start.23 = (bf16[512,512]{1,0:T(8,128)(2,1)}, bf16[512,512]{1,0:T(8,128)(2,1)}, u32[]{:S(2)}, u32[]{:S(2)}) collective-permute-start(bf16[512,512]{1,0:T(8,128)(2,1)} %convolution_convert_fusion.1), channel_id=1, source_target_pairs={{0,8},{8,0},{16,24},{24,16},{1,9},{9,1},{17,25},{25,17},{2,10},{10... | collective-permute-start | bytes 1572872 | tf_op jit(solution)/shard_map/ppermute | solution.py:67
  997.6 94.0 %reduce-scatter.20.cloned.1.call-start = ((), (), s32[]{:S(2)}) async-start(), calls=%async_computation.28 | async-start | bytes 4718592 | tf_op jit(solution)/shard_map/reduce_scatter | solution.py:139
  999.4 21.0 %collective-permute-start.25 = (bf16[512,384]{1,0:T(8,128)(2,1)}, bf16[512,384]{1,0:T(8,128)(2,1)}, u32[]{:S(2)}, u32[]{:S(2)}) collective-permute-start(bf16[512,384]{1,0:T(8,128)(2,1)} %slice.136), channel_id=1, source_target_pairs={{0,8},{8,0},{16,24},{24,16},{1,9},{9,1},{17,25},{25,17},{2,10},{10... | collective-permute-start | bytes 1179656 | tf_op jit(solution)/shard_map/ppermute | solution.py:67
  1035.4 74.2 %all-to-all-start.7 = ((bf16[4,512,1152]{2,1,0:T(8,128)(2,1)}), bf16[4,512,1152]{2,1,0:T(8,128)(2,1)}, u32[]{:S(2)}, u32[]{:S(2)}) async-start(bf16[4,512,1152]{2,1,0:T(8,128)(2,1)} %bitcast.184), calls=%async_computation.14 | async-start | bytes 9437184 | tf_op jit(solution)/shard_map/all_to_all | solution.py:124
  1051.0 23.4 %collective-permute-start.32 = (f32[512,64]{0,1:T(8,128)S(1)}, f32[512,64]{0,1:T(8,128)S(1)}, u32[]{:S(2)}, u32[]{:S(2)}) collective-permute-start(f32[512,64]{0,1:T(8,128)S(1)} %add.146), channel_id=1, source_target_pairs={{0,4},{1,5},{2,6},{3,7},{4,0},{5,1},{6,2},{7,3},{8,12},{9,13},{10,... | collective-permute-start | bytes 393224 | tf_op jit(solution)/shard_map/ppermute | solution.py:131
  (81 other events, 1371.0 us)
Sparse Core Ops, SparseCore 0:
  9.6 52.6 all-gather.7
  66.4 47.5 all-gather.9
  116.2 21.8 all-gather.11
  140.1 46.9 all-gather.13
  189.2 48.7 reduce-scatter.7
  247.4 50.5 all-gather.17
  300.1 45.8 all-gather.15
  369.3 50.1 reduce-scatter.9
  422.3 48.1 reduce-scatter.13
  767.6 52.1 reduce-scatter.11
  835.3 45.7 all-gather.19
  943.2 32.4 reduce-scatter.15
  986.3 52.0 reduce-scatter.17
  1040.5 51.0 reduce-scatter.19

commit v3 on v2

--- a/solution.py
+++ b/solution.py
@@ -375,13 +375,18 @@
     grad_low,
     grad_high,
     factors,
+    chosen,
     own_out,
     x_out,
     y_out,
     d_out,
     hid_out,
+    tokens_out,
+    gate_out,
+    hidden_x_out,
+    hidden_y_out,
     back_out,
-    gate_out,
+    chosen_held,
     first_sent,
     first,
     second,
@@ -400,6 +405,11 @@
     own_sem,
     weight_sem,
     load_sem,
+    chosen_sem,
+    hidden_x_send,
+    hidden_x_recv,
+    hidden_y_send,
+    hidden_y_recv,
 ):
     x, y, x_other, y_other = neighbours()
     me = 2 * y + x
@@ -542,6 +552,22 @@
             (x_copy if odd else y_copy)(pair, odd).wait_recv()
             far_copy(pair, odd).start()
 
+        @pl.when(pair == pairs - 1)
+        def _():
+            for odd in range(2):
+                hidden_x_copy(odd).start()
+                hidden_y_copy(odd).start()
+
+    def hidden_x_copy(odd):
+        return remote(
+            hid_out.at[odd], hidden_x_out.at[odd], hidden_x_send.at[odd], hidden_x_recv.at[odd], x_other
+        )
+
+    def hidden_y_copy(odd):
+        return remote(
+            hid_out.at[odd], hidden_y_out.at[odd], hidden_y_send.at[odd], hidden_y_recv.at[odd], y_other
+        )
+
     def load(pair, odd, number):
         expert = 2 * pair + odd
         source = (x_out, y_out, d_out)[number]
@@ -585,7 +611,35 @@
 
         return 0
 
+    experts, quarters = rows.shape[:2]
+    block, cap = chosen_held.shape[1], chosen.shape[1] // experts
+    per_quarter = slots // cap
+    blocks = quarters * per_quarter
+
+    def chosen_copy(number):
+        return pltpu.make_async_copy(
+            chosen.at[pl.ds(number * block, block)], chosen_held.at[number % 2], chosen_sem.at[number % 2]
+        )
+
+    def to_tokens_of(number, _):
+        chosen_copy(number).wait()
+
+        @pl.when(number + 1 < blocks)
+        def _():
+            chosen_copy(number + 1).start()
+
+        spots = pl.ds((number % per_quarter) * cap, cap)
+        pieces = [back_out[expert, number // per_quarter, spots] for expert in range(experts)]
+        total = dot(chosen_held[number % 2], jnp.concatenate(pieces, axis=0))
+        tokens_out[pl.ds(number * block, block)] = total.astype(BF16)
+        return 0
+
+    chosen_copy(0).start()
     lax.fori_loop(0, pairs + 4, step, 0)
+    lax.fori_loop(0, blocks, to_tokens_of, 0)
+    for odd in range(2):
+        hidden_x_copy(odd).wait()
+        hidden_y_copy(odd).wait()
 
     def drain(pair, _):
         for odd in range(2):
@@ -604,7 +658,7 @@
     lax.fori_loop(0, pairs, drain, 0)
 
 
-def routed_experts(rows, w_gate, w_up, grad_low, grad_high, factors):
+def routed_experts(rows, w_gate, w_up, grad_low, grad_high, factors, chosen, blocks):
     experts, quarters, slots, depth = rows.shape
     width = w_gate.shape[2]
     vmem = pl.BlockSpec(memory_space=pltpu.VMEM)
@@ -613,15 +667,19 @@
     dma = pltpu.SemaphoreType.DMA
     return pl.pallas_call(
         experts_kernel,
-        in_specs=[vmem, anywhere, anywhere, vmem, vmem, vmem],
-        out_specs=[anywhere] * 4 + [vmem] * 3,
+        in_specs=[vmem, anywhere, anywhere, vmem, vmem, vmem, anywhere],
+        out_specs=[anywhere] * 4 + [vmem] * 3 + [anywhere] * 2,
         out_shape=[block] * 4
         + [
             jax.ShapeDtypeStruct((experts, 1, slots, width), BF16),
-            jax.ShapeDtypeStruct((experts, quarters, slots, depth), BF16),
+            jax.ShapeDtypeStruct((chosen.shape[0], depth), BF16),
             jax.ShapeDtypeStruct((experts, slots, 1), F32),
+            jax.ShapeDtypeStruct((2, 1, slots, width), BF16),
+            jax.ShapeDtypeStruct((2, 1, slots, width), BF16),
         ],
         scratch_shapes=[
+            pltpu.VMEM((experts, quarters, slots, depth), BF16),
+            pltpu.VMEM((2, chosen.shape[0] // blocks, chosen.shape[1]), BF16),
             pltpu.VMEM((2, 2, 2, 2, slots, width), BF16),
             pltpu.VMEM((experts, 2, 2, slots, width), BF16),
             pltpu.VMEM((experts, 2, slots, width), BF16),
@@ -629,13 +687,14 @@
             pltpu.VMEM((2, 3, 2, slots, width), BF16),
         ]
         + [dma((experts,))] * 11
-        + [dma((2, 2)), dma((2, 3))],
+        + [dma((2, 2)), dma((2, 3))]
+        + [dma((2,))] * 5,
         compiler_params=pltpu.CompilerParams(
             collective_id=0, has_side_effects=True, vmem_limit_bytes=VMEM_LIMIT
         ),
         cost_estimate=cost(390),
         name="routed_experts",
-    )(rows, w_gate, w_up, grad_low, grad_high, factors)
+    )(rows, w_gate, w_up, grad_low, grad_high, factors, chosen)
 
 
 def sum_kernel(base, by_quarter, own_weights, transposed, rows, weight, out, sent, first, second, held, *sems):
@@ -644,7 +703,6 @@
     me = 2 * y + x
     pairs = sent.shape[0] // 2
     slots = sent.shape[2]
-    greet(x_other, y_other)
 
     def side(odd):
         if odd:
@@ -706,6 +764,7 @@
 
     if own_weights:
         lax.fori_loop(0, 2 * pairs, fetch, 0)
+    greet(x_other, y_other)
 
     def step(number, _):
         for lag, stage in enumerate((send_first, send_second, finish)):
@@ -1139,15 +1198,18 @@
     return value * cosine + other * sine
 
 
-def visible(starts_ref, sequence):
-    length = SEQ_LEN
-    query = lax.broadcasted_iota(jnp.int32, (length, 1), 0)
-    key = lax.broadcasted_iota(jnp.int32, (1, length), 1)
-    seen = key <= query
-    for number in range(2):
-        low = starts_ref[sequence, number]
-        seen |= ((query >= low) & (query < low + PIECE)) & ((key >= low) & (key < low + PIECE))
-    return seen
+def query_blocks(starts_ref, sequence):
+    blocks = []
+    for first in range(0, SEQ_LEN, PIECE):
+        keys = min(SEQ_LEN, first + 2 * PIECE)
+        query = first + lax.broadcasted_iota(jnp.int32, (PIECE, 1), 0)
+        key = lax.broadcasted_iota(jnp.int32, (1, keys), 1)
+        seen = key <= query
+        for number in range(2):
+            low = starts_ref[sequence, number]
+            seen |= ((query >= low) & (query < low + PIECE)) & ((key >= low) & (key < low + PIECE))
+        blocks.append((first, keys, seen))
+    return blocks
 
 
 def attention_kernel(heads, starts_ref, proj_ref, rows_scale, latent, gain, w_expand, cos, sin, out, logs, q_out, k_out, v_out, n_out):
@@ -1161,7 +1223,7 @@
     n_out[...] = normed
     key_rope = turn(lat[:, L:], cosine, sine).astype(BF16)
     expanded = dot(normed, w_expand[...]).astype(BF16)
-    seen = visible(starts_ref, pl.program_id(0))
+    blocks = query_blocks(starts_ref, pl.program_id(0))
     for head in range(heads):
         plain = proj[:, head * DN : (head + 1) * DN].astype(BF16)
         start = heads * DN + head * DR
@@ -1172,13 +1234,15 @@
         q_out[0, head] = query
         k_out[0, head] = key
         v_out[0, head] = value
-        scores = jnp.where(seen, dot_nt(query, key) * scale, -1e30)
-        peak = jnp.max(scores, axis=1, keepdims=True)
-        expo = jnp.exp(scores - peak)
-        total = jnp.sum(expo, axis=1, keepdims=True)
-        weights = (expo / total).astype(BF16)
-        out[:, head * DV : (head + 1) * DV] = dot(weights, value).astype(BF16)
-        logs[0, head] = peak + jnp.log(total)
+        for first, keys, seen in blocks:
+            rows = slice(first, first + PIECE)
+            scores = jnp.where(seen, dot_nt(query[rows], key[:keys]) * scale, -1e30)
+            peak = jnp.max(scores, axis=1, keepdims=True)
+            expo = jnp.exp(scores - peak)
+            total = jnp.sum(expo, axis=1, keepdims=True)
+            weights = (expo * (1.0 / total)).astype(BF16)
+            out[rows, head * DV : (head + 1) * DV] = dot(weights, value[:keys]).astype(BF16)
+            logs[0, head, rows] = peak + jnp.log(total)
 
 
 def attention_forward(starts, proj, rows_scale, latent, gain, w_expand, cosine, sine, heads):
@@ -1227,26 +1291,40 @@
     )(starts, proj, rows_scale, latent, gain[None], w_expand, cosine, sine)
 
 
+def longer(total, part):
+    if total is None:
+        return part
+    rows = total.shape[0]
+    if rows == part.shape[0]:
+        return total + part
+    return jnp.concatenate([total + part[:rows], part[rows:]], axis=0)
+
+
 def attention_back_kernel(heads, starts_ref, q_ref, k_ref, v_ref, logs, grad, w_expand, cos, sin, dq_out, de_out, dl_out):
     scale = (DN + DR) ** (-0.5)
     cosine, sine = cos[...], -sin[...]
-    seen = visible(starts_ref, pl.program_id(0))
+    blocks = query_blocks(starts_ref, pl.program_id(0))
     rope = None
     latent = None
     for head in range(heads):
         query, key, value = q_ref[0, head], k_ref[0, head], v_ref[0, head]
         grad_here = grad[:, head * DV : (head + 1) * DV]
-        scores = jnp.where(seen, dot_nt(query, key) * scale, -1e30)
-        weights = jnp.exp(scores - logs[0, head])
-        grad_weights = dot_nt(grad_here, value)
-        centre = jnp.sum(weights * grad_weights, axis=1, keepdims=True)
-        grad_scores = (weights * (grad_weights - centre)).astype(BF16)
-        grad_query = dot(grad_scores, key) * scale
-        grad_key = dot_tn(grad_scores, query) * scale
-        grad_value = dot_tn(weights.astype(BF16), grad_here)
-        dq_out[:, head * DN : (head + 1) * DN] = grad_query[:, :DN].astype(BF16)
-        start = heads * DN + head * DR
-        dq_out[:, start : start + DR] = turn(grad_query[:, DN:], cosine, sine).astype(BF16)
+        grad_key = grad_value = None
+        for first, keys, seen in blocks:
+            rows = slice(first, first + PIECE)
+            scores = jnp.where(seen, dot_nt(query[rows], key[:keys]) * scale, -1e30)
+            weights = jnp.exp(scores - logs[0, head, rows])
+            grad_weights = dot_nt(grad_here[rows], value[:keys])
+            centre = jnp.sum(weights * grad_weights, axis=1, keepdims=True)
+            grad_scores = (weights * (grad_weights - centre)).astype(BF16)
+            grad_query = dot(grad_scores, key[:keys]) * scale
+            dq_out[rows, head * DN : (head + 1) * DN] = grad_query[:, :DN].astype(BF16)
+            start = heads * DN + head * DR
+            turned = turn(grad_query[:, DN:], cosine[rows], sine[rows])
+            dq_out[rows, start : start + DR] = turned.astype(BF16)
+            grad_key = longer(grad_key, dot_tn(grad_scores, query[rows]))
+            grad_value = longer(grad_value, dot_tn(weights.astype(BF16), grad_here[rows]))
+        grad_key = grad_key * scale
         part = turn(grad_key[:, DN:], cosine, sine)
         rope = part if rope is None else rope + part
         both = jnp.concatenate([grad_key[:, :DN].astype(BF16), grad_value.astype(BF16)], axis=1)
@@ -1470,26 +1548,30 @@
     gained_all = spread_rows(gained)
     gained_tokens = to_tokens(gained)
     gained_band = spread_rows(gained_tokens)
-    squares = jnp.sum(after_attention * after_attention, axis=1, keepdims=True)
-    logits = dot(gained, router_weight)
-    totals = widen(jnp.concatenate([logits, squares], axis=1), 128)
+    squares = jnp.sum(after_attention * after_attention, axis=1)[None]
+    logits = lax.dot_general(
+        router_weight, gained, (((0,), (1,)), ((), ())), preferred_element_type=F32
+    )
+    totals = jnp.concatenate([logits, squares, jnp.zeros((7, local_rows), F32)], axis=0)
     if on_square:
         norm_one_all = hidden_all.astype(F32) * scale_one_all[:, None] * attention_gain
         norm_one_all = after(norm_one_all.astype(BF16), totals)
         rows, norm_one_all = together(after(grad_rows, totals), norm_one_all)
         grad_hidden_high = square_sum(rows, down_weight, half, half, 3, True, False, BF16)
     totals = square_total(totals)
-    scale_two = lax.rsqrt(totals[:, EXPERTS] / D + EPS)
-    probs = jax.nn.softmax(totals[:, :EXPERTS] * scale_two[:, None], axis=-1)
+    scale_two = lax.rsqrt(totals[EXPERTS] / D + EPS)
+    probs_across = jax.nn.softmax(totals[:EXPERTS] * scale_two[None], axis=0)
+    probs = probs_across.T
     norm_two = (after_attention * scale_two[:, None] * ffn_gain).astype(BF16)
     sent = jnp.concatenate(
         [
-            probs.reshape(local_rows, column_parts, experts_here),
-            jnp.broadcast_to(scale_two[:, None, None], (local_rows, column_parts, 1)),
+            probs_across.reshape(column_parts, experts_here, local_rows),
+            jnp.broadcast_to(scale_two[None, None], (column_parts, 1, local_rows)),
         ],
-        axis=2,
-    ).transpose(1, 0, 2)
+        axis=1,
+    )
     received = lax.all_to_all(sent, "gy", split_axis=0, concat_axis=0, tiled=True)
+    received = received.transpose(0, 2, 1)
     scale_two_all = received[:, :, experts_here].reshape(all_tokens)
     received = pick(received.reshape(row_parts, quarter_blocks, local_rows, experts_here + 1), here_x, 0)
     factors = jnp.stack(
@@ -1517,8 +1599,8 @@
 
     both_weights = (gate_weight, up_weight)
     if on_square:
-        own, from_x, from_y, across, scaled, back_rows, slot_grad = routed_experts(
-            after(rows_two, shared_part), gate_weight, up_weight, grad_hidden_low, grad_hidden_high, factors
+        own, from_x, from_y, across, scaled, grad_norm_part, slot_grad, pair_x, pair_y = routed_experts(
+            after(rows_two, shared_part), gate_weight, up_weight, grad_hidden_low, grad_hidden_high, factors, chosen, blocks
         )
         whole = [(own, 0), (from_x, 0), (from_y, 0), (across, 0)]
         grad_groups = [(0, experts_here, whole)]
@@ -1544,9 +1626,10 @@
         hidden_groups = [(0, experts_here, [(whole[q], 0) for q in range(row_parts)])]
 
         back_rows = back(grad_groups, order_of, both_weights, True)
-
-    back_rows = back_rows.reshape(experts_here, blocks * cap, -1)
-    grad_norm_part = combine(after(chosen, shared_out), [back_rows], cap, blocks)
+        back_rows = back_rows.reshape(experts_here, blocks * cap, -1)
+        grad_norm_part = combine(chosen, [back_rows], cap, blocks)
+
+    grad_norm_part = after(grad_norm_part, shared_out)
     grad_norm_routed = outer_total(grad_norm_part)
 
     both_shared = after(jnp.stack([grad_norm_shared, shared_out]), grad_norm_part)
@@ -1554,7 +1637,7 @@
     grad_norm_shared, shared_out = both_shared[0].astype(F32), both_shared[1].astype(F32)
     if on_square:
         scaled = after(scaled, grad_norm_shared)
-        low, high = scaled[:half], scaled[half:]
+        low, high = scaled[2:half], scaled[half:]
         low_x, low_y, high_x, high_y = swap(low, 1), swap(low, 2), swap(high, 1), swap(high, 2)
     slot_grad = after(slot_grad, grad_norm_part)
     slot_grad = slot_grad.reshape(experts_here, quarter_blocks, cap).transpose(1, 0, 2)
@@ -1567,12 +1650,7 @@
     grad_logits = (probs * (grad_probs - centre)).astype(BF16)
     grad_norm_router = dot_nt(grad_logits, router_weight)
     grad_router_part = dot_tn(norm_two, grad_logits)
-    grad_shared = shared_weights(
-        after(gained_band, grad_norm_shared), grad_shared_both, grad_top_band, shared_hidden
-    )
-    grad_norm_routed, grad_norm_router, grad_shared = lax.optimization_barrier(
-        (grad_norm_routed, grad_norm_router, grad_shared)
-    )
+    grad_norm_routed, grad_norm_router = together(grad_norm_routed, grad_norm_router)
     grad_norm_two = grad_norm_routed.astype(F32) + grad_norm_shared + grad_norm_router
 
     scaled_after = after_attention * ffn_gain
@@ -1592,8 +1670,11 @@
     grad_after_all, grad_router = together(grad_after_all, grad_router)
     waiting = after(rows_two, grad_after_sent)
     grad_gate, grad_up = weight_grad(waiting, grad_groups, order_of, False, slot_scale)
-    grad_after_all, grad_gate, grad_up = lax.optimization_barrier(
-        (grad_after_all, grad_gate, grad_up)
+    grad_shared = shared_weights(
+        after(gained_band, grad_gate), grad_shared_both, grad_top_band, shared_hidden
+    )
+    grad_after_all, grad_gate, grad_up, grad_shared = together(
+        grad_after_all, grad_gate, grad_up, grad_shared
     )
     if on_square:
         grad_after_all, low_x, low_y, high_x, high_y = together(
@@ -1602,10 +1683,11 @@
 
     grad_attended = band_total(grad_after_all, output_weight, 6, True, BF16)
     if on_square:
-        low_y, high_x = after((low_y, high_x), grad_attended)
-        low_far, high_far = swap(low_y, 1), swap(high_x, 2)
+        pair_far, low_y, high_x = after((pair_y, low_y, high_x), grad_attended)
+        pair_far, low_far, high_far = swap(pair_far, 1), swap(low_y, 1), swap(high_x, 2)
         hidden_groups = [
-            (0, half, [(low, 0), (low_x, 0), (low_y, 0), (low_far, 0)]),
+            (0, 2, [(scaled, 0), (pair_x, 0), (pair_y, 0), (pair_far, 0)]),
+            (2, half - 2, [(low, 0), (low_x, 0), (low_y, 0), (low_far, 0)]),
             (half, half, [(high, 0), (high_x, 0), (high_y, 0), (high_far, 0)]),
         ]
     grad_query_pre, grad_expanded, latent_grads = attention_backward(

time: 1130 us -> 1110 us (0.982)
  waiting for transfers between devices: 143 us -> 118 us
    ppermute x30 -> x31, waiting for transfers between devices: 81 us -> 61.2 us  [swap(): return lax.ppermute(value, 'gx', [(i, i ^ bit) for i in range(4)])]
    pallas_call x1, Pallas kernels: 388 us -> 400 us  [routed_experts(): pl.pallas_call(experts_kernel, in_specs=[vmem, anywhere, anywhere, vmem,...]
    ppermute x30 -> x31, starting transfers between devices: 32.2 us -> 31.9 us  [swap(): return lax.ppermute(value, 'gx', [(i, i ^ bit) for i in range(4)])]
  transfers between devices with their start and end apart: 53 -> 54, of which waited for: 27 -> 27; matrix products, arithmetic and copies ran while one was open for 8% -> 8% of each run, Pallas kernels for 63% -> 64%
where the time goes in v3:
time: 1110 us; the launch traced here: 1100 us
  Pallas kernels  765 us (69%)
  waiting for transfers between devices  118 us (11%)
  starting transfers between devices  59.3 us (5%)
  local copies, waits for them, and re-layouts  51.3 us (5%)
  other arithmetic  39.6 us (4%)
  blocking collectives  35.4 us (3%)
  matrix products  17.8 us (2%)
  between operations  15.4 us (1%)
    pallas_call x1, Pallas kernels, routed_experts(): pl.pallas_call(experts_kernel, in_specs=[vmem, anywhere, anywhere, vmem,...  400 us
    pallas_call x4, Pallas kernels, square_sum(): pl.pallas_call(functools.partial(sum_kernel, base, by_quarter, own_weight...  178 us
    ppermute x31, waiting for transfers between devices, swap(): return lax.ppermute(value, 'gx', [(i, i ^ bit) for i in range(4)])  61.2 us
    pallas_call x2, Pallas kernels, weight_grad(): pl.pallas_call(functools.partial(weight_grad_kernel, shapes_of(groups), f...  48.9 us
    ppermute x31, starting transfers between devices, swap(): return lax.ppermute(value, 'gx', [(i, i ^ bit) for i in range(4)])  31.9 us
    all_to_all x2, blocking collectives, to_tokens(): return lax.all_to_all(value, 'gx', split_axis=0, concat_axis=1, tiled=True)  24.1 us
  transfers between devices with their start and end apart: 54, of which 27 were waited for; matrix products, arithmetic and copies ran while one was open for 8% of the time, Pallas kernels for 64%

profile of v3, /device:TPU:0, one launch (start us, length us, event | category | flops | bytes accessed | tf_op | source)
XLA Modules:
  0.0 1102.2 jit_solution(3588185606451821348)
XLA Ops:
  9.2 11.4 %psum.7 = f32[512]{0:T(512)S(1)} all-reduce(f32[512]{0:T(512)S(1)} %fusion.6), channel_id=1, replica_groups=mesh['gx'=4,'gy'=8] {'gx'}, use_global_device_ids=true, to_apply=%region_1.0 | all-reduce | flops 512 | bytes 4096 | tf_op jit(solution)/shard_map/psum | solution.py:111
  43.4 7.0 one_hot.1.chosen_ref.chosen
  50.4 15.7 %collective-permute-done.refs_1_ = bf16[512,1152]{1,0:T(8,128)(2,1)} collective-permute-done((bf16[512,1152]{1,0:T(8,128)(2,1)}, bf16[512,1152]{1,0:T(8,128)(2,1)}, u32[]{:S(2)}, u32[]{:S(2)}) %collective-permute-start) | collective-permute-done | bytes 1179680 | tf_op jit(solution)/shard_map/ppermute | solution.py:67
  66.4 5.7 fusion.2
  72.1 41.1 %square_sum.4 = f32[4,256,512]{2,1,0:T(8,128)} custom-call(bf16[4,4,256,512]{3,2,1,0:T(8,128)(2,1)} %bitcast.207, bf16[512,512]{1,0:T(8,128)(2,1)} %fusion.19.weight.refs_10_), custom_call_target="tpu_custom_call" | custom-call | flops 25874999296 | tf_op jit(solution)/shard_map/square_sum/pallas_call | solution.py:797
  115.4 11.8 %all_to_all.88 = bf16[4,128,512]{2,1,0:T(8,128)(2,1)S(1)} all-to-all(bf16[4,128,512]{2,1,0:T(8,128)(2,1)S(1)} %bitcast.203), channel_id=1, replica_groups=mesh['gx'=4,'gy'=8] {'gx'}, dimensions={0} | all-to-all | bytes 1048576 | tf_op jit(solution)/shard_map/all_to_all | solution.py:143
  128.0 10.0 all-gather.12.cloned.1.call-done
  146.9 11.2 %attention.1 = (bf16[1024,256]{1,0:T(8,128)(2,1)}, f32[1,2,1024,1]{3,2,1,0:T(8,128)}, bf16[1,2,1024,192]{3,2,1,0:T(8,128)(2,1)}, bf16[1,2,1024,192]{3,2,1,0:T(8,...) custom-call(s32[1,2]{1,0:T(1,128)} %starts_ref.3, f32[1024,512]{1,0:T(8,128)} %bitcast.246, ...), custom_call_target="tpu_custom_call" | custom-call | flops 6899999744 | tf_op jit(solution)/shard_map/attention/pallas_call | solution.py:1264
  161.5 9.0 dispatch.2
  186.9 55.9 %square_sum.5.grad_low.refs_10_ = bf16[4,128,1408]{2,1,0:T(8,128)(2,1)} custom-call(bf16[8,4,128,512]{3,2,1,0:T(8,128)(2,1)} %bitcast.189, bf16[8,1408,512]{2,1,0:T(8,128)(2,1)} %refs_12_), custom_call_target="tpu_custom_call" | custom-call | flops 31050000384 | tf_op jit(solution)/shard_map/square_sum/pallas_call | solution.py:797
  246.0 12.3 %all_to_all.89 = bf16[4,128,512]{2,1,0:T(8,128)(2,1)S(1)} all-to-all(bf16[4,128,512]{2,1,0:T(8,128)(2,1)} %bitcast.202), channel_id=1, replica_groups=mesh['gx'=4,'gy'=8] {'gx'}, dimensions={0} | all-to-all | bytes 1048576 | tf_op jit(solution)/shard_map/all_to_all | solution.py:143
  275.6 55.4 %square_sum.6.grad_high = bf16[4,128,1408]{2,1,0:T(8,128)(2,1)} custom-call(bf16[8,4,128,512]{3,2,1,0:T(8,128)(2,1)} %bitcast.190, bf16[8,1408,512]{2,1,0:T(8,128)(2,1)} %refs_12_), custom_call_target="tpu_custom_call" | custom-call | flops 31050000384 | tf_op jit(solution)/shard_map/square_sum/pallas_call | solution.py:797
  335.1 10.8 dispatch.3
  345.9 17.1 %shared_experts.1 = (bf16[1024,384]{1,0:T(8,128)(2,1)}, bf16[1024,768]{1,0:T(8,128)(2,1)}, bf16[1024,2048]{1,0:T(8,128)(2,1)}, bf16[1024,2048]{1,0:T(8,128)(2,1)}) custom-call(s32[4]{0:T(128)} %pad_add_fusion.picks_ref, bf16[1024,2048]{1,0:T(8,128)(2,1)} %all-gather.18.cloned.1.call-done.norm, f32[1024,1]{1,0:T(8,128)} %copy.176.scale, ...), custom_call_target="tpu_custom_call" | custom-call | flops 9200000000 | tf_op jit(solution)/shard_map/shared_experts/pallas_call | solution.py:1128
  364.4 400.3 %routed_experts.1 = (bf16[8,2,128,1408]{3,2,1,0:T(8,128)(2,1)}, bf16[8,2,128,1408]{3,2,1,0:T(8,128)(2,1)}, bf16[8,2,128,1408]{3,2,1,0:T(8,128)(2,1)}, bf16[8,2,1...) custom-call(bf16[8,4,128,512]{3,2,1,0:T(8,128)(2,1)} %bitcast.183, ...), custom_call_target="tpu_custom_call" | custom-call | flops 224250003456 | tf_op jit(solution)/shard_map/routed_experts/pallas_call | solution.py:668
  783.6 6.0 all-to-all-done.4
  793.7 13.0 %all-to-all-done.5 = bf16[2,128,2048]{1,0,2:T(2,128)(2,1)S(1)} async-done(((bf16[2,128,2048]{1,0,2:T(2,128)(2,1)}), bf16[2,128,2048]{1,0,2:T(2,128)(2,1)S(1)}, u32[]{:S(2)}, u32[]{:S(2)}) %all-to-all-start.5) | async-done | bytes 1048608 | tf_op jit(solution)/shard_map/all_to_all | solution.py:1636
  819.7 6.1 small_totals.2
  836.6 29.5 %weight_grad.2 = (f32[8,512,1408]{2,1,0:T(8,128)}, f32[8,512,1408]{2,1,0:T(8,128)}) custom-call(s32[4]{0:T(128)} %pad_add_fusion.picks_ref, bf16[8,4,128,512]{3,2,1,0:T(8,128)(2,1)} %bitcast.184, bf16[8,4,128,512]{3,2,1,0:T(8,128)(2,1)} %bitcast.185, bf16[8,4,128,512]{3,2,1,0:T(8,128)(2,1)} %bitcast.186, bf16[8,4,128,512]{3,2,1,0:T(8,128)(2,1)} %bitcast.187, ...), custom_call_target="tpu_custom_call" | custom-call | flops 575000000 | tf_op jit(solution)/shard_map/weight_grad/pallas_call | solution.py:1053
  866.1 11.8 %shared_weights.1 = bf16[2048,1152]{1,0:T(8,128)(2,1)} custom-call(bf16[1024,2048]{1,0:T(8,128)(2,1)} %all-gather.18.cloned.1.call-done.norm, bf16[1024,768]{1,0:T(8,128)(2,1)} %get-tuple-element.217.grads, bf16[1024,2048]{1,0:T(8,128)(2,1)} %all-gather.14.cloned.1.call-done.grad.refs_9_, bf16[1024,384]{1,0:T(8,128)(2,1)} %get-tuple-element.218.hidden), custom_call_target="tpu_custom_call" | custom-call | flops 5750000128 | tf_op jit(solution)/shard_map/shared_weights/pallas_call | solution.py:1169
  878.0 25.4 %square_sum.7 = bf16[4,256,256]{2,1,0:T(8,128)(2,1)} custom-call(bf16[4,4,256,512]{3,2,1,0:T(8,128)(2,1)} %bitcast.265, bf16[256,512]{1,0:T(8,128)(2,1)} %weight.5), custom_call_target="tpu_custom_call" | custom-call | flops 18400000000 | tf_op jit(solution)/shard_map/square_sum/pallas_call | solution.py:797
  906.1 12.5 %attention_back.1 = (bf16[1024,384]{1,0:T(8,128)(2,1)}, bf16[1024,512]{1,0:T(8,128)(2,1)}, bf16[1024,576]{1,0:T(8,128)(2,1)}) custom-call(s32[1,2]{1,0:T(1,128)} %starts_ref.3, bf16[1,2,1024,192]{3,2,1,0:T(8,128)(2,1)} %get-tuple-element.182.q_ref, bf16[1,2,1024,192]{3,2,1,0:T(8,128)(2,1)} %get-tuple-element.183.k_ref, ...), custom_call_target="tpu_custom_call" | custom-call | flops 8049999872 | tf_op jit(solution)/shard_map/attention_back/pallas_call | solution.py:1353
  927.4 11.3 %collective-permute-done.20.refs_7_.refs_11_ = bf16[2,1,128,1408]{3,2,1,0:T(8,128)(2,1)} collective-permute-done((bf16[2,1,128,1408]{3,2,1,0:T(8,128)(2,1)}, bf16[2,1,128,1408]{3,2,1,0:T(8,128)(2,1)}, u32[]{:S(2)}, u32[]{:S(2)}) %collective-permute-start.20) | collective-permute-done | bytes 720928 | tf_op jit(solution)/shard_map/ppermute | solution.py:67
  939.8 15.4 %back.1 = bf16[8,4,128,512]{3,2,1,0:T(8,128)(2,1)} custom-call(s32[4]{0:T(128)} %pad_add_fusion.picks_ref, bf16[8,1,128,1408]{3,2,1,0:T(8,128)(2,1)} %get-tuple-element.221.refs_0_.refs_4_, bf16[2,1,128,1408]{3,2,1,0:T(8,128)(2,1)} %get-tuple-element.224.refs_1_.refs_5_, bf16[2,1,128,1408]{3,2,1,0:T(8,128)(2,1)} %get-tuple-element.228.refs_2_.refs_6_, ...), custom_call_target="tpu_custom_call" | custom-call | flops 18400000000 | tf_op jit(solution)/shard_map/back/pallas_call | solution.py:1000
  955.5 8.8 combine.1
  979.0 7.6 all-to-all-done.6
  990.5 5.7 collective-permute-done.30.refs_7_
  1006.6 7.9 norm_products.1
  1022.4 6.0 fusion.52
  1029.2 19.5 %weight_grad.3 = f32[8,1408,512]{2,1,0:T(8,128)} custom-call(s32[4]{0:T(128)} %pad_add_fusion.picks_ref, bf16[8,4,128,512]{3,2,1,0:T(8,128)(2,1)} %bitcast.191, bf16[8,4,128,512]{3,2,1,0:T(8,128)(2,1)} %bitcast.192, bf16[8,4,128,512]{3,2,1,0:T(8,128)(2,1)} %bitcast.193, bf16[8,4,128,512]{3,2,1,0:T(8,128)(2,1)} %bitcast.194, ...), custom_call_target="tpu_custom_call" | custom-call | flops 575000000 | tf_op jit(solution)/shard_map/weight_grad/pallas_call | solution.py:1053
  1056.1 13.8 %reduce-scatter.20.cloned.1.call-done = bf16[512,512]{1,0:T(8,128)(2,1)} async-done(((bf16[4096,512]{1,0:T(8,128)(2,1)}), bf16[512,512]{1,0:T(8,128)(2,1)}) %reduce-scatter.20.cloned.1.call-update) | async-done | bytes 524304 | tf_op jit(solution)/shard_map/reduce_scatter | solution.py:139
  1073.9 12.3 %small_totals.3 = (f32[8,128]{1,0:T(8,128)}, f32[16,128]{1,0:T(8,128)}) custom-call(f32[8,128]{1,0:T(8,128)} %pad_maximum_fusion.7.inner_ref, f32[8,128]{1,0:T(8,128)} %pad_maximum_fusion.8.outer_ref), custom_call_target="tpu_custom_call" | custom-call | flops 3449999872 | tf_op jit(solution)/shard_map/small_totals/pallas_call | solution.py:885
  (396 shorter events, 199.8 us)
Async XLA Ops:
  7.2 58.9 %all-gather.8.cloned.1.call-start = ((), (), s32[]{:S(2)}) async-start(), calls=%async_computation.15 | async-start | bytes 4718592 | tf_op jit(solution)/shard_map/all_gather | solution.py:135
  27.4 87.1 %all-gather.10.cloned.1.call-start = ((), (), s32[]{:S(2)}) async-start(), calls=%async_computation.16 | async-start | bytes 4718592 | tf_op jit(solution)/shard_map/all_gather | solution.py:135
  37.6 28.5 %collective-permute-start = (bf16[512,1152]{1,0:T(8,128)(2,1)}, bf16[512,1152]{1,0:T(8,128)(2,1)}, u32[]{:S(2)}, u32[]{:S(2)}) collective-permute-start(bf16[512,1152]{1,0:T(8,128)(2,1)} %side_by_side.1.refs_0_), channel_id=1, source_target_pairs={{0,8},{8,0},{16,24},{24,16},{1,9},{9,1},{17,25},{25,17},{2,10},{10... | collective-permute-start | bytes 3538952 | tf_op jit(solution)/shard_map/ppermute | solution.py:67
  38.6 27.6 %collective-permute-start.1 = (bf16[512,1152]{1,0:T(8,128)(2,1)}, bf16[512,1152]{1,0:T(8,128)(2,1)}, u32[]{:S(2)}, u32[]{:S(2)}) collective-permute-start(bf16[512,1152]{1,0:T(8,128)(2,1)} %side_by_side.1.refs_0_), channel_id=1, source_target_pairs={{0,16},{8,24},{16,0},{24,8},{1,17},{9,25},{17,1},{25,9},{2,18},{10... | collective-permute-start | bytes 3538952 | tf_op jit(solution)/shard_map/ppermute | solution.py:67
  66.2 71.8 %all-gather.12.cloned.1.call-start = ((), (), s32[]{:S(2)}) async-start(), calls=%async_computation.17 | async-start | bytes 1327104 | tf_op jit(solution)/shard_map/all_gather | solution.py:1518
  115.3 71.6 %all-gather.14.cloned.1.call-start = ((), (), s32[]{:S(2)}) async-start(), calls=%async_computation.19 | async-start | bytes 4718592 | tf_op jit(solution)/shard_map/all_gather | solution.py:135
  138.0 104.8 %reduce-scatter.8.cloned.1.call-start = ((), (), s32[]{:S(2)}) async-start(), calls=%async_computation.18 | async-start | bytes 4718592 | tf_op jit(solution)/shard_map/reduce_scatter | solution.py:139
  185.0 150.1 %all-gather.16.cloned.1.call-start = ((), (), s32[]{:S(2)}) async-start(), calls=%async_computation.20 | async-start | bytes 4718592 | tf_op jit(solution)/shard_map/all_gather | solution.py:135
  245.9 100.0 %all-gather.18.cloned.1.call-start = ((), (), s32[]{:S(2)}) async-start(), calls=%async_computation.21 | async-start | bytes 4718592 | tf_op jit(solution)/shard_map/all_gather | solution.py:135
  272.2 58.9 %all-to-all-start.2 = ((f32[8,9,512]{2,1,0:T(8,128)}), f32[8,9,512]{2,1,0:T(8,128)S(1)}, u32[]{:S(2)}, u32[]{:S(2)}) async-start(f32[8,9,512]{2,1,0:T(8,128)} %pad_maximum_fusion.4), calls=%async_computation.3 | async-start | bytes 524288 | tf_op jit(solution)/shard_map/all_to_all | solution.py:1573
  275.6 489.1 %reduce-scatter.10.cloned.1.call-start = ((), (), s32[]{:S(2)}) async-start(), calls=%async_computation.22 | async-start | bytes 4718592 | tf_op jit(solution)/shard_map/reduce_scatter | solution.py:139
  363.0 417.4 %reduce-scatter.14.cloned.1.call-start = ((), (), s32[]{:S(2)}) async-start(), calls=%async_computation.24 | async-start | bytes 4718592 | tf_op jit(solution)/shard_map/reduce_scatter | solution.py:139
  364.1 452.8 %reduce-scatter.12.cloned.1.call-start = ((), (), s32[]{:S(2)}) async-start(), calls=%async_computation.23 | async-start | bytes 4718592 | tf_op jit(solution)/shard_map/reduce_scatter | solution.py:139
  789.7 17.0 %all-to-all-start.5 = ((bf16[2,128,2048]{1,0,2:T(2,128)(2,1)}), bf16[2,128,2048]{1,0,2:T(2,128)(2,1)S(1)}, u32[]{:S(2)}, u32[]{:S(2)}) async-start(bf16[2,128,2048]{1,0,2:T(2,128)(2,1)} %copy.179), calls=%async_computation.9 | async-start | bytes 2097152 | tf_op jit(solution)/shard_map/all_to_all | solution.py:1636
  793.2 84.7 %all-gather.20.cloned.1.call-start = ((), (), s32[]{:S(2)}) async-start(), calls=%async_computation.25 | async-start | bytes 4718592 | tf_op jit(solution)/shard_map/all_gather | solution.py:135
  828.2 136.8 %reduce-scatter.16.cloned.1.call-start = ((), (), s32[]{:S(2)}) async-start(), calls=%async_computation.26 | async-start | bytes 1474560 | tf_op jit(solution)/shard_map/reduce_scatter | solution.py:139
  830.8 47.2 %collective-permute-start.17 = (bf16[4,1,128,1408]{3,2,1,0:T(8,128)(2,1)S(1)}, bf16[4,1,128,1408]{3,2,1,0:T(8,128)(2,1)}, u32[]{:S(2)}, u32[]{:S(2)}) collective-permute-start(bf16[4,1,128,1408]{3,2,1,0:T(8,128)(2,1)S(1)} %slice.134.refs_8_.refs_12_), channel_id=1, source_target_pairs={{0,8},{8,0},{16,24},{24,16},{1,9},{9,1},{17,25},{25,17},{2,10},{10... | collective-permute-start | bytes 4325384 | tf_op jit(solution)/shard_map/ppermute | solution.py:67
  832.4 45.6 %collective-permute-start.18 = (bf16[4,1,128,1408]{3,2,1,0:T(8,128)(2,1)S(1)}, bf16[4,1,128,1408]{3,2,1,0:T(8,128)(2,1)}, u32[]{:S(2)}, u32[]{:S(2)}) collective-permute-start(bf16[4,1,128,1408]{3,2,1,0:T(8,128)(2,1)S(1)} %slice.134.refs_8_.refs_12_), channel_id=1, source_target_pairs={{0,16},{8,24},{16,0},{24,8},{1,17},{9,25},{17,1},{25,9},{2,18},{10... | collective-permute-start | bytes 4325384 | tf_op jit(solution)/shard_map/ppermute | solution.py:67
  835.0 42.9 %collective-permute-start.15 = (bf16[2,1,128,1408]{3,2,1,0:T(8,128)(2,1)S(1)}, bf16[2,1,128,1408]{3,2,1,0:T(8,128)(2,1)}, u32[]{:S(2)}, u32[]{:S(2)}) collective-permute-start(bf16[2,1,128,1408]{3,2,1,0:T(8,128)(2,1)S(1)} %slice.133.refs_4_.refs_8_), channel_id=1, source_target_pairs={{0,8},{8,0},{16,24},{24,16},{1,9},{9,1},{17,25},{25,17},{2,10},{10... | collective-permute-start | bytes 2162696 | tf_op jit(solution)/shard_map/ppermute | solution.py:67
  835.7 42.3 %collective-permute-start.16 = (bf16[2,1,128,1408]{3,2,1,0:T(8,128)(2,1)S(1)}, bf16[2,1,128,1408]{3,2,1,0:T(8,128)(2,1)}, u32[]{:S(2)}, u32[]{:S(2)}) collective-permute-start(bf16[2,1,128,1408]{3,2,1,0:T(8,128)(2,1)S(1)} %slice.133.refs_4_.refs_8_), channel_id=1, source_target_pairs={{0,16},{8,24},{16,0},{24,8},{1,17},{9,25},{17,1},{25,9},{2,18},{10... | collective-permute-start | bytes 2162696 | tf_op jit(solution)/shard_map/ppermute | solution.py:67
  836.5 41.4 %collective-permute-start.14 = (f32[512,64]{0,1:T(8,128)S(1)}, f32[512,64]{0,1:T(8,128)S(1)}, u32[]{:S(2)}, u32[]{:S(2)}) collective-permute-start(f32[512,64]{0,1:T(8,128)S(1)} %fusion.20), channel_id=1, source_target_pairs={{0,1},{1,0},{2,3},{3,2},{4,5},{5,4},{6,7},{7,6},{8,9},{9,8},{10,11... | collective-permute-start | bytes 393224 | tf_op jit(solution)/shard_map/ppermute | solution.py:131
  903.4 35.3 %collective-permute-start.21 = (bf16[4,1,128,1408]{3,2,1,0:T(8,128)(2,1)}, bf16[4,1,128,1408]{3,2,1,0:T(8,128)(2,1)S(1)}, u32[]{:S(2)}, u32[]{:S(2)}) collective-permute-start(bf16[4,1,128,1408]{3,2,1,0:T(8,128)(2,1)} %collective-permute-done.17.refs_9_.refs_13_), channel_id=1, source_target_pairs={{0,16},{8,24},{16,0},{24,8},{1,17},{9,25},{17,1},{25,9},{2,18},{10... | collective-permute-start | bytes 4325384 | tf_op jit(solution)/shard_map/ppermute | solution.py:67
  904.1 22.2 %collective-permute-start.19 = (bf16[2,1,128,1408]{3,2,1,0:T(8,128)(2,1)S(1)}, bf16[2,1,128,1408]{3,2,1,0:T(8,128)(2,1)}, u32[]{:S(2)}, u32[]{:S(2)}) collective-permute-start(bf16[2,1,128,1408]{3,2,1,0:T(8,128)(2,1)S(1)} %copy-done.27), channel_id=1, source_target_pairs={{0,8},{8,0},{16,24},{24,16},{1,9},{9,1},{17,25},{25,17},{2,10},{10... | collective-permute-start | bytes 2162696 | tf_op jit(solution)/shard_map/ppermute | solution.py:67
  905.5 33.2 %collective-permute-start.20 = (bf16[2,1,128,1408]{3,2,1,0:T(8,128)(2,1)}, bf16[2,1,128,1408]{3,2,1,0:T(8,128)(2,1)}, u32[]{:S(2)}, u32[]{:S(2)}) collective-permute-start(bf16[2,1,128,1408]{3,2,1,0:T(8,128)(2,1)} %collective-permute-done.16.refs_6_.refs_10_), channel_id=1, source_target_pairs={{0,8},{8,0},{16,24},{24,16},{1,9},{9,1},{17,25},{25,17},{2,10},{10... | collective-permute-start | bytes 2162696 | tf_op jit(solution)/shard_map/ppermute | solution.py:67
  918.6 135.1 %reduce-scatter.18.cloned.1.call-start = ((), (), s32[]{:S(2)}) async-start(), calls=%async_computation.27 | async-start | bytes 4718592 | tf_op jit(solution)/shard_map/reduce_scatter | solution.py:139
  918.8 36.7 %collective-permute-start.22 = (bf16[1024,384]{1,0:T(8,128)(2,1)}, bf16[1024,384]{1,0:T(8,128)(2,1)}, u32[]{:S(2)}, u32[]{:S(2)}) collective-permute-start(bf16[1024,384]{1,0:T(8,128)(2,1)} %get-tuple-element.234.refs_0_), channel_id=1, source_target_pairs={{0,8},{8,0},{16,24},{24,16},{1,9},{9,1},{17,25},{25,17},{2,10},{10... | collective-permute-start | bytes 2359304 | tf_op jit(solution)/shard_map/ppermute | solution.py:67
  925.4 30.2 %collective-permute-start.23 = (bf16[1024,384]{1,0:T(8,128)(2,1)S(1)}, bf16[1024,384]{1,0:T(8,128)(2,1)}, u32[]{:S(2)}, u32[]{:S(2)}) collective-permute-start(bf16[1024,384]{1,0:T(8,128)(2,1)S(1)} %copy-done.62), channel_id=1, source_target_pairs={{0,16},{8,24},{16,0},{24,8},{1,17},{9,25},{17,1},{25,9},{2,18},{10... | collective-permute-start | bytes 2359304 | tf_op jit(solution)/shard_map/ppermute | solution.py:67
  926.3 38.7 %collective-permute-start.24 = (bf16[512,512]{1,0:T(8,128)(2,1)}, bf16[512,512]{1,0:T(8,128)(2,1)S(1)}, u32[]{:S(2)}, u32[]{:S(2)}) collective-permute-start(bf16[512,512]{1,0:T(8,128)(2,1)} %convolution_convert_fusion.1), channel_id=1, source_target_pairs={{0,8},{8,0},{16,24},{24,16},{1,9},{9,1},{17,25},{25,17},{2,10},{10... | collective-permute-start | bytes 1572872 | tf_op jit(solution)/shard_map/ppermute | solution.py:67
  976.8 93.2 %reduce-scatter.20.cloned.1.call-start = ((), (), s32[]{:S(2)}) async-start(), calls=%async_computation.28 | async-start | bytes 4718592 | tf_op jit(solution)/shard_map/reduce_scatter | solution.py:139
  978.6 20.3 %collective-permute-start.26 = (bf16[512,384]{1,0:T(8,128)(2,1)}, bf16[512,384]{1,0:T(8,128)(2,1)}, u32[]{:S(2)}, u32[]{:S(2)}) collective-permute-start(bf16[512,384]{1,0:T(8,128)(2,1)} %slice.136), channel_id=1, source_target_pairs={{0,8},{8,0},{16,24},{24,16},{1,9},{9,1},{17,25},{25,17},{2,10},{10... | collective-permute-start | bytes 1179656 | tf_op jit(solution)/shard_map/ppermute | solution.py:67
  1014.5 73.8 %all-to-all-start.7 = ((bf16[4,512,1152]{2,1,0:T(8,128)(2,1)}), bf16[4,512,1152]{2,1,0:T(8,128)(2,1)}, u32[]{:S(2)}, u32[]{:S(2)}) async-start(bf16[4,512,1152]{2,1,0:T(8,128)(2,1)} %bitcast.204), calls=%async_computation.14 | async-start | bytes 9437184 | tf_op jit(solution)/shard_map/all_to_all | solution.py:124
  1029.2 23.8 %collective-permute-start.33 = (f32[512,64]{0,1:T(8,128)S(1)}, f32[512,64]{0,1:T(8,128)S(1)}, u32[]{:S(2)}, u32[]{:S(2)}) collective-permute-start(f32[512,64]{0,1:T(8,128)S(1)} %add.150), channel_id=1, source_target_pairs={{0,4},{1,5},{2,6},{3,7},{4,0},{5,1},{6,2},{7,3},{8,12},{9,13},{10,... | collective-permute-start | bytes 393224 | tf_op jit(solution)/shard_map/ppermute | solution.py:131
  (88 other events, 1377.2 us)
Sparse Core Ops, SparseCore 0:
  9.6 52.6 all-gather.7
  66.3 47.5 all-gather.9
  116.1 21.7 all-gather.11
  140.0 46.9 all-gather.13
  189.1 48.7 reduce-scatter.7
  246.1 50.5 all-gather.15
  298.8 45.8 all-gather.17
  363.2 50.1 reduce-scatter.9
  416.2 48.1 reduce-scatter.13
  764.9 52.0 reduce-scatter.11
  828.3 45.2 all-gather.19
  918.7 31.8 reduce-scatter.15
  966.1 50.6 reduce-scatter.17
  1018.9 51.0 reduce-scatter.19

commit v4 on v3

--- a/solution.py
+++ b/solution.py
@@ -1670,12 +1670,7 @@
     grad_after_all, grad_router = together(grad_after_all, grad_router)
     waiting = after(rows_two, grad_after_sent)
     grad_gate, grad_up = weight_grad(waiting, grad_groups, order_of, False, slot_scale)
-    grad_shared = shared_weights(
-        after(gained_band, grad_gate), grad_shared_both, grad_top_band, shared_hidden
-    )
-    grad_after_all, grad_gate, grad_up, grad_shared = together(
-        grad_after_all, grad_gate, grad_up, grad_shared
-    )
+    grad_after_all, grad_gate, grad_up = together(grad_after_all, grad_gate, grad_up)
     if on_square:
         grad_after_all, low_x, low_y, high_x, high_y = together(
             grad_after_all, low_x, low_y, high_x, high_y
@@ -1702,7 +1697,10 @@
 
     if on_square:
         query_x, query_y = swap(grad_query_pre, 1), swap(grad_query_pre, 2)
-    waiting = after(down_weight, latent_grads)
+    grad_shared = shared_weights(
+        after(gained_band, latent_grads), grad_shared_both, grad_top_band, shared_hidden
+    )
+    waiting = after(down_weight, latent_grads, grad_shared)
     out = back(hidden_groups, order_of, (waiting,), False)
     if on_square:
         out, query_x, query_y = together(out, query_x, query_y)

time: 1110 us -> 1130 us (1.018)
  transfers between devices with their start and end apart: 54 -> 54, of which waited for: 27 -> 28; matrix products, arithmetic and copies ran while one was open for 8% -> 8% of each run, Pallas kernels for 64% -> 64%
where the time goes in v4:
time: 1130 us; the launch traced here: 1120 us
  Pallas kernels  761 us (67%)
  waiting for transfers between devices  129 us (11%)
  starting transfers between devices  69.4 us (6%)
  local copies, waits for them, and re-layouts  48.8 us (4%)
  other arithmetic  39.7 us (4%)
  blocking collectives  35.5 us (3%)
  matrix products  16.4 us (1%)
  between operations  15.6 us (1%)
    pallas_call x1, Pallas kernels, routed_experts(): pl.pallas_call(experts_kernel, in_specs=[vmem, anywhere, anywhere, vmem,...  400 us
    pallas_call x4, Pallas kernels, square_sum(): pl.pallas_call(functools.partial(sum_kernel, base, by_quarter, own_weight...  174 us
    ppermute x31, waiting for transfers between devices, swap(): return lax.ppermute(value, 'gx', [(i, i ^ bit) for i in range(4)])  58.5 us
    pallas_call x2, Pallas kernels, weight_grad(): pl.pallas_call(functools.partial(weight_grad_kernel, shapes_of(groups), f...  48.5 us
    ppermute x31, starting transfers between devices, swap(): return lax.ppermute(value, 'gx', [(i, i ^ bit) for i in range(4)])  35.8 us
    all_to_all x2, blocking collectives, to_tokens(): return lax.all_to_all(value, 'gx', split_axis=0, concat_axis=1, tiled=True)  24.1 us
  transfers between devices with their start and end apart: 54, of which 28 were waited for; matrix products, arithmetic and copies ran while one was open for 8% of the time, Pallas kernels for 64%

profile of v4, /device:TPU:0, one launch (start us, length us, event | category | flops | bytes accessed | tf_op | source)
XLA Modules:
  0.0 1115.4 jit_solution(18343297180828357147)
XLA Ops:
  9.2 11.4 %psum.7 = f32[512]{0:T(512)S(1)} all-reduce(f32[512]{0:T(512)S(1)} %fusion.6), channel_id=1, replica_groups=mesh['gx'=4,'gy'=8] {'gx'}, use_global_device_ids=true, to_apply=%region_1.0 | all-reduce | flops 512 | bytes 4096 | tf_op jit(solution)/shard_map/psum | solution.py:111
  43.4 6.9 one_hot.1.chosen_ref.chosen
  50.4 15.7 %collective-permute-done.refs_1_ = bf16[512,1152]{1,0:T(8,128)(2,1)} collective-permute-done((bf16[512,1152]{1,0:T(8,128)(2,1)}, bf16[512,1152]{1,0:T(8,128)(2,1)}, u32[]{:S(2)}, u32[]{:S(2)}) %collective-permute-start) | collective-permute-done | bytes 1179680 | tf_op jit(solution)/shard_map/ppermute | solution.py:67
  72.1 41.1 %square_sum.4 = f32[4,256,512]{2,1,0:T(8,128)} custom-call(bf16[4,4,256,512]{3,2,1,0:T(8,128)(2,1)} %bitcast.207, bf16[512,512]{1,0:T(8,128)(2,1)} %fusion.19.weight.refs_10_), custom_call_target="tpu_custom_call" | custom-call | flops 25874999296 | tf_op jit(solution)/shard_map/square_sum/pallas_call | solution.py:797
  115.4 11.7 %all_to_all.88 = bf16[4,128,512]{2,1,0:T(8,128)(2,1)S(1)} all-to-all(bf16[4,128,512]{2,1,0:T(8,128)(2,1)S(1)} %bitcast.204), channel_id=1, replica_groups=mesh['gx'=4,'gy'=8] {'gx'}, dimensions={0} | all-to-all | bytes 1048576 | tf_op jit(solution)/shard_map/all_to_all | solution.py:143
  128.0 10.0 all-gather.12.cloned.1.call-done
  146.6 11.3 %attention.1 = (bf16[1024,256]{1,0:T(8,128)(2,1)}, f32[1,2,1024,1]{3,2,1,0:T(8,128)}, bf16[1,2,1024,192]{3,2,1,0:T(8,128)(2,1)}, bf16[1,2,1024,192]{3,2,1,0:T(8,...) custom-call(s32[1,2]{1,0:T(1,128)} %starts_ref.3, f32[1024,512]{1,0:T(8,128)} %bitcast.246, ...), custom_call_target="tpu_custom_call" | custom-call | flops 6899999744 | tf_op jit(solution)/shard_map/attention/pallas_call | solution.py:1264
  161.2 9.0 dispatch.2
  186.9 55.8 %square_sum.5.grad_low.refs_10_ = bf16[4,128,1408]{2,1,0:T(8,128)(2,1)} custom-call(bf16[8,4,128,512]{3,2,1,0:T(8,128)(2,1)} %bitcast.189, bf16[8,1408,512]{2,1,0:T(8,128)(2,1)} %refs_12_), custom_call_target="tpu_custom_call" | custom-call | flops 31050000384 | tf_op jit(solution)/shard_map/square_sum/pallas_call | solution.py:797
  246.0 12.4 %all_to_all.89 = bf16[4,128,512]{2,1,0:T(8,128)(2,1)S(1)} all-to-all(bf16[4,128,512]{2,1,0:T(8,128)(2,1)} %bitcast.203), channel_id=1, replica_groups=mesh['gx'=4,'gy'=8] {'gx'}, dimensions={0} | all-to-all | bytes 1048576 | tf_op jit(solution)/shard_map/all_to_all | solution.py:143
  275.7 55.4 %square_sum.6.grad_high = bf16[4,128,1408]{2,1,0:T(8,128)(2,1)} custom-call(bf16[8,4,128,512]{3,2,1,0:T(8,128)(2,1)} %bitcast.190, bf16[8,1408,512]{2,1,0:T(8,128)(2,1)} %refs_12_), custom_call_target="tpu_custom_call" | custom-call | flops 31050000384 | tf_op jit(solution)/shard_map/square_sum/pallas_call | solution.py:797
  335.1 10.9 dispatch.3
  346.0 17.1 %shared_experts.1 = (bf16[1024,384]{1,0:T(8,128)(2,1)}, bf16[1024,768]{1,0:T(8,128)(2,1)}, bf16[1024,2048]{1,0:T(8,128)(2,1)}, bf16[1024,2048]{1,0:T(8,128)(2,1)}) custom-call(s32[4]{0:T(128)} %pad_add_fusion.picks_ref, bf16[1024,2048]{1,0:T(8,128)(2,1)} %all-gather.18.cloned.1.call-done.norm, f32[1024,1]{1,0:T(8,128)} %copy.176.scale, ...), custom_call_target="tpu_custom_call" | custom-call | flops 9200000000 | tf_op jit(solution)/shard_map/shared_experts/pallas_call | solution.py:1128
  364.6 400.3 %routed_experts.1 = (bf16[8,2,128,1408]{3,2,1,0:T(8,128)(2,1)}, bf16[8,2,128,1408]{3,2,1,0:T(8,128)(2,1)}, bf16[8,2,128,1408]{3,2,1,0:T(8,128)(2,1)}, bf16[8,2,1...) custom-call(bf16[8,4,128,512]{3,2,1,0:T(8,128)(2,1)} %bitcast.183, ...), custom_call_target="tpu_custom_call" | custom-call | flops 224250003456 | tf_op jit(solution)/shard_map/routed_experts/pallas_call | solution.py:668
  794.1 13.0 %all-to-all-done.5 = bf16[2,128,2048]{1,0,2:T(2,128)(2,1)S(1)} async-done(((bf16[2,128,2048]{1,0,2:T(2,128)(2,1)}), bf16[2,128,2048]{1,0,2:T(2,128)(2,1)S(1)}, u32[]{:S(2)}, u32[]{:S(2)}) %all-to-all-start.5) | async-done | bytes 1048608 | tf_op jit(solution)/shard_map/all_to_all | solution.py:1636
  811.1 6.2 reduce-scatter.12.cloned.1.call-done
  820.0 6.1 small_totals.2
  837.1 29.1 %weight_grad.2 = (f32[8,512,1408]{2,1,0:T(8,128)}, f32[8,512,1408]{2,1,0:T(8,128)}) custom-call(s32[4]{0:T(128)} %pad_add_fusion.picks_ref, bf16[8,4,128,512]{3,2,1,0:T(8,128)(2,1)} %bitcast.184, bf16[8,4,128,512]{3,2,1,0:T(8,128)(2,1)} %bitcast.185, bf16[8,4,128,512]{3,2,1,0:T(8,128)(2,1)} %bitcast.186, bf16[8,4,128,512]{3,2,1,0:T(8,128)(2,1)} %bitcast.187, ...), custom_call_target="tpu_custom_call" | custom-call | flops 575000000 | tf_op jit(solution)/shard_map/weight_grad/pallas_call | solution.py:1053
  866.2 7.7 all-gather.20.cloned.1.call-done
  878.2 21.7 %square_sum.7 = bf16[4,256,256]{2,1,0:T(8,128)(2,1)} custom-call(bf16[4,4,256,512]{3,2,1,0:T(8,128)(2,1)} %bitcast.265, bf16[256,512]{1,0:T(8,128)(2,1)} %weight.5), custom_call_target="tpu_custom_call" | custom-call | flops 18400000000 | tf_op jit(solution)/shard_map/square_sum/pallas_call | solution.py:797
  902.5 12.6 %attention_back.1 = (bf16[1024,384]{1,0:T(8,128)(2,1)}, bf16[1024,512]{1,0:T(8,128)(2,1)}, bf16[1024,576]{1,0:T(8,128)(2,1)}) custom-call(s32[1,2]{1,0:T(1,128)} %starts_ref.3, bf16[1,2,1024,192]{3,2,1,0:T(8,128)(2,1)} %get-tuple-element.182.q_ref, bf16[1,2,1024,192]{3,2,1,0:T(8,128)(2,1)} %get-tuple-element.183.k_ref, ...), custom_call_target="tpu_custom_call" | custom-call | flops 8049999872 | tf_op jit(solution)/shard_map/attention_back/pallas_call | solution.py:1353
  917.5 11.9 %shared_weights.1.refs_25_ = bf16[2048,1152]{1,0:T(8,128)(2,1)} custom-call(bf16[1024,2048]{1,0:T(8,128)(2,1)} %all-gather.18.cloned.1.call-done.norm, bf16[1024,768]{1,0:T(8,128)(2,1)} %get-tuple-element.231.grads, bf16[1024,2048]{1,0:T(8,128)(2,1)} %all-gather.14.cloned.1.call-done.grad.refs_9_, bf16[1024,384]{1,0:T(8,128)(2,1)} %get-tuple-element.232.hidden), custom_call_target="tpu_custom_call" | custom-call | flops 5750000128 | tf_op jit(solution)/shard_map/shared_weights/pallas_call | solution.py:1169
  941.3 8.7 collective-permute-done.20.refs_7_.refs_11_
  951.4 15.4 %back.1 = bf16[8,4,128,512]{3,2,1,0:T(8,128)(2,1)} custom-call(s32[4]{0:T(128)} %pad_add_fusion.picks_ref, bf16[8,1,128,1408]{3,2,1,0:T(8,128)(2,1)} %get-tuple-element.218.refs_0_.refs_4_, bf16[2,1,128,1408]{3,2,1,0:T(8,128)(2,1)} %get-tuple-element.221.refs_1_.refs_5_, bf16[2,1,128,1408]{3,2,1,0:T(8,128)(2,1)} %get-tuple-element.225.refs_2_.refs_6_, ...), custom_call_target="tpu_custom_call" | custom-call | flops 18400000000 | tf_op jit(solution)/shard_map/back/pallas_call | solution.py:1000
  966.8 8.8 combine.1
  982.5 6.0 all-to-all-start.6
  991.9 6.5 all-to-all-done.6
  1018.4 7.9 norm_products.1
  1034.3 6.2 fusion.52
  1041.3 19.4 %weight_grad.3 = f32[8,1408,512]{2,1,0:T(8,128)} custom-call(s32[4]{0:T(128)} %pad_add_fusion.picks_ref, bf16[8,4,128,512]{3,2,1,0:T(8,128)(2,1)} %bitcast.191, bf16[8,4,128,512]{3,2,1,0:T(8,128)(2,1)} %bitcast.192, bf16[8,4,128,512]{3,2,1,0:T(8,128)(2,1)} %bitcast.193, bf16[8,4,128,512]{3,2,1,0:T(8,128)(2,1)} %bitcast.194, ...), custom_call_target="tpu_custom_call" | custom-call | flops 575000000 | tf_op jit(solution)/shard_map/weight_grad/pallas_call | solution.py:1053
  1068.1 15.2 %reduce-scatter.20.cloned.1.call-done = bf16[512,512]{1,0:T(8,128)(2,1)} async-done(((bf16[4096,512]{1,0:T(8,128)(2,1)}), bf16[512,512]{1,0:T(8,128)(2,1)}) %reduce-scatter.20.cloned.1.call-update) | async-done | bytes 524304 | tf_op jit(solution)/shard_map/reduce_scatter | solution.py:139
  1087.3 12.0 %small_totals.3 = (f32[8,128]{1,0:T(8,128)}, f32[16,128]{1,0:T(8,128)}) custom-call(f32[8,128]{1,0:T(8,128)} %pad_maximum_fusion.7.inner_ref, f32[8,128]{1,0:T(8,128)} %pad_maximum_fusion.8.outer_ref), custom_call_target="tpu_custom_call" | custom-call | flops 3449999872 | tf_op jit(solution)/shard_map/small_totals/pallas_call | solution.py:885
  (402 shorter events, 216.6 us)
Async XLA Ops:
  7.2 58.9 %all-gather.8.cloned.1.call-start = ((), (), s32[]{:S(2)}) async-start(), calls=%async_computation.15 | async-start | bytes 4718592 | tf_op jit(solution)/shard_map/all_gather | solution.py:135
  27.4 87.1 %all-gather.10.cloned.1.call-start = ((), (), s32[]{:S(2)}) async-start(), calls=%async_computation.16 | async-start | bytes 4718592 | tf_op jit(solution)/shard_map/all_gather | solution.py:135
  37.6 28.5 %collective-permute-start = (bf16[512,1152]{1,0:T(8,128)(2,1)}, bf16[512,1152]{1,0:T(8,128)(2,1)}, u32[]{:S(2)}, u32[]{:S(2)}) collective-permute-start(bf16[512,1152]{1,0:T(8,128)(2,1)} %side_by_side.1.refs_0_), channel_id=1, source_target_pairs={{0,8},{8,0},{16,24},{24,16},{1,9},{9,1},{17,25},{25,17},{2,10},{10... | collective-permute-start | bytes 3538952 | tf_op jit(solution)/shard_map/ppermute | solution.py:67
  38.6 27.6 %collective-permute-start.1 = (bf16[512,1152]{1,0:T(8,128)(2,1)}, bf16[512,1152]{1,0:T(8,128)(2,1)}, u32[]{:S(2)}, u32[]{:S(2)}) collective-permute-start(bf16[512,1152]{1,0:T(8,128)(2,1)} %side_by_side.1.refs_0_), channel_id=1, source_target_pairs={{0,16},{8,24},{16,0},{24,8},{1,17},{9,25},{17,1},{25,9},{2,18},{10... | collective-permute-start | bytes 3538952 | tf_op jit(solution)/shard_map/ppermute | solution.py:67
  66.2 71.8 %all-gather.12.cloned.1.call-start = ((), (), s32[]{:S(2)}) async-start(), calls=%async_computation.17 | async-start | bytes 1327104 | tf_op jit(solution)/shard_map/all_gather | solution.py:1518
  115.3 71.6 %all-gather.14.cloned.1.call-start = ((), (), s32[]{:S(2)}) async-start(), calls=%async_computation.19 | async-start | bytes 4718592 | tf_op jit(solution)/shard_map/all_gather | solution.py:135
  138.0 104.8 %reduce-scatter.8.cloned.1.call-start = ((), (), s32[]{:S(2)}) async-start(), calls=%async_computation.18 | async-start | bytes 4718592 | tf_op jit(solution)/shard_map/reduce_scatter | solution.py:139
  184.7 150.4 %all-gather.16.cloned.1.call-start = ((), (), s32[]{:S(2)}) async-start(), calls=%async_computation.20 | async-start | bytes 4718592 | tf_op jit(solution)/shard_map/all_gather | solution.py:135
  245.9 100.1 %all-gather.18.cloned.1.call-start = ((), (), s32[]{:S(2)}) async-start(), calls=%async_computation.21 | async-start | bytes 4718592 | tf_op jit(solution)/shard_map/all_gather | solution.py:135
  272.2 58.9 %all-to-all-start.2 = ((f32[8,9,512]{2,1,0:T(8,128)}), f32[8,9,512]{2,1,0:T(8,128)S(1)}, u32[]{:S(2)}, u32[]{:S(2)}) async-start(f32[8,9,512]{2,1,0:T(8,128)} %pad_maximum_fusion.4), calls=%async_computation.3 | async-start | bytes 524288 | tf_op jit(solution)/shard_map/all_to_all | solution.py:1573
  275.6 489.4 %reduce-scatter.10.cloned.1.call-start = ((), (), s32[]{:S(2)}) async-start(), calls=%async_computation.22 | async-start | bytes 4718592 | tf_op jit(solution)/shard_map/reduce_scatter | solution.py:139
  363.1 417.7 %reduce-scatter.14.cloned.1.call-start = ((), (), s32[]{:S(2)}) async-start(), calls=%async_computation.24 | async-start | bytes 4718592 | tf_op jit(solution)/shard_map/reduce_scatter | solution.py:139
  364.2 453.1 %reduce-scatter.12.cloned.1.call-start = ((), (), s32[]{:S(2)}) async-start(), calls=%async_computation.23 | async-start | bytes 4718592 | tf_op jit(solution)/shard_map/reduce_scatter | solution.py:139
  790.0 17.0 %all-to-all-start.5 = ((bf16[2,128,2048]{1,0,2:T(2,128)(2,1)}), bf16[2,128,2048]{1,0,2:T(2,128)(2,1)S(1)}, u32[]{:S(2)}, u32[]{:S(2)}) async-start(bf16[2,128,2048]{1,0,2:T(2,128)(2,1)} %copy.179), calls=%async_computation.9 | async-start | bytes 2097152 | tf_op jit(solution)/shard_map/all_to_all | solution.py:1636
  793.5 80.4 %all-gather.20.cloned.1.call-start = ((), (), s32[]{:S(2)}) async-start(), calls=%async_computation.25 | async-start | bytes 4718592 | tf_op jit(solution)/shard_map/all_gather | solution.py:135
  828.5 147.1 %reduce-scatter.16.cloned.1.call-start = ((), (), s32[]{:S(2)}) async-start(), calls=%async_computation.26 | async-start | bytes 1474560 | tf_op jit(solution)/shard_map/reduce_scatter | solution.py:139
  831.3 46.8 %collective-permute-start.17 = (bf16[4,1,128,1408]{3,2,1,0:T(8,128)(2,1)S(1)}, bf16[4,1,128,1408]{3,2,1,0:T(8,128)(2,1)}, u32[]{:S(2)}, u32[]{:S(2)}) collective-permute-start(bf16[4,1,128,1408]{3,2,1,0:T(8,128)(2,1)S(1)} %slice.134.refs_8_.refs_12_), channel_id=1, source_target_pairs={{0,8},{8,0},{16,24},{24,16},{1,9},{9,1},{17,25},{25,17},{2,10},{10... | collective-permute-start | bytes 4325384 | tf_op jit(solution)/shard_map/ppermute | solution.py:67
  832.8 45.3 %collective-permute-start.18 = (bf16[4,1,128,1408]{3,2,1,0:T(8,128)(2,1)S(1)}, bf16[4,1,128,1408]{3,2,1,0:T(8,128)(2,1)}, u32[]{:S(2)}, u32[]{:S(2)}) collective-permute-start(bf16[4,1,128,1408]{3,2,1,0:T(8,128)(2,1)S(1)} %slice.134.refs_8_.refs_12_), channel_id=1, source_target_pairs={{0,16},{8,24},{16,0},{24,8},{1,17},{9,25},{17,1},{25,9},{2,18},{10... | collective-permute-start | bytes 4325384 | tf_op jit(solution)/shard_map/ppermute | solution.py:67
  835.5 41.5 %collective-permute-start.15 = (bf16[2,1,128,1408]{3,2,1,0:T(8,128)(2,1)S(1)}, bf16[2,1,128,1408]{3,2,1,0:T(8,128)(2,1)}, u32[]{:S(2)}, u32[]{:S(2)}) collective-permute-start(bf16[2,1,128,1408]{3,2,1,0:T(8,128)(2,1)S(1)} %slice.133.refs_4_.refs_8_), channel_id=1, source_target_pairs={{0,8},{8,0},{16,24},{24,16},{1,9},{9,1},{17,25},{25,17},{2,10},{10... | collective-permute-start | bytes 2162696 | tf_op jit(solution)/shard_map/ppermute | solution.py:67
  836.2 42.0 %collective-permute-start.16 = (bf16[2,1,128,1408]{3,2,1,0:T(8,128)(2,1)S(1)}, bf16[2,1,128,1408]{3,2,1,0:T(8,128)(2,1)}, u32[]{:S(2)}, u32[]{:S(2)}) collective-permute-start(bf16[2,1,128,1408]{3,2,1,0:T(8,128)(2,1)S(1)} %slice.133.refs_4_.refs_8_), channel_id=1, source_target_pairs={{0,16},{8,24},{16,0},{24,8},{1,17},{9,25},{17,1},{25,9},{2,18},{10... | collective-permute-start | bytes 2162696 | tf_op jit(solution)/shard_map/ppermute | solution.py:67
  837.0 29.2 %collective-permute-start.14 = (f32[512,64]{0,1:T(8,128)S(1)}, f32[512,64]{0,1:T(8,128)S(1)}, u32[]{:S(2)}, u32[]{:S(2)}) collective-permute-start(f32[512,64]{0,1:T(8,128)S(1)} %fusion.20), channel_id=1, source_target_pairs={{0,1},{1,0},{2,3},{3,2},{4,5},{5,4},{6,7},{7,6},{8,9},{9,8},{10,11... | collective-permute-start | bytes 393224 | tf_op jit(solution)/shard_map/ppermute | solution.py:131
  899.9 50.1 %collective-permute-start.21 = (bf16[4,1,128,1408]{3,2,1,0:T(8,128)(2,1)}, bf16[4,1,128,1408]{3,2,1,0:T(8,128)(2,1)S(1)}, u32[]{:S(2)}, u32[]{:S(2)}) collective-permute-start(bf16[4,1,128,1408]{3,2,1,0:T(8,128)(2,1)} %collective-permute-done.17.refs_9_.refs_13_), channel_id=1, source_target_pairs={{0,16},{8,24},{16,0},{24,8},{1,17},{9,25},{17,1},{25,9},{2,18},{10... | collective-permute-start | bytes 4325384 | tf_op jit(solution)/shard_map/ppermute | solution.py:67
  915.1 150.6 %reduce-scatter.18.cloned.1.call-start = ((), (), s32[]{:S(2)}) async-start(), calls=%async_computation.27 | async-start | bytes 4718592 | tf_op jit(solution)/shard_map/reduce_scatter | solution.py:139
  915.4 25.0 %collective-permute-start.19 = (bf16[2,1,128,1408]{3,2,1,0:T(8,128)(2,1)S(1)}, bf16[2,1,128,1408]{3,2,1,0:T(8,128)(2,1)S(1)}, u32[]{:S(2)}, u32[]{:S(2)}) collective-permute-start(bf16[2,1,128,1408]{3,2,1,0:T(8,128)(2,1)S(1)} %copy-done.26), channel_id=1, source_target_pairs={{0,8},{8,0},{16,24},{24,16},{1,9},{9,1},{17,25},{25,17},{2,10},{10... | collective-permute-start | bytes 2162696 | tf_op jit(solution)/shard_map/ppermute | solution.py:67
  915.5 34.5 %collective-permute-start.20 = (bf16[2,1,128,1408]{3,2,1,0:T(8,128)(2,1)}, bf16[2,1,128,1408]{3,2,1,0:T(8,128)(2,1)S(1)}, u32[]{:S(2)}, u32[]{:S(2)}) collective-permute-start(bf16[2,1,128,1408]{3,2,1,0:T(8,128)(2,1)} %collective-permute-done.16.refs_6_.refs_10_), channel_id=1, source_target_pairs={{0,8},{8,0},{16,24},{24,16},{1,9},{9,1},{17,25},{25,17},{2,10},{10... | collective-permute-start | bytes 2162696 | tf_op jit(solution)/shard_map/ppermute | solution.py:67
  929.5 37.3 %collective-permute-start.22 = (bf16[1024,384]{1,0:T(8,128)(2,1)S(1)}, bf16[1024,384]{1,0:T(8,128)(2,1)}, u32[]{:S(2)}, u32[]{:S(2)}) collective-permute-start(bf16[1024,384]{1,0:T(8,128)(2,1)S(1)} %copy-done.63), channel_id=1, source_target_pairs={{0,8},{8,0},{16,24},{24,16},{1,9},{9,1},{17,25},{25,17},{2,10},{10... | collective-permute-start | bytes 2359304 | tf_op jit(solution)/shard_map/ppermute | solution.py:67
  939.0 27.8 %collective-permute-start.23 = (bf16[1024,384]{1,0:T(8,128)(2,1)S(1)}, bf16[1024,384]{1,0:T(8,128)(2,1)}, u32[]{:S(2)}, u32[]{:S(2)}) collective-permute-start(bf16[1024,384]{1,0:T(8,128)(2,1)S(1)} %copy-done.63), channel_id=1, source_target_pairs={{0,16},{8,24},{16,0},{24,8},{1,17},{9,25},{17,1},{25,9},{2,18},{10... | collective-permute-start | bytes 2359304 | tf_op jit(solution)/shard_map/ppermute | solution.py:67
  940.5 35.1 %collective-permute-start.24 = (bf16[512,512]{1,0:T(8,128)(2,1)}, bf16[512,512]{1,0:T(8,128)(2,1)S(1)}, u32[]{:S(2)}, u32[]{:S(2)}) collective-permute-start(bf16[512,512]{1,0:T(8,128)(2,1)} %convolution_convert_fusion.1), channel_id=1, source_target_pairs={{0,8},{8,0},{16,24},{24,16},{1,9},{9,1},{17,25},{25,17},{2,10},{10... | collective-permute-start | bytes 1572872 | tf_op jit(solution)/shard_map/ppermute | solution.py:67
  988.5 94.8 %reduce-scatter.20.cloned.1.call-start = ((), (), s32[]{:S(2)}) async-start(), calls=%async_computation.28 | async-start | bytes 4718592 | tf_op jit(solution)/shard_map/reduce_scatter | solution.py:139
  990.3 21.5 %collective-permute-start.26 = (bf16[512,384]{1,0:T(8,128)(2,1)}, bf16[512,384]{1,0:T(8,128)(2,1)}, u32[]{:S(2)}, u32[]{:S(2)}) collective-permute-start(bf16[512,384]{1,0:T(8,128)(2,1)} %slice.136), channel_id=1, source_target_pairs={{0,8},{8,0},{16,24},{24,16},{1,9},{9,1},{17,25},{25,17},{2,10},{10... | collective-permute-start | bytes 1179656 | tf_op jit(solution)/shard_map/ppermute | solution.py:67
  1026.3 75.0 %all-to-all-start.7 = ((bf16[4,512,1152]{2,1,0:T(8,128)(2,1)}), bf16[4,512,1152]{2,1,0:T(8,128)(2,1)}, u32[]{:S(2)}, u32[]{:S(2)}) async-start(bf16[4,512,1152]{2,1,0:T(8,128)(2,1)} %bitcast.200), calls=%async_computation.14 | async-start | bytes 9437184 | tf_op jit(solution)/shard_map/all_to_all | solution.py:124
  1041.3 23.8 %collective-permute-start.33 = (f32[512,64]{0,1:T(8,128)S(1)}, f32[512,64]{0,1:T(8,128)S(1)}, u32[]{:S(2)}, u32[]{:S(2)}) collective-permute-start(f32[512,64]{0,1:T(8,128)S(1)} %add.150), channel_id=1, source_target_pairs={{0,4},{1,5},{2,6},{3,7},{4,0},{5,1},{6,2},{7,3},{8,12},{9,13},{10,... | collective-permute-start | bytes 393224 | tf_op jit(solution)/shard_map/ppermute | solution.py:131
  (91 other events, 1450.6 us)
Sparse Core Ops, SparseCore 0:
  9.6 52.6 all-gather.7
  66.3 47.5 all-gather.9
  116.1 21.7 all-gather.11
  140.0 46.9 all-gather.13
  189.1 48.7 reduce-scatter.7
  246.0 50.5 all-gather.15
  298.8 45.8 all-gather.17
  363.2 50.1 reduce-scatter.9
  416.3 48.1 reduce-scatter.13
  765.2 52.0 reduce-scatter.11
  828.6 45.2 all-gather.19
  915.3 34.2 reduce-scatter.15
  976.7 53.3 reduce-scatter.17
  1032.3 51.0 reduce-scatter.19
